TPU v7x, 256 devices: a whole 4x4x8 slice. The times are simulated.
256 devices in a mesh: context: 32 (over y_hi, z, core), tensor: 8 (over y_lo, x).
Axes of the slice: x: 4, y: 4 (y_hi: 2, y_lo: 2; y = y_hi * 2 + y_lo), z: 8, core: 2. Of those that a mesh axis runs over, the one named last changes fastest.
Arguments:
- gate_proj: bfloat16 [8192, 8192], P('context', 'tensor'), may hold values from -5 to 5
- key_proj: bfloat16 [8192, 8192], P('context', 'tensor'), may hold values from -5 to 5
- value_proj: bfloat16 [8192, 8192], P('context', 'tensor'), may hold values from -5 to 5
- filters: bfloat16 [8192, 128], P('tensor'), may hold values from -0.5 to 0.5
- residual_in: bfloat16 [8192, 8192], P('context', 'tensor'), may hold values from -55 to 55
- norm_gain: float32 [8192], P('tensor'), may hold values from 0.5 to 1.5
- queries: bfloat16 [8192, 4096], P('context', 'tensor'), may hold values from -22 to 22
- attn_keys: bfloat16 [8192, 4096], P('context', 'tensor'), may hold values from -22 to 22
- attn_values: bfloat16 [8192, 4096], P('context', 'tensor'), may hold values from -5 to 5
Outputs:
- residual_out: bfloat16 [8192, 8192], P('context', 'tensor')
- normed: bfloat16 [8192, 8192], P('context', 'tensor')
- heads_out: bfloat16 [8192, 4096], P('context', 'tensor')
All inputs are finite; a program needn't handle non-finite values.
Results may differ from a plain program's by a relative error of at most 0.0065.
Values may be sent and summed in bfloat16 or wider, within the bound.
No kernel may reach another device: no remote copies, remote signals or barrier semaphores. Data moves between devices by JAX's collectives and lax.ppermute only.
A program may use at most 128 MiB of HBM per device.

v0:
```python
import math

import jax
import jax.numpy as jnp
from jax import lax
from jax.sharding import PartitionSpec as P

D = 8192
DH = 128


def shifted(shard, axis, by):
    peers = lax.axis_size(axis)
    pairs = [(i, i + by) for i in range(peers) if 0 <= i + by < peers]
    return lax.ppermute(shard, axis, pairs)


def merge_block(state, query_rows, query_pos, key_rows, value_rows, key_pos):
    highest, totals, summed = state
    scale = 1.0 / math.sqrt(DH)
    scores = (
        jnp.einsum("qhd,khd->hqk", query_rows, key_rows, preferred_element_type=jnp.float32) * scale
    )
    allowed = key_pos[None, None, :] <= query_pos[None, :, None]
    scores = jnp.where(allowed, scores, -1e30)
    new_high = jnp.maximum(highest, jnp.max(scores, axis=2))
    factor = jnp.exp(highest - new_high)
    weights = jnp.where(allowed, jnp.exp(scores - new_high[:, :, None]), 0.0).astype(jnp.bfloat16)
    totals = totals * factor + jnp.sum(weights.astype(jnp.float32), axis=2)
    summed = summed * factor[:, :, None] + jnp.einsum(
        "hqk,khd->hqd", weights, value_rows, preferred_element_type=jnp.float32
    )
    return (new_high, totals, summed)


def attend(groups, key_heads, value_heads):
    head_count = key_heads.shape[1]
    initial = tuple(
        (
            (
                jnp.full((head_count, rows_in.shape[0]), -1e30, jnp.float32),
                jnp.zeros((head_count, rows_in.shape[0]), jnp.float32),
                jnp.zeros((head_count, rows_in.shape[0], DH), jnp.float32),
            )
            for rows_in, first_pos in groups
        )
    )
    key_piece = lax.all_gather(key_heads, "context", axis=0, tiled=True)
    value_piece = lax.all_gather(value_heads, "context", axis=0, tiled=True)
    piece_rows = key_piece.shape[0]
    span = math.gcd(piece_rows, 512)

    def visit(block_index, state):
        key_first = block_index * span
        key_rows = lax.dynamic_slice_in_dim(key_piece, block_index * span, span, 0)
        value_rows = lax.dynamic_slice_in_dim(value_piece, block_index * span, span, 0)
        key_pos = key_first + jnp.arange(span, dtype=jnp.int32)
        updated = []
        for (query_rows, first_pos), group_state in zip(groups, state):
            query_pos = first_pos + jnp.arange(query_rows.shape[0], dtype=jnp.int32)
            last_pos = first_pos + query_rows.shape[0] - 1
            updated.append(
                lax.cond(
                    key_first <= last_pos,
                    lambda given: merge_block(
                        given, query_rows, query_pos, key_rows, value_rows, key_pos
                    ),
                    lambda given: given,
                    group_state,
                )
            )
        return tuple(updated)

    final = lax.fori_loop(0, piece_rows // span, visit, initial)
    results = []
    for highest, totals, summed in final:
        normal_out = summed / totals[:, :, None]
        results.append(
            normal_out.transpose(1, 0, 2)
            .reshape(normal_out.shape[1], head_count * DH)
            .astype(jnp.bfloat16)
        )
    return results


def local(
    gate_proj,
    key_proj,
    value_proj,
    filters,
    residual_in,
    norm_gain,
    queries,
    attn_keys,
    attn_values,
):
    row_count, channels = gate_proj.shape
    length = filters.shape[1]
    gated = (key_proj.astype(jnp.float32) * value_proj.astype(jnp.float32)).astype(jnp.bfloat16)
    before = shifted(gated[row_count - length :], "context", 1)
    padded = jnp.concatenate([before, gated], axis=0)[1:]
    kernel = jnp.flip(filters, axis=1).T.reshape(length, 1, channels)
    filtered = lax.conv_general_dilated(
        padded[None],
        kernel,
        (1,),
        "VALID",
        dimension_numbers=("NWC", "WIO", "NWC"),
        feature_group_count=channels,
        preferred_element_type=jnp.float32,
    )[0]
    residual_out = (
        residual_in.astype(jnp.float32) + gate_proj.astype(jnp.float32) * filtered
    ).astype(jnp.bfloat16)
    widened = residual_out.astype(jnp.float32)
    squares = lax.psum(jnp.sum(widened * widened, axis=1), "tensor")
    mean_square = squares[:, None] / D
    normed = (widened * lax.rsqrt(mean_square + 1e-06) * norm_gain[None, :]).astype(jnp.bfloat16)
    head_count = queries.shape[1] // DH
    query_heads = queries.reshape(row_count, head_count, DH)
    key_heads = attn_keys.reshape(row_count, head_count, DH)
    value_heads = attn_values.reshape(row_count, head_count, DH)
    position = lax.axis_index("context")
    groups = [(query_heads, position * row_count)]
    heads_out = attend(groups, key_heads, value_heads)[0]
    return (residual_out, normed, heads_out)


def solution(mesh):
    placed = (
        P("context", "tensor"),
        P("context", "tensor"),
        P("context", "tensor"),
        P("tensor", None),
        P("context", "tensor"),
        P("tensor"),
        P("context", "tensor"),
        P("context", "tensor"),
        P("context", "tensor"),
    )
    return jax.shard_map(
        local,
        mesh=mesh,
        in_specs=placed,
        out_specs=(P("context", "tensor"), P("context", "tensor"), P("context", "tensor")),
        check_vma=False,
    )
```

profile of v0, /device:TPU:249, one launch (start us, length us, event | category | flops | bytes accessed | tf_op | source)
XLA Modules:
  0.0 315.1 jit_solution(15583808696134235608)
XLA Ops:
  7.2 1.8 copy.18
  9.1 1.8 copy.20
  11.0 1.4 multiply_convert_fusion
  12.4 1.3 collective-permute-start
  13.7 0.8 rev.4
  15.3 0.7 collective-permute-done
  16.3 14.1 %fusion.6 = f32[1,256,1024]{2,0,1:T(1,128)S(1)} fusion(bf16[128,1,1024]{2,1,0:T(2,128)(2,1)S(1)} %copy.17, bf16[1,383,1024]{2,1,0:T(8,128)(2,1)S(1)} %fusion.13), kind=kOutput, calls=%fused_computation.15 | convolution fusion | flops 67108864 | bytes 2095104 | tf_op jit(solution)/shard_map/conv_general_dilated | solution.py:103
  30.7 15.2 %psum.7 = f32[256]{0:T(256)S(1)} all-reduce(f32[256]{0:T(256)S(1)} %get-tuple-element.373), channel_id=1, replica_groups=mesh['context'=32,'tensor'=8] {'tensor'}, use_global_device_ids=true, to_apply=%region_1.2 | all-reduce | flops 256 | bytes 2048 | tf_op jit(solution)/shard_map/psum | solution.py:116
  46.0 1.0 fusion.10
  46.9 70.9 %all-gather.3.cloned.1.call-done = bf16[8192,4,128]{0,2,1:T(8,128)(2,1)} async-done(((bf16[256,4,128]{0,2,1:T(8,128)(2,1)}), bf16[8192,4,128]{0,2,1:T(8,128)(2,1)}) %all-gather.3.cloned.1.call-update) | async-done | bytes 8388624 | tf_op jit(solution)/shard_map/all_gather | solution.py:48
  117.9 11.9 %copy.21 = bf16[8192,4,128]{2,0,1:T(8,128)(2,1)} copy(bf16[8192,4,128]{0,2,1:T(8,128)(2,1)} %all-gather.3.cloned.1.call-done) | data formatting | bytes 16777216 | tf_op jit(solution)/shard_map/while | solution.py:74
  129.8 95.3 %all-gather.5.cloned.1.call-done = bf16[8192,4,128]{0,2,1:T(8,128)(2,1)} async-done(((bf16[256,4,128]{0,2,1:T(8,128)(2,1)}), bf16[8192,4,128]{0,2,1:T(8,128)(2,1)}) %all-gather.5.cloned.1.call-update) | async-done | bytes 8388624 | tf_op jit(solution)/shard_map/all_gather | solution.py:49
  225.2 11.9 %copy.23 = bf16[8192,4,128]{2,0,1:T(8,128)(2,1)} copy(bf16[8192,4,128]{0,2,1:T(8,128)(2,1)} %all-gather.5.cloned.1.call-done) | data formatting | bytes 16777216 | tf_op jit(solution)/shard_map/while | solution.py:74
  237.2 70.2 %while.19 = (s32[]{:T(128)}, f32[4,256]{1,0:T(4,128)S(1)}, f32[4,256]{1,0:T(4,128)S(1)}, f32[4,256,128]{2,1,0:T(8,128)S(1)}, s32[]{:T(128)}, /*index=5*/s32[]{:T...) while((s32[]{:T(128)}, f32[4,256]{1,0:T(4,128)S(1)}, ...), condition=%wide.region_7.8_spmd, body=%wide.region_2.7_spmd.sunk | while | flops 276695808 | bytes 9253185 | solution.py:74
  237.2 4.3 %conditional.2 = ((f32[4,256]{1,0:T(4,128)S(1)}, f32[4,256]{1,0:T(4,128)S(1)}, f32[4,256,128]{2,1,0:T(8,128)S(1)})) conditional(s32[]{:T(128)} %convert_element_type.93, (f32[4,256]{1,0:T(4,128)S(1)}, f32[4,256]{1,0:T(4,128)S(1)}, f32[4,256,128]{2,1,0:T(8,128)S(1)}) %tuple.62, (s32[]{:T(128)}, s32[512]{0:T(512)S(1)}, s32[]{:T(128)}, ...), branch_computations={%region_3.3_spmd, %region_4.6_spmd} | conditional | flops 276695808 | bytes 9249874 | solution.py:63
  237.4 1.5 fusion
  238.9 0.5 convert_reduce_fusion
  239.5 2.0 convolution_add_fusion
  241.6 4.3 %conditional.2 = ((f32[4,256]{1,0:T(4,128)S(1)}, f32[4,256]{1,0:T(4,128)S(1)}, f32[4,256,128]{2,1,0:T(8,128)S(1)})) conditional(s32[]{:T(128)} %convert_element_type.93, (f32[4,256]{1,0:T(4,128)S(1)}, f32[4,256]{1,0:T(4,128)S(1)}, f32[4,256,128]{2,1,0:T(8,128)S(1)}) %tuple.62, (s32[]{:T(128)}, s32[512]{0:T(512)S(1)}, s32[]{:T(128)}, ...), branch_computations={%region_3.3_spmd, %region_4.6_spmd} | conditional | flops 276695808 | bytes 9249874 | solution.py:63
  241.8 1.5 fusion
  243.9 2.0 convolution_add_fusion
  246.0 4.3 %conditional.2 = ((f32[4,256]{1,0:T(4,128)S(1)}, f32[4,256]{1,0:T(4,128)S(1)}, f32[4,256,128]{2,1,0:T(8,128)S(1)})) conditional(s32[]{:T(128)} %convert_element_type.93, (f32[4,256]{1,0:T(4,128)S(1)}, f32[4,256]{1,0:T(4,128)S(1)}, f32[4,256,128]{2,1,0:T(8,128)S(1)}) %tuple.62, (s32[]{:T(128)}, s32[512]{0:T(512)S(1)}, s32[]{:T(128)}, ...), branch_computations={%region_3.3_spmd, %region_4.6_spmd} | conditional | flops 276695808 | bytes 9249874 | solution.py:63
  246.2 1.5 fusion
  248.3 2.0 convolution_add_fusion
  250.4 4.3 %conditional.2 = ((f32[4,256]{1,0:T(4,128)S(1)}, f32[4,256]{1,0:T(4,128)S(1)}, f32[4,256,128]{2,1,0:T(8,128)S(1)})) conditional(s32[]{:T(128)} %convert_element_type.93, (f32[4,256]{1,0:T(4,128)S(1)}, f32[4,256]{1,0:T(4,128)S(1)}, f32[4,256,128]{2,1,0:T(8,128)S(1)}) %tuple.62, (s32[]{:T(128)}, s32[512]{0:T(512)S(1)}, s32[]{:T(128)}, ...), branch_computations={%region_3.3_spmd, %region_4.6_spmd} | conditional | flops 276695808 | bytes 9249874 | solution.py:63
  250.6 1.5 fusion
  252.7 2.0 convolution_add_fusion
  254.7 4.3 %conditional.2 = ((f32[4,256]{1,0:T(4,128)S(1)}, f32[4,256]{1,0:T(4,128)S(1)}, f32[4,256,128]{2,1,0:T(8,128)S(1)})) conditional(s32[]{:T(128)} %convert_element_type.93, (f32[4,256]{1,0:T(4,128)S(1)}, f32[4,256]{1,0:T(4,128)S(1)}, f32[4,256,128]{2,1,0:T(8,128)S(1)}) %tuple.62, (s32[]{:T(128)}, s32[512]{0:T(512)S(1)}, s32[]{:T(128)}, ...), branch_computations={%region_3.3_spmd, %region_4.6_spmd} | conditional | flops 276695808 | bytes 9249874 | solution.py:63
  254.9 1.5 fusion
  257.0 2.0 convolution_add_fusion
  259.1 4.3 %conditional.2 = ((f32[4,256]{1,0:T(4,128)S(1)}, f32[4,256]{1,0:T(4,128)S(1)}, f32[4,256,128]{2,1,0:T(8,128)S(1)})) conditional(s32[]{:T(128)} %convert_element_type.93, (f32[4,256]{1,0:T(4,128)S(1)}, f32[4,256]{1,0:T(4,128)S(1)}, f32[4,256,128]{2,1,0:T(8,128)S(1)}) %tuple.62, (s32[]{:T(128)}, s32[512]{0:T(512)S(1)}, s32[]{:T(128)}, ...), branch_computations={%region_3.3_spmd, %region_4.6_spmd} | conditional | flops 276695808 | bytes 9249874 | solution.py:63
  259.3 1.5 fusion
  261.4 2.0 convolution_add_fusion
  263.5 4.3 %conditional.2 = ((f32[4,256]{1,0:T(4,128)S(1)}, f32[4,256]{1,0:T(4,128)S(1)}, f32[4,256,128]{2,1,0:T(8,128)S(1)})) conditional(s32[]{:T(128)} %convert_element_type.93, (f32[4,256]{1,0:T(4,128)S(1)}, f32[4,256]{1,0:T(4,128)S(1)}, f32[4,256,128]{2,1,0:T(8,128)S(1)}) %tuple.62, (s32[]{:T(128)}, s32[512]{0:T(512)S(1)}, s32[]{:T(128)}, ...), branch_computations={%region_3.3_spmd, %region_4.6_spmd} | conditional | flops 276695808 | bytes 9249874 | solution.py:63
  263.7 1.5 fusion
  265.8 2.0 convolution_add_fusion
  267.9 4.3 %conditional.2 = ((f32[4,256]{1,0:T(4,128)S(1)}, f32[4,256]{1,0:T(4,128)S(1)}, f32[4,256,128]{2,1,0:T(8,128)S(1)})) conditional(s32[]{:T(128)} %convert_element_type.93, (f32[4,256]{1,0:T(4,128)S(1)}, f32[4,256]{1,0:T(4,128)S(1)}, f32[4,256,128]{2,1,0:T(8,128)S(1)}) %tuple.62, (s32[]{:T(128)}, s32[512]{0:T(512)S(1)}, s32[]{:T(128)}, ...), branch_computations={%region_3.3_spmd, %region_4.6_spmd} | conditional | flops 276695808 | bytes 9249874 | solution.py:63
  268.1 1.5 fusion
  270.2 2.0 convolution_add_fusion
  272.3 4.3 %conditional.2 = ((f32[4,256]{1,0:T(4,128)S(1)}, f32[4,256]{1,0:T(4,128)S(1)}, f32[4,256,128]{2,1,0:T(8,128)S(1)})) conditional(s32[]{:T(128)} %convert_element_type.93, (f32[4,256]{1,0:T(4,128)S(1)}, f32[4,256]{1,0:T(4,128)S(1)}, f32[4,256,128]{2,1,0:T(8,128)S(1)}) %tuple.62, (s32[]{:T(128)}, s32[512]{0:T(512)S(1)}, s32[]{:T(128)}, ...), branch_computations={%region_3.3_spmd, %region_4.6_spmd} | conditional | flops 276695808 | bytes 9249874 | solution.py:63
  272.5 1.5 fusion
  274.6 2.0 convolution_add_fusion
  276.7 4.3 %conditional.2 = ((f32[4,256]{1,0:T(4,128)S(1)}, f32[4,256]{1,0:T(4,128)S(1)}, f32[4,256,128]{2,1,0:T(8,128)S(1)})) conditional(s32[]{:T(128)} %convert_element_type.93, (f32[4,256]{1,0:T(4,128)S(1)}, f32[4,256]{1,0:T(4,128)S(1)}, f32[4,256,128]{2,1,0:T(8,128)S(1)}) %tuple.62, (s32[]{:T(128)}, s32[512]{0:T(512)S(1)}, s32[]{:T(128)}, ...), branch_computations={%region_3.3_spmd, %region_4.6_spmd} | conditional | flops 276695808 | bytes 9249874 | solution.py:63
  276.9 1.5 fusion
  279.0 2.0 convolution_add_fusion
  281.0 4.3 %conditional.2 = ((f32[4,256]{1,0:T(4,128)S(1)}, f32[4,256]{1,0:T(4,128)S(1)}, f32[4,256,128]{2,1,0:T(8,128)S(1)})) conditional(s32[]{:T(128)} %convert_element_type.93, (f32[4,256]{1,0:T(4,128)S(1)}, f32[4,256]{1,0:T(4,128)S(1)}, f32[4,256,128]{2,1,0:T(8,128)S(1)}) %tuple.62, (s32[]{:T(128)}, s32[512]{0:T(512)S(1)}, s32[]{:T(128)}, ...), branch_computations={%region_3.3_spmd, %region_4.6_spmd} | conditional | flops 276695808 | bytes 9249874 | solution.py:63
  281.2 1.5 fusion
  283.3 2.0 convolution_add_fusion
  285.4 4.3 %conditional.2 = ((f32[4,256]{1,0:T(4,128)S(1)}, f32[4,256]{1,0:T(4,128)S(1)}, f32[4,256,128]{2,1,0:T(8,128)S(1)})) conditional(s32[]{:T(128)} %convert_element_type.93, (f32[4,256]{1,0:T(4,128)S(1)}, f32[4,256]{1,0:T(4,128)S(1)}, f32[4,256,128]{2,1,0:T(8,128)S(1)}) %tuple.62, (s32[]{:T(128)}, s32[512]{0:T(512)S(1)}, s32[]{:T(128)}, ...), branch_computations={%region_3.3_spmd, %region_4.6_spmd} | conditional | flops 276695808 | bytes 9249874 | solution.py:63
  285.6 1.5 fusion
  287.7 2.0 convolution_add_fusion
  289.8 4.3 %conditional.2 = ((f32[4,256]{1,0:T(4,128)S(1)}, f32[4,256]{1,0:T(4,128)S(1)}, f32[4,256,128]{2,1,0:T(8,128)S(1)})) conditional(s32[]{:T(128)} %convert_element_type.93, (f32[4,256]{1,0:T(4,128)S(1)}, f32[4,256]{1,0:T(4,128)S(1)}, f32[4,256,128]{2,1,0:T(8,128)S(1)}) %tuple.62, (s32[]{:T(128)}, s32[512]{0:T(512)S(1)}, s32[]{:T(128)}, ...), branch_computations={%region_3.3_spmd, %region_4.6_spmd} | conditional | flops 276695808 | bytes 9249874 | solution.py:63
  290.0 1.5 fusion
  292.1 2.0 convolution_add_fusion
  294.2 4.3 %conditional.2 = ((f32[4,256]{1,0:T(4,128)S(1)}, f32[4,256]{1,0:T(4,128)S(1)}, f32[4,256,128]{2,1,0:T(8,128)S(1)})) conditional(s32[]{:T(128)} %convert_element_type.93, (f32[4,256]{1,0:T(4,128)S(1)}, f32[4,256]{1,0:T(4,128)S(1)}, f32[4,256,128]{2,1,0:T(8,128)S(1)}) %tuple.62, (s32[]{:T(128)}, s32[512]{0:T(512)S(1)}, s32[]{:T(128)}, ...), branch_computations={%region_3.3_spmd, %region_4.6_spmd} | conditional | flops 276695808 | bytes 9249874 | solution.py:63
  294.4 1.5 fusion
  296.5 2.0 convolution_add_fusion
  298.6 4.3 %conditional.2 = ((f32[4,256]{1,0:T(4,128)S(1)}, f32[4,256]{1,0:T(4,128)S(1)}, f32[4,256,128]{2,1,0:T(8,128)S(1)})) conditional(s32[]{:T(128)} %convert_element_type.93, (f32[4,256]{1,0:T(4,128)S(1)}, f32[4,256]{1,0:T(4,128)S(1)}, f32[4,256,128]{2,1,0:T(8,128)S(1)}) %tuple.62, (s32[]{:T(128)}, s32[512]{0:T(512)S(1)}, s32[]{:T(128)}, ...), branch_computations={%region_3.3_spmd, %region_4.6_spmd} | conditional | flops 276695808 | bytes 9249874 | solution.py:63
  298.8 1.5 fusion
  300.9 2.0 convolution_add_fusion
  303.0 4.3 %conditional.2 = ((f32[4,256]{1,0:T(4,128)S(1)}, f32[4,256]{1,0:T(4,128)S(1)}, f32[4,256,128]{2,1,0:T(8,128)S(1)})) conditional(s32[]{:T(128)} %convert_element_type.93, (f32[4,256]{1,0:T(4,128)S(1)}, f32[4,256]{1,0:T(4,128)S(1)}, f32[4,256,128]{2,1,0:T(8,128)S(1)}) %tuple.62, (s32[]{:T(128)}, s32[512]{0:T(512)S(1)}, s32[]{:T(128)}, ...), branch_computations={%region_3.3_spmd, %region_4.6_spmd} | conditional | flops 276695808 | bytes 9249874 | solution.py:63
  303.2 1.5 fusion
  305.3 2.0 convolution_add_fusion
  307.3 0.9 copy_bitcast_fusion
  (169 shorter events, 12.3 us)
Async XLA Ops:
  7.2 6.6 %copy-start.3 = (bf16[1024,128]{1,0:T(8,128)(2,1)S(1)}, bf16[1024,128]{1,0:T(8,128)(2,1)}, u32[]{:S(2)}) copy-start(bf16[1024,128]{1,0:T(8,128)(2,1)} %param.16) | copy-start | bytes 786436
  7.2 110.7 %all-gather.3.cloned.1.call-start = ((), (), s32[]{:S(2)}) async-start(), calls=%async_computation | async-start | bytes 8650752 | tf_op jit(solution)/shard_map/all_gather | solution.py:48
  9.1 5.9 %copy-start.4 = (bf16[256,512]{1,0:T(8,128)(2,1)S(1)}, bf16[256,512]{1,0:T(8,128)(2,1)}, u32[]{:S(2)}) copy-start(bf16[256,512]{1,0:T(8,128)(2,1)} %param.19) | copy-start | bytes 786436
  9.1 216.1 %all-gather.5.cloned.1.call-start = ((), (), s32[]{:S(2)}) async-start(), calls=%async_computation.1 | async-start | bytes 8650752 | tf_op jit(solution)/shard_map/all_gather | solution.py:49
  12.4 3.6 %collective-permute-start = (bf16[128,1024]{1,0:T(8,128)(2,1)S(1)}, bf16[128,1024]{1,0:T(8,128)(2,1)S(1)}, u32[]{:S(2)}, u32[]{:S(2)}) collective-permute-start(bf16[128,1024]{1,0:T(8,128)(2,1)S(1)} %slice.8), channel_id=1, source_target_pairs={{0,8},{8,16},{16,24},{24,32},{32,40},{40,48},{48,56},{56,64},{64,7... | collective-permute-start | bytes 786440 | tf_op jit(solution)/shard_map/ppermute | solution.py:15
  16.2 14.1 %copy-start.1 = (bf16[256,1024]{1,0:T(8,128)(2,1)S(1)}, bf16[256,1024]{1,0:T(8,128)(2,1)}, u32[]{:S(2)}) copy-start(bf16[256,1024]{1,0:T(8,128)(2,1)} %param.13) | copy-start | bytes 1572868
  16.3 14.1 %copy-start.2 = (bf16[256,1024]{1,0:T(8,128)(2,1)S(1)}, bf16[256,1024]{1,0:T(8,128)(2,1)}, u32[]{:S(2)}) copy-start(bf16[256,1024]{1,0:T(8,128)(2,1)} %param.17) | copy-start | bytes 1572868
  30.4 15.6 %copy-start.5 = (f32[1024]{0:T(1024)S(1)}, f32[1024]{0:T(1024)}, u32[]{:S(2)}) copy-start(f32[1024]{0:T(1024)} %param.18) | copy-start | bytes 12292
  30.7 99.1 %copy-start = (bf16[256,1024]{1,0:T(8,128)(2,1)}, bf16[256,1024]{1,0:T(8,128)(2,1)S(1)}, u32[]{:S(2)}) copy-start(bf16[256,1024]{1,0:T(8,128)(2,1)S(1)} %get-tuple-element.374) | copy-start | bytes 1572868
Sparse Core Ops, SparseCore 0:
  11.1 106.7 all-gather.2
  120.4 104.6 all-gather.4
where the time goes:
time: 317 us; the launch traced here: 315 us
  waiting for transfers between devices  167 us (53%)
  matrix products  70.9 us (22%)
  local copies, waits for them, and re-layouts  29.3 us (9%)
  blocking collectives  15.2 us (5%)
  other arithmetic  15 us (5%)
  between operations  14.2 us (4%)
    all_gather x1, waiting for transfers between devices, attend(): value_piece = lax.all_gather(value_heads, 'context', axis=0, tiled=True)  95.3 us
    all_gather x1, waiting for transfers between devices, attend(): key_piece = lax.all_gather(key_heads, 'context', axis=0, tiled=True)  70.9 us
    dot_general x16, matrix products, merge_block(): jnp.einsum('hqk,khd->hqd', weights, value_rows, preferred_element_type=jn...  32.3 us
    dot_general x16, matrix products, merge_block(): jnp.einsum('qhd,khd->hqk', query_rows, key_rows, preferred_element_type=j...  24.6 us
    while x3, local copies, waits for them, and re-layouts, attend(): final = lax.fori_loop(0, piece_rows // span, visit, initial)  24 us
    psum x1, blocking collectives, local(): squares = lax.psum(jnp.sum(widened * widened, axis=1), 'tensor')  15.2 us
    conv_general_dilated x1, matrix products, local(): lax.conv_general_dilated(padded[None], kernel, (1,), 'VALID', dimension_n...  14.1 us
    reduce_sum x16, other arithmetic, merge_block(): totals = totals * factor + jnp.sum(weights.astype(jnp.float32), axis=2)  8.49 us
  transfers between devices with their start and end apart: 3, of which 3 were waited for; matrix products, arithmetic and copies ran while one was open for 10% of the time, Pallas kernels for 0%

commit v1 on v0

v1 whole, which is shorter than its diff:
```python
import functools
import math

import jax
import jax.numpy as jnp
import ml_dtypes
import numpy as np
from jax import lax
from jax.experimental import pallas as pl
from jax.experimental.pallas import tpu as pltpu
from jax.sharding import PartitionSpec as P

D = 8192
DH = 128
ROWS = 256
TAPS = 128
SPAN = ROWS + TAPS
ZS = 8
LOG2E_SCALE = math.log2(math.e) / math.sqrt(DH)
LOW = -1e30
F32 = jnp.float32
BF16 = jnp.bfloat16


def pairs(where):
    out = []
    for plane in range(2):
        for z in range(ZS):
            for core in range(2):
                to = where(plane, z, core)
                if to is not None:
                    p, zz, c = to
                    out.append(((plane * ZS + z) * 2 + core, (p * ZS + zz % ZS) * 2 + c))
    return out


def hop(steps):
    return pairs(lambda p, z, c: (p, z + steps[z % 2], c))


NEAR = [None, hop((-1, 1)), hop((2, -2)), hop((-3, 3))]
SIBLING = pairs(lambda p, z, c: (p, z ^ 1, c))
CORE = pairs(lambda p, z, c: (p, z, 1 - c))
DOWN = pairs(lambda p, z, c: (1, z, c) if p == 0 else None)
NEXT = [(i, i + 1) for i in range(2 * ZS * 2 - 1)]


def send(x, where):
    return lax.ppermute(x, "context", where)


def back(x, where):
    return lax.ppermute(x, "context", [(b, a) for a, b in where])


def place():
    index = lax.axis_index("context")
    core = lax.rem(index, 2)
    z = lax.rem(lax.div(index, 2), ZS)
    plane = lax.div(index, 2 * ZS)
    return plane, z, core


def target_heads(z):
    odd = lax.rem(z, 2)
    offsets = [0, -1 + 2 * odd, 2 - 4 * odd, -3 + 6 * odd]
    return [lax.div(lax.rem(z + o + ZS, ZS), 2) for o in offsets]


def pack_kernel(q_ref, k_ref, v_ref, *outs):
    _, z, _ = place()
    for head, out in zip(target_heads(z), outs):
        columns = pl.ds(pl.multiple_of(head * DH, DH), DH)
        out[0:ROWS, :] = q_ref[:, columns]
        out[ROWS : 2 * ROWS, :] = k_ref[:, columns]
        out[2 * ROWS : 3 * ROWS, :] = v_ref[:, columns]


def pack(q, k, v):
    return pl.pallas_call(
        pack_kernel,
        out_shape=[jax.ShapeDtypeStruct((3 * ROWS, DH), BF16)] * 4,
        in_specs=[pl.BlockSpec(memory_space=pltpu.VMEM)] * 3,
        out_specs=[pl.BlockSpec(memory_space=pltpu.VMEM)] * 4,
        compiler_params=pltpu.CompilerParams(vmem_limit_bytes=16 << 20),
        name="pack",
    )(q, k, v)


def unpack_kernel(o0, o1, o2, o3, out):
    _, z, _ = place()
    for head, piece in zip(target_heads(z), (o0, o1, o2, o3)):
        out[:, pl.ds(pl.multiple_of(head * DH, DH), DH)] = piece[...]


def unpack(pieces):
    return pl.pallas_call(
        unpack_kernel,
        out_shape=jax.ShapeDtypeStruct((ROWS, 4 * DH), BF16),
        in_specs=[pl.BlockSpec(memory_space=pltpu.VMEM)] * 4,
        out_specs=pl.BlockSpec(memory_space=pltpu.VMEM),
        compiler_params=pltpu.CompilerParams(vmem_limit_bytes=16 << 20),
        name="unpack",
    )(*pieces)


def wave_kernel(blocks, first, last, count, *refs):
    q_refs = refs[:4]
    array_refs = refs[4 : 4 + count]
    rest = refs[4 + count :]
    if not first:
        acc_in, high_in = rest[:2]
        rest = rest[2:]
    if last:
        outs = rest[:4]
        q_all, acc, high = rest[4:7]
        rest = rest[7:]
    else:
        acc, high = rest[:2]
        q_all = rest[2]
        rest = rest[3:]
    s_all = rest[0]
    plane, z, core = place()
    odd = lax.rem(z, 2)
    sign = 2 * odd - 1
    for j in range(4):
        q_all[j] = q_refs[j][0:ROWS, :]
    if first:
        acc[...] = jnp.zeros_like(acc)
        high[...] = jnp.full_like(high, LOW)
    else:
        acc[...] = acc_in[...]
        high[...] = high_in[...]
    ones = jnp.ones((ROWS, DH), BF16)
    skew = lax.broadcasted_iota(jnp.int32, (ROWS, ROWS), 1) - lax.broadcasted_iota(
        jnp.int32, (ROWS, ROWS), 0
    )

    def source(far, j):
        if far:
            return lax.rem((z + 1 - 2 * odd) - sign * j + ZS, ZS)
        return lax.rem(z + sign * j + ZS, ZS)

    def run(chosen):
        def per_query(i, carry):
            q = q_all[i]
            q_block = 2 * lax.rem(z + sign * i + ZS, ZS) + core
            rows = pl.ds(pl.multiple_of(i * ROWS, ROWS), ROWS)
            old = high[rows, :]
            top = old
            for n, (array, k_row, v_row, lower, far, j, other) in enumerate(chosen):
                keys = array_refs[array][k_row : k_row + ROWS, :]
                s = lax.dot_general(
                    q, keys, (((1,), (1,)), ((), ())), preferred_element_type=F32
                )
                if not lower:
                    k_block = 2 * source(far, j) + (1 - core if other else core)
                    s = jnp.where(skew <= (q_block - k_block) * ROWS, s, LOW)
                s_all[n] = s
                top = jnp.maximum(top, jnp.maximum(s[:, :DH], s[:, DH:]))
            best = jnp.max(top, axis=1, keepdims=True)
            scale = jnp.exp2((old[:, :1] - best) * LOG2E_SCALE)
            total = acc[rows, :] * scale
            for n, (array, k_row, v_row, lower, far, j, other) in enumerate(chosen):
                p = jnp.exp2((s_all[n] - best) * LOG2E_SCALE).astype(BF16)
                values = array_refs[array][v_row : v_row + ROWS, :]
                total = total + jnp.dot(
                    p, jnp.concatenate([values, ones], axis=1), preferred_element_type=F32
                )
            acc[rows, :] = total
            high[rows, :] = jnp.broadcast_to(best, (ROWS, DH))
            return carry

        lax.fori_loop(0, 4, per_query, 0)

    own = [b for b in blocks if not b[3]]
    lower = [b for b in blocks if b[3]]
    if own:
        run(own)
    if lower:

        @pl.when(plane == 1)
        def _():
            run(lower)

    if last:
        for i in range(4):
            part = acc[i * ROWS : (i + 1) * ROWS, :]
            outs[i][...] = (part[:, :DH] / part[:, DH:]).astype(BF16)


def wave(q_arrays, arrays, blocks, state, last=False):
    first = state is None
    most = max(sum(1 for b in blocks if not b[3]), sum(1 for b in blocks if b[3]))
    state_shapes = [((4 * ROWS, 2 * DH), F32), ((4 * ROWS, DH), F32)]
    q_scratch = pltpu.VMEM((4, ROWS, DH), BF16)
    s_scratch = pltpu.VMEM((most, ROWS, ROWS), F32)
    vmem = pl.BlockSpec(memory_space=pltpu.VMEM)
    if last:
        out_shape = [jax.ShapeDtypeStruct((ROWS, DH), BF16)] * 4
        scratch = [q_scratch] + [pltpu.VMEM(s, d) for s, d in state_shapes] + [s_scratch]
    else:
        out_shape = [jax.ShapeDtypeStruct(s, d) for s, d in state_shapes]
        scratch = [q_scratch, s_scratch]
    operands = list(q_arrays) + list(arrays) + ([] if first else list(state))
    tiles = 4 * len(blocks)
    return pl.pallas_call(
        functools.partial(wave_kernel, blocks, first, last, len(arrays)),
        out_shape=out_shape,
        in_specs=[vmem] * len(operands),
        out_specs=[vmem] * len(out_shape),
        scratch_shapes=scratch,
        compiler_params=pltpu.CompilerParams(vmem_limit_bytes=40 << 20),
        cost_estimate=pl.CostEstimate(
            flops=tiles * 4 * ROWS * ROWS * DH,
            bytes_accessed=sum(o.size * o.dtype.itemsize for o in operands),
            transcendentals=tiles * ROWS * ROWS,
        ),
        name="wave",
    )(*operands)


def kv_of(message):
    return message[ROWS:]


def attention(queries, attn_keys, attn_values):
    messages = pack(queries, attn_keys, attn_values)
    got = [messages[0]] + [send(messages[j], NEAR[j]) for j in (1, 2, 3)]
    kv0 = kv_of(got[0])
    far0 = send(kv0, SIBLING)
    low0 = send(kv0, DOWN)
    kv12 = jnp.concatenate([kv_of(got[1]), kv_of(got[2])])
    far12 = send(kv12, SIBLING)
    mid = jnp.concatenate([kv12, far0])
    low12 = send(mid, DOWN)
    core1 = send(jnp.concatenate([kv0, mid]), CORE)
    kv3 = kv_of(got[3])
    far3 = send(kv3, SIBLING)
    late = jnp.concatenate([kv3, far12])
    low3 = send(late, DOWN)
    core2 = send(late, CORE)
    low4 = send(far3, DOWN)
    core3 = send(jnp.concatenate([far3, low0, low12]), CORE)
    core4 = send(jnp.concatenate([low3, low4]), CORE)

    def block(array, first_row, lower, far, j, other):
        return (array, first_row, first_row + ROWS, lower, far, j, other)

    def group(array, spots, lower, other, skip=0):
        return [
            block(array, skip + 2 * ROWS * n, lower, far, j, other)
            for n, (far, j) in enumerate(spots)
        ]

    first = [(False, 0), (False, 1), (False, 2), (True, 0)]
    second = [(False, 3), (True, 1), (True, 2)]
    third = [(True, 3)]
    state = wave(
        got,
        [got[0], got[1], got[2], far0, core1],
        [block(n, ROWS, False, False, n, False) for n in range(3)]
        + group(3, [(True, 0)], False, False)
        + group(4, first, False, True),
        None,
    )
    state = wave(
        got,
        [got[3], far12, core2],
        [block(0, ROWS, False, False, 3, False)]
        + group(1, second[1:], False, False)
        + group(2, second, False, True),
        state,
    )
    state = wave(
        got,
        [far3, core3, low0, low12],
        group(0, third, False, False)
        + group(1, third, False, True)
        + group(1, first, True, True, 2 * ROWS)
        + group(2, first[:1], True, False)
        + group(3, first[1:], True, False),
        state,
    )
    pieces = wave(
        got,
        [low3, low4, core4],
        group(0, second, True, False)
        + group(1, third, True, False)
        + group(2, second + third, True, True),
        state,
        last=True,
    )
    returned = [pieces[0]] + [back(pieces[j], NEAR[j]) for j in (1, 2, 3)]
    return unpack(returned)


def split(x):
    top = x.astype(BF16)
    return top, (x - top.astype(F32)).astype(BF16)


def transform():
    k = np.arange(SPAN // 2)[:, None] + 0.5
    t = np.arange(SPAN)[None, :]
    angle = 2 * np.pi * k * t / SPAN
    forward = np.concatenate([np.cos(angle), np.sin(angle)], axis=0)
    inverse = forward[:, TAPS:].T * (2.0 / SPAN)

    def halves(a):
        top = a.astype(ml_dtypes.bfloat16)
        return [top, (a - top.astype(np.float64)).astype(ml_dtypes.bfloat16)]

    return halves(forward) + halves(inverse)


def filter_kernel(
    fh_ref, fl_ref, gh_ref, gl_ref, key_ref, value_ref, gate_ref, res_ref, taps_ref, halo_ref,
    out_ref, squares_ref,
):
    def dot(a, b):
        return jnp.dot(a, b, preferred_element_type=F32)

    def dot_t(a, b):
        return lax.dot_general(a, b, (((1,), (1,)), ((), ())), preferred_element_type=F32)

    gated = (key_ref[...].astype(F32) * value_ref[...].astype(F32)).astype(BF16)
    x = jnp.concatenate([halo_ref[...], gated], axis=0)
    spectrum = dot(fh_ref[...], x) + dot(fl_ref[...], x)
    taps = taps_ref[...]
    weight = dot_t(fh_ref[:, :TAPS], taps) + dot_t(fl_ref[:, :TAPS], taps)
    half = SPAN // 2
    xc, xs = spectrum[:half], spectrum[half:]
    wc, ws = weight[:half], weight[half:]
    both = jnp.concatenate([xc * wc - xs * ws, xc * ws + xs * wc], axis=0)
    top, low = split(both)
    filtered = dot(gh_ref[...], top) + dot(gh_ref[...], low) + dot(gl_ref[...], top)
    out = (res_ref[...].astype(F32) + gate_ref[...].astype(F32) * filtered).astype(BF16)
    out_ref[...] = out
    wide = out.astype(F32)
    s_top, s_low = split(wide * wide)
    ones = jnp.ones((8, out.shape[1]), BF16)

    @pl.when(pl.program_id(0) == 0)
    def _():
        squares_ref[...] = jnp.zeros_like(squares_ref)

    squares_ref[...] += dot_t(ones, s_top) + dot_t(ones, s_low)


def filter_block(gate, key, value, filters, residual, halo):
    channels = gate.shape[1]
    tile = 256
    rows = pl.BlockSpec((ROWS, tile), lambda i: (0, i))
    whole = lambda a: pl.BlockSpec(a.shape, lambda i: (0, 0))
    matrices = [jnp.asarray(m) for m in transform()]
    return pl.pallas_call(
        filter_kernel,
        grid=(channels // tile,),
        out_shape=[
            jax.ShapeDtypeStruct((ROWS, channels), BF16),
            jax.ShapeDtypeStruct((8, ROWS), F32),
        ],
        in_specs=[whole(m) for m in matrices]
        + [rows] * 4
        + [
            pl.BlockSpec((tile, TAPS), lambda i: (i, 0)),
            pl.BlockSpec((TAPS, tile), lambda i: (0, i)),
        ],
        out_specs=[rows, pl.BlockSpec((8, ROWS), lambda i: (0, 0))],
        compiler_params=pltpu.CompilerParams(vmem_limit_bytes=32 << 20),
        cost_estimate=pl.CostEstimate(
            flops=1500000000, bytes_accessed=5 << 20, transcendentals=0
        ),
        name="filter",
    )(*matrices, key, value, gate, residual, filters, halo)


def sum_over_tensor(x):
    for bit in (1, 2, 4):
        x = x + lax.ppermute(x, "tensor", [(i, i ^ bit) for i in range(8)])
    return x


def local(
    gate_proj,
    key_proj,
    value_proj,
    filters,
    residual_in,
    norm_gain,
    queries,
    attn_keys,
    attn_values,
):
    heads_out = attention(queries, attn_keys, attn_values)
    tail = slice(ROWS - TAPS, ROWS)
    edge = (key_proj[tail].astype(F32) * value_proj[tail].astype(F32)).astype(BF16)
    halo = send(edge, NEXT)
    residual_out, squares = filter_block(
        gate_proj, key_proj, value_proj, filters, residual_in, halo
    )
    mean_square = sum_over_tensor(squares[0])[:, None] / D
    normed = (
        residual_out.astype(F32) * lax.rsqrt(mean_square + 1e-06) * norm_gain[None, :]
    ).astype(BF16)
    return (residual_out, normed, heads_out)


def solution(mesh):
    split_both = P("context", "tensor")
    return jax.shard_map(
        local,
        mesh=mesh,
        in_specs=(
            split_both,
            split_both,
            split_both,
            P("tensor", None),
            split_both,
            P("tensor"),
            split_both,
            split_both,
            split_both,
        ),
        out_specs=(split_both, split_both, split_both),
        check_vma=False,
    )
```

time: 317 us -> 101 us (0.32)
  the two profiles are of different devices: /device:TPU:249 before, /device:TPU:16 now
where the time goes in v1:
time: 101 us; the launch traced here: 100 us
  starting transfers between devices  37.5 us (37%)
  Pallas kernels  32.6 us (32%)
  waiting for transfers between devices  25.2 us (25%)
  local copies, waits for them, and re-layouts  2.95 us (3%)
  other arithmetic  1.25 us (1%)
  between operations  1.02 us (1%)
    pallas_call x4, Pallas kernels, wave(): pl.pallas_call(functools.partial(wave_kernel, blocks, first, last, len(ar...  25 us
    ppermute x15, starting transfers between devices, send(): return lax.ppermute(x, 'context', where)  23.2 us
    ppermute x15, waiting for transfers between devices, send(): return lax.ppermute(x, 'context', where)  15.6 us
    ppermute x3, starting transfers between devices, back(): return lax.ppermute(x, 'context', [(b, a) for a, b in where])  8.45 us
    pallas_call x1, Pallas kernels, filter_block(): pl.pallas_call(filter_kernel, grid=(channels // tile,), out_shape=[jax.Sh...  6.64 us
    ppermute x3, starting transfers between devices, sum_over_tensor(): x = x + lax.ppermute(x, 'tensor', [(i, i ^ bit) for i in range(8)])  5.8 us
    ppermute x3, waiting for transfers between devices, sum_over_tensor(): x = x + lax.ppermute(x, 'tensor', [(i, i ^ bit) for i in range(8)])  5.59 us
    ppermute x3, waiting for transfers between devices, back(): return lax.ppermute(x, 'context', [(b, a) for a, b in where])  3.95 us
  transfers between devices with their start and end apart: 21, of which 8 were waited for; matrix products, arithmetic and copies ran while one was open for 1% of the time, Pallas kernels for 26%

profile of v1, /device:TPU:16, one launch (start us, length us, event | category | flops | bytes accessed | tf_op | source)
XLA Modules:
  0.0 100.4 jit_solution(16090383566779898292)
XLA Ops:
  0.6 0.9 copy-done
  1.6 0.9 copy-done.1
  2.5 0.9 copy-done.2
  3.5 0.1 pack.1
  3.7 2.0 %collective-permute-start.13 = (bf16[512,128]{1,0:T(8,128)(2,1)S(1)}, bf16[512,128]{1,0:T(8,128)(2,1)S(1)}, u32[]{:S(2)}, u32[]{:S(2)}) collective-permute-start(bf16[512,128]{1,0:T(8,128)(2,1)S(1)} %slice.27), channel_id=1, source_target_pairs={{0,16},{8,24},{16,0},{24,8},{32,48},{40,56},{48,32},{56,40},{64,80... | collective-permute-start | bytes 393224 | tf_op jit(solution)/shard_map/ppermute | solution.py:49
  5.7 1.3 %collective-permute-start.12 = (bf16[512,128]{1,0:T(8,128)(2,1)S(1)}, bf16[512,128]{1,0:T(8,128)(2,1)S(1)}, u32[]{:S(2)}, u32[]{:S(2)}) collective-permute-start(bf16[512,128]{1,0:T(8,128)(2,1)S(1)} %slice.27), channel_id=1, source_target_pairs={{0,128},{8,136},{16,144},{24,152},{32,160},{40,168},{48,176},{56,1... | collective-permute-start | bytes 393224 | tf_op jit(solution)/shard_map/ppermute | solution.py:49
  7.0 5.0 %collective-permute-start.4 = (bf16[768,128]{1,0:T(8,128)(2,1)S(1)}, bf16[768,128]{1,0:T(8,128)(2,1)S(1)}, u32[]{:S(2)}, u32[]{:S(2)}) collective-permute-start(bf16[768,128]{1,0:T(8,128)(2,1)S(1)} %get-tuple-element.22), channel_id=1, source_target_pairs={{0,112},{8,120},{16,32},{24,40},{32,16},{40,24},{48,64},{56,72},{6... | collective-permute-start | bytes 589832 | tf_op jit(solution)/shard_map/ppermute | solution.py:49
  12.0 0.0 collective-permute-start.5
  12.0 4.6 %collective-permute-start.6 = (bf16[768,128]{1,0:T(8,128)(2,1)S(1)}, bf16[768,128]{1,0:T(8,128)(2,1)S(1)}, u32[]{:S(2)}, u32[]{:S(2)}) collective-permute-start(bf16[768,128]{1,0:T(8,128)(2,1)S(1)} %get-tuple-element.24), channel_id=1, source_target_pairs={{0,80},{8,88},{16,64},{24,72},{32,112},{40,120},{48,96},{56,104},{... | collective-permute-start | bytes 589832 | tf_op jit(solution)/shard_map/ppermute | solution.py:49
  16.6 0.0 copy-done.4
  16.6 0.1 multiply_convert_fusion.1
  16.6 8.8 %collective-permute-done.4.refs_1_.refs_5_ = bf16[768,128]{1,0:T(8,128)(2,1)S(1)} collective-permute-done((bf16[768,128]{1,0:T(8,128)(2,1)S(1)}, bf16[768,128]{1,0:T(8,128)(2,1)S(1)}, u32[]{:S(2)}, u32[]{:S(2)}) %collective-permute-start.4) | collective-permute-done | bytes 196640 | tf_op jit(solution)/shard_map/ppermute | solution.py:49
  25.4 1.9 %collective-permute-start = (bf16[128,1024]{1,0:T(8,128)(2,1)S(1)}, bf16[128,1024]{1,0:T(8,128)(2,1)S(1)}, u32[]{:S(2)}, u32[]{:S(2)}) collective-permute-start(bf16[128,1024]{1,0:T(8,128)(2,1)S(1)} %multiply_convert_fusion.1), channel_id=1, source_target_pairs={{0,8},{8,16},{16,24},{24,32},{32,40},{40,48},{48,56},{56,64},{64,7... | collective-permute-start | bytes 786440 | tf_op jit(solution)/shard_map/ppermute | solution.py:49
  27.4 0.0 collective-permute-done.5.refs_2_.refs_6_
  27.4 0.1 collective-permute-start.7
  27.5 0.0 collective-permute-done.13.refs_7_
  27.6 1.3 %collective-permute-start.14 = (bf16[1536,128]{1,0:T(8,128)(2,1)S(1)}, bf16[1536,128]{1,0:T(8,128)(2,1)S(1)}, u32[]{:S(2)}, u32[]{:S(2)}) collective-permute-start(bf16[1536,128]{1,0:T(8,128)(2,1)S(1)} %pad_maximum_fusion.4), channel_id=1, source_target_pairs={{0,128},{8,136},{16,144},{24,152},{32,160},{40,168},{48,176},{56,1... | collective-permute-start | bytes 1179656 | tf_op jit(solution)/shard_map/ppermute | solution.py:49
  28.9 0.0 collective-permute-done.6.refs_3_.refs_4_
  28.9 2.4 %collective-permute-start.9 = (bf16[512,128]{1,0:T(8,128)(2,1)S(1)}, bf16[512,128]{1,0:T(8,128)(2,1)S(1)}, u32[]{:S(2)}, u32[]{:S(2)}) collective-permute-start(bf16[512,128]{1,0:T(8,128)(2,1)S(1)} %slice.28), channel_id=1, source_target_pairs={{0,16},{8,24},{16,0},{24,8},{32,48},{40,56},{48,32},{56,40},{64,80... | collective-permute-start | bytes 393224 | tf_op jit(solution)/shard_map/ppermute | solution.py:49
  31.3 0.0 copy-start.5
  31.3 0.0 copy-start.6
  31.3 0.0 copy-start.7
  31.3 0.0 copy-start.8
  31.3 0.0 copy-start.9
  31.4 0.0 copy-start.10
  31.4 5.7 %collective-permute-done.9.refs_4_ = bf16[512,128]{1,0:T(8,128)(2,1)S(1)} collective-permute-done((bf16[512,128]{1,0:T(8,128)(2,1)S(1)}, bf16[512,128]{1,0:T(8,128)(2,1)S(1)}, u32[]{:S(2)}, u32[]{:S(2)}) %collective-permute-start.9) | collective-permute-done | bytes 131104 | tf_op jit(solution)/shard_map/ppermute | solution.py:49
  37.1 1.3 %collective-permute-start.17 = (bf16[2048,128]{1,0:T(8,128)(2,1)S(1)}, bf16[2048,128]{1,0:T(8,128)(2,1)S(1)}, u32[]{:S(2)}, u32[]{:S(2)}) collective-permute-start(bf16[2048,128]{1,0:T(8,128)(2,1)S(1)} %pad_maximum_fusion.2), channel_id=1, source_target_pairs={{0,8},{8,0},{16,24},{24,16},{32,40},{40,32},{48,56},{56,48},{64,72... | collective-permute-start | bytes 1572872 | tf_op jit(solution)/shard_map/ppermute | solution.py:49
  38.3 0.0 collective-permute-done.7.refs_5_
  38.3 1.3 %collective-permute-start.10 = (bf16[512,128]{1,0:T(8,128)(2,1)S(1)}, bf16[512,128]{1,0:T(8,128)(2,1)S(1)}, u32[]{:S(2)}, u32[]{:S(2)}) collective-permute-start(bf16[512,128]{1,0:T(8,128)(2,1)S(1)} %collective-permute-done.9.refs_4_), channel_id=1, source_target_pairs={{0,128},{8,136},{16,144},{24,152},{32,160},{40,168},{48,176},{56,1... | collective-permute-start | bytes 393224 | tf_op jit(solution)/shard_map/ppermute | solution.py:49
  39.7 0.0 collective-permute-done.12.refs_6_
  39.7 1.3 %collective-permute-start.8 = (bf16[1536,128]{1,0:T(8,128)(2,1)S(1)}, bf16[1536,128]{1,0:T(8,128)(2,1)S(1)}, u32[]{:S(2)}, u32[]{:S(2)}) collective-permute-start(bf16[1536,128]{1,0:T(8,128)(2,1)S(1)} %pad_maximum_fusion.3), channel_id=1, source_target_pairs={{0,128},{8,136},{16,144},{24,152},{32,160},{40,168},{48,176},{56,1... | collective-permute-start | bytes 1179656 | tf_op jit(solution)/shard_map/ppermute | solution.py:49
  41.0 1.1 %collective-permute-done.14.refs_7_ = bf16[1536,128]{1,0:T(8,128)(2,1)S(1)} collective-permute-done((bf16[1536,128]{1,0:T(8,128)(2,1)S(1)}, bf16[1536,128]{1,0:T(8,128)(2,1)S(1)}, u32[]{:S(2)}, u32[]{:S(2)}) %collective-permute-start.14) | collective-permute-done | bytes 393248 | tf_op jit(solution)/shard_map/ppermute | solution.py:49
  42.1 0.1 collective-permute-start.15
  42.2 0.0 collective-permute-done.halo_ref
  42.3 6.6 %filter.1 = (bf16[256,1024]{1,0:T(8,128)(2,1)}, f32[8,256]{1,0:T(8,128)S(1)}) custom-call(bf16[384,384]{1,0:T(8,128)(2,1)S(1)} %copy-done.8, bf16[384,384]{1,0:T(8,128)(2,1)S(1)} %copy-done.9, bf16[256,384]{1,0:T(8,128)(2,1)S(1)} %copy-done.10, bf16[256,384]{1,0:T(8,128)(2,1)S(1)} %copy-done.11, bf16[256,1024]{1,0:T(8,128)(2,1)S(1)} %copy-done.3, ...), custom_call_target="tpu_custom_call" | custom-call | flops 1500000000 | bytes 5242880 | tf_op jit(solution)/shard_map/filter/pallas_call | solution.py:357
  49.0 1.5 %collective-permute-start.1 = (f32[256]{0:T(256)S(1)}, f32[256]{0:T(256)S(1)}, u32[]{:S(2)}, u32[]{:S(2)}) collective-permute-start(f32[256]{0:T(256)S(1)} %bitcast.1), channel_id=1, source_target_pairs={{0,1},{1,0},{2,3},{3,2},{4,5},{5,4},{6,7},{7,6},{8,9},{9,8},{10,11... | collective-permute-start | bytes 3080 | tf_op jit(solution)/shard_map/ppermute | solution.py:381
  50.4 2.1 %collective-permute-done.1 = f32[256]{0:T(256)S(1)} collective-permute-done((f32[256]{0:T(256)S(1)}, f32[256]{0:T(256)S(1)}, u32[]{:S(2)}, u32[]{:S(2)}) %collective-permute-start.1) | collective-permute-done | bytes 1056 | tf_op jit(solution)/shard_map/ppermute | solution.py:381
  52.5 3.0 %collective-permute-start.2 = (f32[256]{0:T(256)S(1)}, f32[256]{0:T(256)S(1)}, u32[]{:S(2)}, u32[]{:S(2)}) collective-permute-start(f32[256]{0:T(256)S(1)} %add.16), channel_id=1, source_target_pairs={{0,2},{1,3},{2,0},{3,1},{4,6},{5,7},{6,4},{7,5},{8,10},{9,11},{10,... | collective-permute-start | bytes 3080 | tf_op jit(solution)/shard_map/ppermute | solution.py:381
  55.6 2.0 %collective-permute-done.2 = f32[256]{0:T(256)S(1)} collective-permute-done((f32[256]{0:T(256)S(1)}, f32[256]{0:T(256)S(1)}, u32[]{:S(2)}, u32[]{:S(2)}) %collective-permute-start.2) | collective-permute-done | bytes 1056 | tf_op jit(solution)/shard_map/ppermute | solution.py:381
  57.6 1.3 %collective-permute-start.3 = (f32[256]{0:T(256)S(1)}, f32[256]{0:T(256)S(1)}, u32[]{:S(2)}, u32[]{:S(2)}) collective-permute-start(f32[256]{0:T(256)S(1)} %add.17), channel_id=1, source_target_pairs={{0,4},{1,5},{2,6},{3,7},{4,0},{5,1},{6,2},{7,3},{8,12},{9,13},{10,... | collective-permute-start | bytes 3080 | tf_op jit(solution)/shard_map/ppermute | solution.py:381
  58.9 0.0 collective-permute-done.10.refs_5_
  58.9 0.0 collective-permute-start.16
  58.9 0.0 collective-permute-done.8.refs_4_
  58.9 0.8 collective-permute-start.11
  59.7 1.5 %collective-permute-done.3 = f32[256]{0:T(256)S(1)} collective-permute-done((f32[256]{0:T(256)S(1)}, f32[256]{0:T(256)S(1)}, u32[]{:S(2)}, u32[]{:S(2)}) %collective-permute-start.3) | collective-permute-done | bytes 1056 | tf_op jit(solution)/shard_map/ppermute | solution.py:381
  61.2 0.0 collective-permute-done.17.refs_8_
  61.2 6.2 %wave.4 = (f32[1024,256]{1,0:T(8,128)S(1)}, f32[1024,128]{1,0:T(8,128)S(1)}) custom-call(bf16[768,128]{1,0:T(8,128)(2,1)S(1)} %get-tuple-element.21.refs_0_.refs_4_, bf16[768,128]{1,0:T(8,128)(2,1)S(1)} %collective-permute-done.4.refs_1_.refs_5_, bf16[768,128]{1,0:T(8,128)(2,1)S(1)} %collective-permute-done.5.refs_2_.refs_6_, ...), custom_call_target="tpu_custom_call" | custom-call | flops 1073741824 | bytes 2031616 | tf_op jit(solution)/shard_map/wave/pallas_call | solution.py:207
  67.4 0.0 collective-permute-done.16.refs_6_
  67.4 4.9 %wave.5 = (f32[1024,256]{1,0:T(8,128)S(1)}, f32[1024,128]{1,0:T(8,128)S(1)}) custom-call(bf16[768,128]{1,0:T(8,128)(2,1)S(1)} %get-tuple-element.21.refs_0_.refs_4_, bf16[768,128]{1,0:T(8,128)(2,1)S(1)} %collective-permute-done.4.refs_1_.refs_5_, bf16[768,128]{1,0:T(8,128)(2,1)S(1)} %collective-permute-done.5.refs_2_.refs_6_, ...), custom_call_target="tpu_custom_call" | custom-call | flops 805306368 | bytes 3211264 | tf_op jit(solution)/shard_map/wave/pallas_call | solution.py:207
  72.3 0.0 collective-permute-done.15.refs_5_
  72.3 8.1 %wave.6 = (f32[1024,256]{1,0:T(8,128)S(1)}, f32[1024,128]{1,0:T(8,128)S(1)}) custom-call(bf16[768,128]{1,0:T(8,128)(2,1)S(1)} %get-tuple-element.21.refs_0_.refs_4_, bf16[768,128]{1,0:T(8,128)(2,1)S(1)} %collective-permute-done.4.refs_1_.refs_5_, bf16[768,128]{1,0:T(8,128)(2,1)S(1)} %collective-permute-done.5.refs_2_.refs_6_, ...), custom_call_target="tpu_custom_call" | custom-call | flops 1342177280 | bytes 3670016 | tf_op jit(solution)/shard_map/wave/pallas_call | solution.py:207
  80.5 0.0 collective-permute-done.11.refs_6_
  80.5 0.0 copy-start.12
  80.5 0.0 copy-start.13
  80.5 5.8 %wave.7 = (bf16[256,128]{1,0:T(8,128)(2,1)S(1)}, bf16[256,128]{1,0:T(8,128)(2,1)S(1)}, bf16[256,128]{1,0:T(8,128)(2,1)S(1)}, bf16[256,128]{1,0:T(8,128)(2,1)S(1)}) custom-call(bf16[768,128]{1,0:T(8,128)(2,1)S(1)} %get-tuple-element.21.refs_0_.refs_4_, bf16[768,128]{1,0:T(8,128)(2,1)S(1)} %collective-permute-done.4.refs_1_.refs_5_, ...), custom_call_target="tpu_custom_call" | custom-call | flops 1073741824 | bytes 3407872 | tf_op jit(solution)/shard_map/wave/pallas_call | solution.py:207
  86.3 6.0 %collective-permute-start.18 = (bf16[256,128]{1,0:T(8,128)(2,1)S(1)}, bf16[256,128]{1,0:T(8,128)(2,1)S(1)}, u32[]{:S(2)}, u32[]{:S(2)}) collective-permute-start(bf16[256,128]{1,0:T(8,128)(2,1)S(1)} %get-tuple-element.32), channel_id=1, source_target_pairs={{112,0},{120,8},{32,16},{40,24},{16,32},{24,40},{64,48},{72,56},{4... | collective-permute-start | bytes 196616 | tf_op jit(solution)/shard_map/ppermute | solution.py:53
  92.3 0.0 collective-permute-start.19
  92.3 2.4 %collective-permute-start.20 = (bf16[256,128]{1,0:T(8,128)(2,1)S(1)}, bf16[256,128]{1,0:T(8,128)(2,1)S(1)}, u32[]{:S(2)}, u32[]{:S(2)}) collective-permute-start(bf16[256,128]{1,0:T(8,128)(2,1)S(1)} %get-tuple-element.34), channel_id=1, source_target_pairs={{80,0},{88,8},{64,16},{72,24},{112,32},{120,40},{96,48},{104,56},{... | collective-permute-start | bytes 196616 | tf_op jit(solution)/shard_map/ppermute | solution.py:53
  94.7 0.0 copy-done.13
  94.8 1.0 multiply_convert_fusion
  95.7 0.0 collective-permute-done.18.o1
  95.7 1.7 %collective-permute-done.19.o2 = bf16[256,128]{1,0:T(8,128)(2,1)S(1)} collective-permute-done((bf16[256,128]{1,0:T(8,128)(2,1)S(1)}, bf16[256,128]{1,0:T(8,128)(2,1)S(1)}, u32[]{:S(2)}, u32[]{:S(2)}) %collective-permute-start.19) | collective-permute-done | bytes 65568 | tf_op jit(solution)/shard_map/ppermute | solution.py:53
  97.5 2.2 %collective-permute-done.20.o3 = bf16[256,128]{1,0:T(8,128)(2,1)S(1)} collective-permute-done((bf16[256,128]{1,0:T(8,128)(2,1)S(1)}, bf16[256,128]{1,0:T(8,128)(2,1)S(1)}, u32[]{:S(2)}, u32[]{:S(2)}) %collective-permute-start.20) | collective-permute-done | bytes 65568 | tf_op jit(solution)/shard_map/ppermute | solution.py:53
  99.7 0.8 unpack.1
  (29 shorter events, 0.3 us)
Async XLA Ops:
  0.6 1.0 copy-start
  1.6 0.9 copy-start.1
  2.5 0.9 copy-start.2
  3.5 13.1 %copy-start.3 = (bf16[256,1024]{1,0:T(8,128)(2,1)S(1)}, bf16[256,1024]{1,0:T(8,128)(2,1)}, u32[]{:S(2)}) copy-start(bf16[256,1024]{1,0:T(8,128)(2,1)} %key_ref.1) | copy-start | bytes 1572868
  3.5 13.1 %copy-start.4 = (bf16[256,1024]{1,0:T(8,128)(2,1)S(1)}, bf16[256,1024]{1,0:T(8,128)(2,1)}, u32[]{:S(2)}) copy-start(bf16[256,1024]{1,0:T(8,128)(2,1)} %value_ref.1) | copy-start | bytes 1572868
  3.7 23.9 %collective-permute-start.13 = (bf16[512,128]{1,0:T(8,128)(2,1)S(1)}, bf16[512,128]{1,0:T(8,128)(2,1)S(1)}, u32[]{:S(2)}, u32[]{:S(2)}) collective-permute-start(bf16[512,128]{1,0:T(8,128)(2,1)S(1)} %slice.27), channel_id=1, source_target_pairs={{0,16},{8,24},{16,0},{24,8},{32,48},{40,56},{48,32},{56,40},{64,80... | collective-permute-start | bytes 393224 | tf_op jit(solution)/shard_map/ppermute | solution.py:49
  5.7 34.0 %collective-permute-start.12 = (bf16[512,128]{1,0:T(8,128)(2,1)S(1)}, bf16[512,128]{1,0:T(8,128)(2,1)S(1)}, u32[]{:S(2)}, u32[]{:S(2)}) collective-permute-start(bf16[512,128]{1,0:T(8,128)(2,1)S(1)} %slice.27), channel_id=1, source_target_pairs={{0,128},{8,136},{16,144},{24,152},{32,160},{40,168},{48,176},{56,1... | collective-permute-start | bytes 393224 | tf_op jit(solution)/shard_map/ppermute | solution.py:49
  7.0 18.5 %collective-permute-start.4 = (bf16[768,128]{1,0:T(8,128)(2,1)S(1)}, bf16[768,128]{1,0:T(8,128)(2,1)S(1)}, u32[]{:S(2)}, u32[]{:S(2)}) collective-permute-start(bf16[768,128]{1,0:T(8,128)(2,1)S(1)} %get-tuple-element.22), channel_id=1, source_target_pairs={{0,112},{8,120},{16,32},{24,40},{32,16},{40,24},{48,64},{56,72},{6... | collective-permute-start | bytes 589832 | tf_op jit(solution)/shard_map/ppermute | solution.py:49
  12.0 15.4 %collective-permute-start.5 = (bf16[768,128]{1,0:T(8,128)(2,1)S(1)}, bf16[768,128]{1,0:T(8,128)(2,1)S(1)}, u32[]{:S(2)}, u32[]{:S(2)}) collective-permute-start(bf16[768,128]{1,0:T(8,128)(2,1)S(1)} %get-tuple-element.23), channel_id=1, source_target_pairs={{0,32},{8,40},{16,112},{24,120},{32,64},{40,72},{48,16},{56,24},{6... | collective-permute-start | bytes 589832 | tf_op jit(solution)/shard_map/ppermute | solution.py:49
  12.0 16.9 %collective-permute-start.6 = (bf16[768,128]{1,0:T(8,128)(2,1)S(1)}, bf16[768,128]{1,0:T(8,128)(2,1)S(1)}, u32[]{:S(2)}, u32[]{:S(2)}) collective-permute-start(bf16[768,128]{1,0:T(8,128)(2,1)S(1)} %get-tuple-element.24), channel_id=1, source_target_pairs={{0,80},{8,88},{16,64},{24,72},{32,112},{40,120},{48,96},{56,104},{... | collective-permute-start | bytes 589832 | tf_op jit(solution)/shard_map/ppermute | solution.py:49
  25.4 16.8 %collective-permute-start = (bf16[128,1024]{1,0:T(8,128)(2,1)S(1)}, bf16[128,1024]{1,0:T(8,128)(2,1)S(1)}, u32[]{:S(2)}, u32[]{:S(2)}) collective-permute-start(bf16[128,1024]{1,0:T(8,128)(2,1)S(1)} %multiply_convert_fusion.1), channel_id=1, source_target_pairs={{0,8},{8,16},{16,24},{24,32},{32,40},{40,48},{48,56},{56,64},{64,7... | collective-permute-start | bytes 786440 | tf_op jit(solution)/shard_map/ppermute | solution.py:49
  27.4 10.9 %collective-permute-start.7 = (bf16[1024,128]{1,0:T(8,128)(2,1)S(1)}, bf16[1024,128]{1,0:T(8,128)(2,1)S(1)}, u32[]{:S(2)}, u32[]{:S(2)}) collective-permute-start(bf16[1024,128]{1,0:T(8,128)(2,1)S(1)} %pad_maximum_fusion.5), channel_id=1, source_target_pairs={{0,16},{8,24},{16,0},{24,8},{32,48},{40,56},{48,32},{56,40},{64,80... | collective-permute-start | bytes 786440 | tf_op jit(solution)/shard_map/ppermute | solution.py:49
  27.6 14.5 %collective-permute-start.14 = (bf16[1536,128]{1,0:T(8,128)(2,1)S(1)}, bf16[1536,128]{1,0:T(8,128)(2,1)S(1)}, u32[]{:S(2)}, u32[]{:S(2)}) collective-permute-start(bf16[1536,128]{1,0:T(8,128)(2,1)S(1)} %pad_maximum_fusion.4), channel_id=1, source_target_pairs={{0,128},{8,136},{16,144},{24,152},{32,160},{40,168},{48,176},{56,1... | collective-permute-start | bytes 1179656 | tf_op jit(solution)/shard_map/ppermute | solution.py:49
  28.9 8.2 %collective-permute-start.9 = (bf16[512,128]{1,0:T(8,128)(2,1)S(1)}, bf16[512,128]{1,0:T(8,128)(2,1)S(1)}, u32[]{:S(2)}, u32[]{:S(2)}) collective-permute-start(bf16[512,128]{1,0:T(8,128)(2,1)S(1)} %slice.28), channel_id=1, source_target_pairs={{0,16},{8,24},{16,0},{24,8},{32,48},{40,56},{48,32},{56,40},{64,80... | collective-permute-start | bytes 393224 | tf_op jit(solution)/shard_map/ppermute | solution.py:49
  31.3 11.0 %copy-start.11 = (bf16[256,384]{1,0:T(8,128)(2,1)S(1)}, bf16[256,384]{1,0:T(8,128)(2,1)}, u32[]{:S(2)}) copy-start(bf16[256,384]{1,0:T(8,128)(2,1)} %constant.16.clone.gl_ref) | copy-start | bytes 589828
  31.3 11.0 %copy-start.5 = (bf16[256,1024]{1,0:T(8,128)(2,1)S(1)}, bf16[256,1024]{1,0:T(8,128)(2,1)}, u32[]{:S(2)}) copy-start(bf16[256,1024]{1,0:T(8,128)(2,1)} %gate_ref.1) | copy-start | bytes 1572868
  31.3 11.0 %copy-start.6 = (bf16[256,1024]{1,0:T(8,128)(2,1)S(1)}, bf16[256,1024]{1,0:T(8,128)(2,1)}, u32[]{:S(2)}) copy-start(bf16[256,1024]{1,0:T(8,128)(2,1)} %res_ref.1) | copy-start | bytes 1572868
  31.3 11.0 %copy-start.7 = (bf16[1024,128]{1,0:T(8,128)(2,1)S(1)}, bf16[1024,128]{1,0:T(8,128)(2,1)}, u32[]{:S(2)}) copy-start(bf16[1024,128]{1,0:T(8,128)(2,1)} %taps_ref.1) | copy-start | bytes 786436
  31.3 11.0 %copy-start.8 = (bf16[384,384]{1,0:T(8,128)(2,1)S(1)}, bf16[384,384]{1,0:T(8,128)(2,1)}, u32[]{:S(2)}) copy-start(bf16[384,384]{1,0:T(8,128)(2,1)} %constant.13.clone.fh_ref) | copy-start | bytes 884740
  31.3 11.0 %copy-start.9 = (bf16[384,384]{1,0:T(8,128)(2,1)S(1)}, bf16[384,384]{1,0:T(8,128)(2,1)}, u32[]{:S(2)}) copy-start(bf16[384,384]{1,0:T(8,128)(2,1)} %constant.14.clone.fl_ref) | copy-start | bytes 884740
  31.4 10.9 %copy-start.10 = (bf16[256,384]{1,0:T(8,128)(2,1)S(1)}, bf16[256,384]{1,0:T(8,128)(2,1)}, u32[]{:S(2)}) copy-start(bf16[256,384]{1,0:T(8,128)(2,1)} %constant.15.clone.gh_ref) | copy-start | bytes 589828
  37.1 24.1 %collective-permute-start.17 = (bf16[2048,128]{1,0:T(8,128)(2,1)S(1)}, bf16[2048,128]{1,0:T(8,128)(2,1)S(1)}, u32[]{:S(2)}, u32[]{:S(2)}) collective-permute-start(bf16[2048,128]{1,0:T(8,128)(2,1)S(1)} %pad_maximum_fusion.2), channel_id=1, source_target_pairs={{0,8},{8,0},{16,24},{24,16},{32,40},{40,32},{48,56},{56,48},{64,72... | collective-permute-start | bytes 1572872 | tf_op jit(solution)/shard_map/ppermute | solution.py:49
  38.3 20.5 %collective-permute-start.10 = (bf16[512,128]{1,0:T(8,128)(2,1)S(1)}, bf16[512,128]{1,0:T(8,128)(2,1)S(1)}, u32[]{:S(2)}, u32[]{:S(2)}) collective-permute-start(bf16[512,128]{1,0:T(8,128)(2,1)S(1)} %collective-permute-done.9.refs_4_), channel_id=1, source_target_pairs={{0,128},{8,136},{16,144},{24,152},{32,160},{40,168},{48,176},{56,1... | collective-permute-start | bytes 393224 | tf_op jit(solution)/shard_map/ppermute | solution.py:49
  39.7 19.2 %collective-permute-start.8 = (bf16[1536,128]{1,0:T(8,128)(2,1)S(1)}, bf16[1536,128]{1,0:T(8,128)(2,1)S(1)}, u32[]{:S(2)}, u32[]{:S(2)}) collective-permute-start(bf16[1536,128]{1,0:T(8,128)(2,1)S(1)} %pad_maximum_fusion.3), channel_id=1, source_target_pairs={{0,128},{8,136},{16,144},{24,152},{32,160},{40,168},{48,176},{56,1... | collective-permute-start | bytes 1179656 | tf_op jit(solution)/shard_map/ppermute | solution.py:49
  42.1 30.2 %collective-permute-start.15 = (bf16[2560,128]{1,0:T(8,128)(2,1)S(1)}, bf16[2560,128]{1,0:T(8,128)(2,1)S(1)}, u32[]{:S(2)}, u32[]{:S(2)}) collective-permute-start(bf16[2560,128]{1,0:T(8,128)(2,1)S(1)} %pad_maximum_fusion), channel_id=1, source_target_pairs={{0,8},{8,0},{16,24},{24,16},{32,40},{40,32},{48,56},{56,48},{64,72... | collective-permute-start | bytes 1966088 | tf_op jit(solution)/shard_map/ppermute | solution.py:49
  49.0 3.6 %collective-permute-start.1 = (f32[256]{0:T(256)S(1)}, f32[256]{0:T(256)S(1)}, u32[]{:S(2)}, u32[]{:S(2)}) collective-permute-start(f32[256]{0:T(256)S(1)} %bitcast.1), channel_id=1, source_target_pairs={{0,1},{1,0},{2,3},{3,2},{4,5},{5,4},{6,7},{7,6},{8,9},{9,8},{10,11... | collective-permute-start | bytes 3080 | tf_op jit(solution)/shard_map/ppermute | solution.py:381
  52.5 5.1 %collective-permute-start.2 = (f32[256]{0:T(256)S(1)}, f32[256]{0:T(256)S(1)}, u32[]{:S(2)}, u32[]{:S(2)}) collective-permute-start(f32[256]{0:T(256)S(1)} %add.16), channel_id=1, source_target_pairs={{0,2},{1,3},{2,0},{3,1},{4,6},{5,7},{6,4},{7,5},{8,10},{9,11},{10,... | collective-permute-start | bytes 3080 | tf_op jit(solution)/shard_map/ppermute | solution.py:381
  57.6 3.6 %collective-permute-start.3 = (f32[256]{0:T(256)S(1)}, f32[256]{0:T(256)S(1)}, u32[]{:S(2)}, u32[]{:S(2)}) collective-permute-start(f32[256]{0:T(256)S(1)} %add.17), channel_id=1, source_target_pairs={{0,4},{1,5},{2,6},{3,7},{4,0},{5,1},{6,2},{7,3},{8,12},{9,13},{10,... | collective-permute-start | bytes 3080 | tf_op jit(solution)/shard_map/ppermute | solution.py:381
  58.9 8.5 %collective-permute-start.16 = (bf16[1536,128]{1,0:T(8,128)(2,1)S(1)}, bf16[1536,128]{1,0:T(8,128)(2,1)S(1)}, u32[]{:S(2)}, u32[]{:S(2)}) collective-permute-start(bf16[1536,128]{1,0:T(8,128)(2,1)S(1)} %pad_maximum_fusion.3), channel_id=1, source_target_pairs={{0,8},{8,0},{16,24},{24,16},{32,40},{40,32},{48,56},{56,48},{64,72... | collective-permute-start | bytes 1179656 | tf_op jit(solution)/shard_map/ppermute | solution.py:49
  58.9 21.5 %collective-permute-start.11 = (bf16[2048,128]{1,0:T(8,128)(2,1)S(1)}, bf16[2048,128]{1,0:T(8,128)(2,1)S(1)}, u32[]{:S(2)}, u32[]{:S(2)}) collective-permute-start(bf16[2048,128]{1,0:T(8,128)(2,1)S(1)} %pad_maximum_fusion.1), channel_id=1, source_target_pairs={{0,8},{8,0},{16,24},{24,16},{32,40},{40,32},{48,56},{56,48},{64,72... | collective-permute-start | bytes 1572872 | tf_op jit(solution)/shard_map/ppermute | solution.py:49
  80.5 14.3 %copy-start.12 = (bf16[256,1024]{1,0:T(8,128)(2,1)S(1)}, bf16[256,1024]{1,0:T(8,128)(2,1)}, u32[]{:S(2)}) copy-start(bf16[256,1024]{1,0:T(8,128)(2,1)} %get-tuple-element.16) | copy-start | bytes 1572868
  80.5 14.3 %copy-start.13 = (f32[1024]{0:T(1024)S(1)}, f32[1024]{0:T(1024)}, u32[]{:S(2)}) copy-start(f32[1024]{0:T(1024)} %param.18) | copy-start | bytes 12292
  86.3 9.4 %collective-permute-start.18 = (bf16[256,128]{1,0:T(8,128)(2,1)S(1)}, bf16[256,128]{1,0:T(8,128)(2,1)S(1)}, u32[]{:S(2)}, u32[]{:S(2)}) collective-permute-start(bf16[256,128]{1,0:T(8,128)(2,1)S(1)} %get-tuple-element.32), channel_id=1, source_target_pairs={{112,0},{120,8},{32,16},{40,24},{16,32},{24,40},{64,48},{72,56},{4... | collective-permute-start | bytes 196616 | tf_op jit(solution)/shard_map/ppermute | solution.py:53
  92.3 5.2 %collective-permute-start.19 = (bf16[256,128]{1,0:T(8,128)(2,1)S(1)}, bf16[256,128]{1,0:T(8,128)(2,1)S(1)}, u32[]{:S(2)}, u32[]{:S(2)}) collective-permute-start(bf16[256,128]{1,0:T(8,128)(2,1)S(1)} %get-tuple-element.33), channel_id=1, source_target_pairs={{32,0},{40,8},{112,16},{120,24},{64,32},{72,40},{16,48},{24,56},{9... | collective-permute-start | bytes 196616 | tf_op jit(solution)/shard_map/ppermute | solution.py:53
  92.3 7.4 %collective-permute-start.20 = (bf16[256,128]{1,0:T(8,128)(2,1)S(1)}, bf16[256,128]{1,0:T(8,128)(2,1)S(1)}, u32[]{:S(2)}, u32[]{:S(2)}) collective-permute-start(bf16[256,128]{1,0:T(8,128)(2,1)S(1)} %get-tuple-element.34), channel_id=1, source_target_pairs={{80,0},{88,8},{64,16},{72,24},{112,32},{120,40},{96,48},{104,56},{... | collective-permute-start | bytes 196616 | tf_op jit(solution)/shard_map/ppermute | solution.py:53

commit v2 on v1

v2 whole, which is shorter than its diff:
```python
import functools
import math

import jax
import jax.numpy as jnp
import ml_dtypes
import numpy as np
from jax import lax
from jax.experimental import pallas as pl
from jax.experimental.pallas import tpu as pltpu
from jax.sharding import PartitionSpec as P

D = 8192
DH = 128
ROWS = 256
TAPS = 128
SPAN = 2 * TAPS
ZS = 8
LOG2E_SCALE = math.log2(math.e) / math.sqrt(DH)
LOW = -1e30
F32 = jnp.float32
BF16 = jnp.bfloat16


def pairs(where):
    out = []
    for plane in range(2):
        for z in range(ZS):
            for core in range(2):
                to = where(plane, z, core)
                if to is not None:
                    p, zz, c = to
                    out.append(((plane * ZS + z) * 2 + core, (p * ZS + zz % ZS) * 2 + c))
    return out


def hop(steps):
    return pairs(lambda p, z, c: (p, z + steps[z % 2], c))


NEAR = [None, hop((-1, 1)), hop((2, -2)), hop((-3, 3))]
SIBLING = pairs(lambda p, z, c: (p, z ^ 1, c))
CORE = pairs(lambda p, z, c: (p, z, 1 - c))
DOWN = pairs(lambda p, z, c: (1, z, c) if p == 0 else None)
NEXT = [(i, i + 1) for i in range(2 * ZS * 2 - 1)]


def send(x, where):
    return lax.ppermute(x, "context", where)


def back(x, where):
    return lax.ppermute(x, "context", [(b, a) for a, b in where])


def place():
    index = lax.axis_index("context")
    core = lax.rem(index, 2)
    z = lax.rem(lax.div(index, 2), ZS)
    plane = lax.div(index, 2 * ZS)
    return plane, z, core


def target_heads(z):
    odd = lax.rem(z, 2)
    offsets = [0, -1 + 2 * odd, 2 - 4 * odd, -3 + 6 * odd]
    return [lax.div(lax.rem(z + o + ZS, ZS), 2) for o in offsets]


def pack_kernel(
    q_ref, k_ref, v_ref, key_ref, value_ref, edge, o0, o1, o2, o3, own, key_tail, value_tail, sems
):
    _, z, _ = place()
    tails = [
        pltpu.make_async_copy(ref.at[ROWS - TAPS : ROWS, :], tail, sems.at[12 + n])
        for n, (ref, tail) in enumerate(((key_ref, key_tail), (value_ref, value_tail)))
    ]
    copies = []
    for j, (head, out) in enumerate(zip(target_heads(z), (o0, o1, o2, o3))):
        columns = pl.ds(pl.multiple_of(head * DH, DH), DH)
        for n, ref in enumerate((q_ref, k_ref, v_ref)):
            copies.append(
                pltpu.make_async_copy(
                    ref.at[:, columns], out.at[n * ROWS : (n + 1) * ROWS, :], sems.at[3 * j + n]
                )
            )
    columns = pl.ds(pl.multiple_of(target_heads(z)[0] * DH, DH), DH)
    for n, ref in enumerate((k_ref, v_ref)):
        copies.append(
            pltpu.make_async_copy(
                ref.at[:, columns], own.at[n * ROWS : (n + 1) * ROWS, :], sems.at[14 + n]
            )
        )
    for copy in copies + tails:
        copy.start()
    for copy in tails:
        copy.wait()
    edge[...] = (key_tail[...].astype(F32) * value_tail[...].astype(F32)).astype(BF16)
    for copy in copies:
        copy.wait()


def pack(q, k, v, key, value):
    channels = key.shape[1]
    return pl.pallas_call(
        pack_kernel,
        out_shape=[jax.ShapeDtypeStruct((TAPS, channels), BF16)]
        + [jax.ShapeDtypeStruct((3 * ROWS, DH), BF16)] * 4
        + [jax.ShapeDtypeStruct((2 * ROWS, DH), BF16)],
        in_specs=[pl.BlockSpec(memory_space=pltpu.HBM)] * 5,
        out_specs=[pl.BlockSpec(memory_space=pltpu.VMEM)] * 6,
        scratch_shapes=[pltpu.VMEM((TAPS, channels), BF16)] * 2
        + [pltpu.SemaphoreType.DMA((16,))],
        compiler_params=pltpu.CompilerParams(vmem_limit_bytes=60 << 20),
        name="pack",
    )(q, k, v, key, value)


def unpack_kernel(o0, o1, o2, o3, out):
    _, z, _ = place()
    for head, piece in zip(target_heads(z), (o0, o1, o2, o3)):
        out[:, pl.ds(pl.multiple_of(head * DH, DH), DH)] = piece[...]


def unpack(pieces):
    return pl.pallas_call(
        unpack_kernel,
        out_shape=jax.ShapeDtypeStruct((ROWS, 4 * DH), BF16),
        in_specs=[pl.BlockSpec(memory_space=pltpu.VMEM)] * 4,
        out_specs=pl.BlockSpec(memory_space=pltpu.VMEM),
        compiler_params=pltpu.CompilerParams(vmem_limit_bytes=16 << 20),
        name="unpack",
    )(*pieces)


def wave_kernel(blocks, first, last, count, *refs):
    q_refs = refs[:4]
    array_refs = refs[4 : 4 + count]
    rest = refs[4 + count :]
    if not first:
        acc_in, high_in = rest[:2]
        rest = rest[2:]
    if last:
        outs = rest[:4]
        rest = rest[4:]
    else:
        acc, high = rest[:2]
        rest = rest[2:]
    s_all, values_all = rest
    plane, z, core = place()
    odd = lax.rem(z, 2)
    sign = 2 * odd - 1
    skew = lax.broadcasted_iota(jnp.int32, (ROWS, ROWS), 1) - lax.broadcasted_iota(
        jnp.int32, (ROWS, ROWS), 0
    )
    values_all[:, DH:] = jnp.ones((values_all.shape[0], DH), BF16)

    def source(far, j):
        if far:
            return lax.rem((z + 1 - 2 * odd) - sign * j + ZS, ZS)
        return lax.rem(z + sign * j + ZS, ZS)

    def run(chosen):
        width = len(chosen) * ROWS
        for n, (array, k_row, v_row, lower, far, j, other) in enumerate(chosen):
            values_all[n * ROWS : (n + 1) * ROWS, :DH] = array_refs[array][v_row : v_row + ROWS, :]

        def scores(i):
            q = q_refs[i][0:ROWS, :]
            q_block = 2 * lax.rem(z + sign * i + ZS, ZS) + core
            old = None if first else high_in[i * ROWS : (i + 1) * ROWS, :]
            top = old
            for n, (array, k_row, v_row, lower, far, j, other) in enumerate(chosen):
                keys = array_refs[array][k_row : k_row + ROWS, :]
                s = lax.dot_general(
                    q, keys, (((1,), (1,)), ((), ())), preferred_element_type=F32
                )
                if not lower:
                    k_block = 2 * source(far, j) + (1 - core if other else core)
                    s = jnp.where(skew <= (q_block - k_block) * ROWS, s, LOW)
                s_all[i % 2, :, n * ROWS : (n + 1) * ROWS] = s
                pair = jnp.maximum(s[:, :DH], s[:, DH:])
                top = pair if top is None else jnp.maximum(top, pair)
            best = jnp.max(top, axis=1, keepdims=True)
            scale = None if first else jnp.exp2((old[:, :1] - best) * LOG2E_SCALE)
            return best, scale

        def weigh(i, best, scale):
            rows = slice(i * ROWS, (i + 1) * ROWS)
            p = jnp.exp2((s_all[i % 2, :, :width] - best) * LOG2E_SCALE).astype(BF16)
            total = jnp.dot(p, values_all[:width, :], preferred_element_type=F32)
            if not first:
                total = total + acc_in[rows, :] * scale
            if last:
                outs[i][...] = (total[:, :DH] / total[:, DH:]).astype(BF16)
            else:
                acc[rows, :] = total
                high[rows, :] = jnp.broadcast_to(best, (ROWS, DH))

        state = scores(0)
        for i in range(4):
            following = scores(i + 1) if i < 3 else None
            weigh(i, *state)
            state = following

    def keep():
        if last:
            for i in range(4):
                part = acc_in[i * ROWS : (i + 1) * ROWS, :]
                outs[i][...] = (part[:, :DH] / part[:, DH:]).astype(BF16)
        else:
            acc[...] = acc_in[...]
            high[...] = high_in[...]

    own = [b for b in blocks if not b[3]]
    if len(own) == len(blocks):
        run(own)
    else:

        @pl.when(plane == 1)
        def _():
            run(blocks)

        @pl.when(plane == 0)
        def _():
            if own:
                run(own)
            else:
                keep()


SMALL = pl.CostEstimate(flops=1024, bytes_accessed=1024, transcendentals=0)


def wave(q_arrays, arrays, blocks, state, last=False):
    first = state is None
    width = len(blocks) * ROWS
    state_shapes = [((4 * ROWS, 2 * DH), F32), ((4 * ROWS, DH), F32)]
    vmem = pl.BlockSpec(memory_space=pltpu.VMEM)
    if last:
        out_shape = [jax.ShapeDtypeStruct((ROWS, DH), BF16)] * 4
    else:
        out_shape = [jax.ShapeDtypeStruct(s, d) for s, d in state_shapes]
    operands = list(q_arrays) + list(arrays) + ([] if first else list(state))
    tiles = 4 * len(blocks)
    return pl.pallas_call(
        functools.partial(wave_kernel, blocks, first, last, len(arrays)),
        out_shape=out_shape,
        in_specs=[vmem] * len(operands),
        out_specs=[vmem] * len(out_shape),
        scratch_shapes=[
            pltpu.VMEM((2, ROWS, width), F32),
            pltpu.VMEM((width, 2 * DH), BF16),
        ],
        compiler_params=pltpu.CompilerParams(vmem_limit_bytes=32 << 20),
        cost_estimate=SMALL,
        name="wave",
    )(*operands)


def tie(x, *before):
    return lax.optimization_barrier((x,) + before)[0]


def kv_of(message):
    return message[ROWS:]


def tie(x, *before):
    return lax.optimization_barrier((x,) + before)[0]


def block(array, first_row, lower, far, j, other):
    return (array, first_row, first_row + ROWS, lower, far, j, other)


def group(array, spots, lower, other, skip=0):
    return [
        block(array, skip + 2 * ROWS * n, lower, far, j, other) for n, (far, j) in enumerate(spots)
    ]


def split(x):
    top = x.astype(BF16)
    return top, (x - top.astype(F32)).astype(BF16)


def transform():
    k = np.arange(SPAN // 2)[:, None] + 0.5
    t = np.arange(SPAN)[None, :]
    angle = 2 * np.pi * k * t / SPAN
    forward = np.concatenate([np.cos(angle), np.sin(angle)], axis=0)
    inverse = forward[:, TAPS:].T * (2.0 / SPAN)

    def halves(a):
        top = a.astype(ml_dtypes.bfloat16)
        return [top, (a - top.astype(np.float64)).astype(ml_dtypes.bfloat16)]

    return np.concatenate(
        [np.concatenate(halves(forward), axis=1), np.concatenate(halves(inverse), axis=1)], axis=0
    )


def filter_kernel(
    matrix_ref, key_ref, value_ref, gate_ref, res_ref, taps_ref, halo_ref,
    out_ref, squares_ref,
):
    def dot(a, b):
        return jnp.dot(a, b, preferred_element_type=F32)

    def dot_t(a, b):
        return lax.dot_general(a, b, (((1,), (1,)), ((), ())), preferred_element_type=F32)

    half = SPAN // 2
    fh, fl = matrix_ref[:SPAN, :SPAN], matrix_ref[:SPAN, SPAN:]
    gh, gl = matrix_ref[SPAN:, :SPAN], matrix_ref[SPAN:, SPAN:]
    gated = (key_ref[...].astype(F32) * value_ref[...].astype(F32)).astype(BF16)
    width = gated.shape[1]
    x = jnp.concatenate(
        [jnp.concatenate([halo_ref[...], gated[:TAPS]], axis=0), gated], axis=1
    )
    spectrum = dot(fh, x) + dot(fl, x)
    taps = taps_ref[...]
    weight = dot_t(fh[:, :TAPS], taps) + dot_t(fl[:, :TAPS], taps)
    xc, xs = spectrum[:half], spectrum[half:]
    wc, ws = [jnp.concatenate([w, w], axis=1) for w in (weight[:half], weight[half:])]
    both = jnp.concatenate([xc * wc - xs * ws, xc * ws + xs * wc], axis=0)
    top, low = split(both)
    filtered = dot(gh, top) + dot(gh, low) + dot(gl, top)
    filtered = jnp.concatenate([filtered[:, :width], filtered[:, width:]], axis=0)
    out = (res_ref[...].astype(F32) + gate_ref[...].astype(F32) * filtered).astype(BF16)
    out_ref[...] = out
    wide = out.astype(F32)
    s_top, s_low = split(wide * wide)
    ones = jnp.ones((8, out.shape[1]), BF16)

    @pl.when(pl.program_id(0) == 0)
    def _():
        squares_ref[...] = jnp.zeros_like(squares_ref)

    squares_ref[...] += dot_t(ones, s_top) + dot_t(ones, s_low)


def filter_block(gate, key, value, filters, residual, halo):
    channels = gate.shape[1]
    tile = 256
    rows = pl.BlockSpec((ROWS, tile), lambda i: (0, i))
    whole = lambda a: pl.BlockSpec(a.shape, lambda i: (0, 0))
    matrix = jnp.asarray(transform())
    return pl.pallas_call(
        filter_kernel,
        grid=(channels // tile,),
        out_shape=[
            jax.ShapeDtypeStruct((ROWS, channels), BF16),
            jax.ShapeDtypeStruct((8, ROWS), F32),
        ],
        in_specs=[whole(matrix)]
        + [rows] * 4
        + [
            pl.BlockSpec((tile, TAPS), lambda i: (i, 0)),
            pl.BlockSpec((TAPS, tile), lambda i: (0, i)),
        ],
        out_specs=[rows, pl.BlockSpec((8, ROWS), lambda i: (0, 0))],
        compiler_params=pltpu.CompilerParams(vmem_limit_bytes=32 << 20),
        cost_estimate=SMALL,
        name="filter",
    )(matrix, key, value, gate, residual, filters, halo)


def swap_sum(x, bit):
    return x + lax.ppermute(x, "tensor", [(i, i ^ bit) for i in range(8)])


def local(
    gate_proj,
    key_proj,
    value_proj,
    filters,
    residual_in,
    norm_gain,
    queries,
    attn_keys,
    attn_values,
):
    edge, *messages, kv0 = pack(queries, attn_keys, attn_values, key_proj, value_proj)
    one = send(messages[1], NEAR[1])
    two = send(messages[2], NEAR[2])
    far0 = send(kv0, SIBLING)
    low0 = send(kv0, DOWN)
    halo = send(edge, NEXT)

    three = send(tie(messages[3], one), NEAR[3])
    kv12 = tie(jnp.concatenate([kv_of(one), kv_of(two)]), far0, low0)
    far12 = send(kv12, SIBLING)
    mid = jnp.concatenate([kv12, far0])
    low12 = send(mid, DOWN)
    core1 = send(jnp.concatenate([kv0, mid]), CORE)

    gate_proj, key_proj, value_proj, filters, residual_in, _ = lax.optimization_barrier(
        (gate_proj, key_proj, value_proj, filters, residual_in, messages[0])
    )
    residual_out, squares = filter_block(
        gate_proj, key_proj, value_proj, filters, residual_in, tie(halo, kv12)
    )
    total = swap_sum(squares[0], 1)

    kv3 = tie(kv_of(three), squares)
    far3 = send(kv3, SIBLING)
    late = jnp.concatenate([kv3, far12])
    low3 = send(late, DOWN)
    core2 = send(late, CORE)
    got = [messages[0], one, two, three]
    first = [(False, 0), (False, 1), (False, 2), (True, 0)]
    second = [(False, 3), (True, 1), (True, 2)]
    third = [(True, 3)]
    state = wave(
        got,
        [got[0], got[1], got[2], far0, core1],
        [block(n, ROWS, False, False, n, False) for n in range(3)]
        + group(3, [(True, 0)], False, False)
        + group(4, first, False, True),
        None,
    )
    far3 = tie(far3, state[1])
    low4 = send(far3, DOWN)
    core3 = send(jnp.concatenate([far3, low0, low12]), CORE)
    total = swap_sum(total, 2)
    state = wave(
        got,
        [got[3], far12, tie(core2, total)],
        [block(0, ROWS, False, False, 3, False)]
        + group(1, second[1:], False, False)
        + group(2, second, False, True),
        state,
    )
    low3 = tie(low3, state[1])
    core4 = send(jnp.concatenate([low3, low4]), CORE)
    total = swap_sum(total, 4)
    state = wave(
        got,
        [far3, tie(core3, total), low0, low12],
        group(0, third, False, False)
        + group(1, third, False, True)
        + group(1, first, True, True, 2 * ROWS)
        + group(2, first[:1], True, False)
        + group(3, first[1:], True, False),
        state,
    )
    pieces = wave(
        got,
        [low3, low4, core4],
        group(0, second, True, False)
        + group(1, third, True, False)
        + group(2, second + third, True, True),
        state,
        last=True,
    )
    returning = [back(pieces[j], NEAR[j]) for j in (3, 2, 1)]
    returned = [pieces[0]] + returning[::-1]
    heads_out = unpack(returned)

    mean_square = total[:, None] / D
    normed = (
        residual_out.astype(F32) * lax.rsqrt(mean_square + 1e-06) * norm_gain[None, :]
    ).astype(BF16)
    return (residual_out, normed, heads_out)


def solution(mesh):
    split_both = P("context", "tensor")
    return jax.shard_map(
        local,
        mesh=mesh,
        in_specs=(
            split_both,
            split_both,
            split_both,
            P("tensor", None),
            split_both,
            P("tensor"),
            split_both,
            split_both,
            split_both,
        ),
        out_specs=(split_both, split_both, split_both),
        check_vma=False,
    )
```

time: 101 us -> 80.8 us (0.80)
  Pallas kernels: 32.6 us -> 20.3 us
  starting transfers between devices: 37.5 us -> 32.4 us
  local copies, waits for them, and re-layouts: 2.95 us -> 0.13 us
    pallas_call x4, Pallas kernels: 25 us -> 11.7 us  [wave(): pl.pallas_call(functools.partial(wave_kernel, blocks, first, last, len(ar...]
    ppermute x15, starting transfers between devices: 23.2 us -> 20.1 us  [send(): return lax.ppermute(x, 'context', where)]
    unnamed x28 -> x21, local copies, waits for them, and re-layouts: 2.91 us -> 0.06 us
    ppermute x15, waiting for transfers between devices: 15.6 us -> 12.9 us  [send(): return lax.ppermute(x, 'context', where)]
    ppermute x3, waiting for transfers between devices: 3.95 us -> 6.56 us  [back(): return lax.ppermute(x, 'context', [(b, a) for a, b in where])]
    pallas_call x1, Pallas kernels: 0.14 us -> 2.71 us  [pack(): pl.pallas_call(pack_kernel, out_shape=[jax.ShapeDtypeStruct((TAPS, channe...]
    ppermute x3, starting transfers between devices: 8.45 us -> 6.39 us  [back(): return lax.ppermute(x, 'context', [(b, a) for a, b in where])]
    pallas_call x1, Pallas kernels: 6.64 us -> 5.06 us  [filter_block(): pl.pallas_call(filter_kernel, grid=(channels // tile,), out_shape=[jax.Sh...]
  transfers between devices with their start and end apart: 21 -> 21, of which waited for: 8 -> 9; matrix products, arithmetic and copies ran while one was open for 1% -> 2% of each run, Pallas kernels for 26% -> 17%
where the time goes in v2:
time: 80.8 us; the launch traced here: 80.6 us
  starting transfers between devices  32.4 us (40%)
  waiting for transfers between devices  25.6 us (32%)
  Pallas kernels  20.3 us (25%)
  other arithmetic  1.16 us (1%)
  between operations  1.02 us (1%)
    ppermute x15, starting transfers between devices, send(): return lax.ppermute(x, 'context', where)  20.1 us
    ppermute x15, waiting for transfers between devices, send(): return lax.ppermute(x, 'context', where)  12.9 us
    pallas_call x4, Pallas kernels, wave(): pl.pallas_call(functools.partial(wave_kernel, blocks, first, last, len(ar...  11.7 us
    ppermute x3, waiting for transfers between devices, back(): return lax.ppermute(x, 'context', [(b, a) for a, b in where])  6.56 us
    ppermute x3, starting transfers between devices, back(): return lax.ppermute(x, 'context', [(b, a) for a, b in where])  6.39 us
    ppermute x3, waiting for transfers between devices, swap_sum(): return x + lax.ppermute(x, 'tensor', [(i, i ^ bit) for i in range(8)])  6.13 us
    ppermute x3, starting transfers between devices, swap_sum(): return x + lax.ppermute(x, 'tensor', [(i, i ^ bit) for i in range(8)])  5.87 us
    pallas_call x1, Pallas kernels, filter_block(): pl.pallas_call(filter_kernel, grid=(channels // tile,), out_shape=[jax.Sh...  5.06 us
  transfers between devices with their start and end apart: 21, of which 9 were waited for; matrix products, arithmetic and copies ran while one was open for 2% of the time, Pallas kernels for 17%

profile of v2, /device:TPU:16, one launch (start us, length us, event | category | flops | bytes accessed | tf_op | source)
XLA Modules:
  0.0 80.6 jit_solution(1536569573813656673)
XLA Ops:
  0.6 2.7 %pack.1 = (bf16[128,1024]{1,0:T(8,128)(2,1)}, bf16[768,128]{1,0:T(8,128)(2,1)}, bf16[768,128]{1,0:T(8,128)(2,1)}, bf16[768,128]{1,0:T(8,128)(2,1)}, bf16[768,128]{1,0:T(8,128)(2,1)}, /*index=5*/bf16[512,128]{1,0:T(8,128)(2,1)}) custom-call(bf16[256,512]{1,0:T(8,128)(2,1)} %q_ref.1, bf16[256,512]{1,0:T(8,128)(2,1)} %k_ref.1, bf16[256,512]{1,0:T(8,128)(2,1)} %v_ref.1, ...), custom_call_target="tpu_custom_call" | custom-call | tf_op jit(solution)/shard_map/pack/pallas_call | solution.py:105
  3.3 0.0 copy-start.8
  3.4 5.9 %collective-permute-start.1 = (bf16[768,128]{1,0:T(8,128)(2,1)}, bf16[768,128]{1,0:T(8,128)(2,1)S(1)}, u32[]{:S(2)}, u32[]{:S(2)}) collective-permute-start(bf16[768,128]{1,0:T(8,128)(2,1)} %get-tuple-element.41), channel_id=1, source_target_pairs={{0,112},{8,120},{16,32},{24,40},{32,16},{40,24},{48,64},{56,72},{6... | collective-permute-start | bytes 589832 | tf_op jit(solution)/shard_map/ppermute | solution.py:49
  9.3 0.0 collective-permute-start.2
  9.3 1.5 %collective-permute-start.3 = (bf16[512,128]{1,0:T(8,128)(2,1)}, bf16[512,128]{1,0:T(8,128)(2,1)S(1)}, u32[]{:S(2)}, u32[]{:S(2)}) collective-permute-start(bf16[512,128]{1,0:T(8,128)(2,1)} %get-tuple-element.43), channel_id=1, source_target_pairs={{0,16},{8,24},{16,0},{24,8},{32,48},{40,56},{48,32},{56,40},{64,80... | collective-permute-start | bytes 393224 | tf_op jit(solution)/shard_map/ppermute | solution.py:49
  10.9 1.3 %collective-permute-start.4 = (bf16[512,128]{1,0:T(8,128)(2,1)}, bf16[512,128]{1,0:T(8,128)(2,1)S(1)}, u32[]{:S(2)}, u32[]{:S(2)}) collective-permute-start(bf16[512,128]{1,0:T(8,128)(2,1)} %get-tuple-element.43), channel_id=1, source_target_pairs={{0,128},{8,136},{16,144},{24,152},{32,160},{40,168},{48,176},{56,1... | collective-permute-start | bytes 393224 | tf_op jit(solution)/shard_map/ppermute | solution.py:49
  12.1 1.9 %collective-permute-start = (bf16[128,1024]{1,0:T(8,128)(2,1)}, bf16[128,1024]{1,0:T(8,128)(2,1)S(1)}, u32[]{:S(2)}, u32[]{:S(2)}) collective-permute-start(bf16[128,1024]{1,0:T(8,128)(2,1)} %get-tuple-element.40), channel_id=1, source_target_pairs={{0,8},{8,16},{16,24},{24,32},{32,40},{40,48},{48,56},{56,64},{64,7... | collective-permute-start | bytes 786440 | tf_op jit(solution)/shard_map/ppermute | solution.py:49
  14.1 3.9 %collective-permute-done.1.refs_1_.refs_5_ = bf16[768,128]{1,0:T(8,128)(2,1)S(1)} collective-permute-done((bf16[768,128]{1,0:T(8,128)(2,1)}, bf16[768,128]{1,0:T(8,128)(2,1)S(1)}, u32[]{:S(2)}, u32[]{:S(2)}) %collective-permute-start.1) | collective-permute-done | bytes 196640 | tf_op jit(solution)/shard_map/ppermute | solution.py:49
  18.0 1.4 %collective-permute-done.2.refs_2_.refs_6_ = bf16[768,128]{1,0:T(8,128)(2,1)S(1)} collective-permute-done((bf16[768,128]{1,0:T(8,128)(2,1)}, bf16[768,128]{1,0:T(8,128)(2,1)S(1)}, u32[]{:S(2)}, u32[]{:S(2)}) %collective-permute-start.2) | collective-permute-done | bytes 196640 | tf_op jit(solution)/shard_map/ppermute | solution.py:49
  19.4 0.0 copy-start.4
  19.5 0.0 copy-start.1
  19.5 0.0 copy-start.2
  19.5 0.0 copy-start.3
  19.5 0.0 collective-permute-done.3.refs_7_
  19.5 0.0 collective-permute-done.4.refs_6_
  19.5 2.9 %collective-permute-start.8 = (bf16[768,128]{1,0:T(8,128)(2,1)}, bf16[768,128]{1,0:T(8,128)(2,1)S(1)}, u32[]{:S(2)}, u32[]{:S(2)}) collective-permute-start(bf16[768,128]{1,0:T(8,128)(2,1)} %get-tuple-element.49), channel_id=1, source_target_pairs={{0,80},{8,88},{16,64},{24,72},{32,112},{40,120},{48,96},{56,104},{... | collective-permute-start | bytes 589832 | tf_op jit(solution)/shard_map/ppermute | solution.py:49
  22.4 2.0 %collective-permute-start.9 = (bf16[1024,128]{1,0:T(8,128)(2,1)S(1)}, bf16[1024,128]{1,0:T(8,128)(2,1)S(1)}, u32[]{:S(2)}, u32[]{:S(2)}) collective-permute-start(bf16[1024,128]{1,0:T(8,128)(2,1)S(1)} %pad_maximum_fusion.4), channel_id=1, source_target_pairs={{0,16},{8,24},{16,0},{24,8},{32,48},{40,56},{48,32},{56,40},{64,80... | collective-permute-start | bytes 786440 | tf_op jit(solution)/shard_map/ppermute | solution.py:49
  24.5 0.0 copy-done.8
  24.5 0.1 collective-permute-start.12
  24.6 1.3 %collective-permute-start.16 = (bf16[1536,128]{1,0:T(8,128)(2,1)S(1)}, bf16[1536,128]{1,0:T(8,128)(2,1)S(1)}, u32[]{:S(2)}, u32[]{:S(2)}) collective-permute-start(bf16[1536,128]{1,0:T(8,128)(2,1)S(1)} %pad_maximum_fusion.3), channel_id=1, source_target_pairs={{0,128},{8,136},{16,144},{24,152},{32,160},{40,168},{48,176},{56,1... | collective-permute-start | bytes 1179656 | tf_op jit(solution)/shard_map/ppermute | solution.py:49
  25.9 0.0 collective-permute-done.halo_ref
  25.9 0.0 copy-done.6
  26.0 0.0 copy-done.5
  26.0 0.0 copy-done.4
  26.0 0.0 copy-done.1
  26.0 0.0 copy-done.2
  26.0 5.1 %filter.1 = (bf16[256,1024]{1,0:T(8,128)(2,1)}, f32[8,256]{1,0:T(8,128)S(1)}) custom-call(bf16[384,512]{1,0:T(8,128)(2,1)S(1)} %copy-done.5, bf16[256,1024]{1,0:T(8,128)(2,1)S(1)} %copy-done.1, bf16[256,1024]{1,0:T(8,128)(2,1)S(1)} %copy-done.2, bf16[256,1024]{1,0:T(8,128)(2,1)S(1)} %copy-done.3, bf16[256,1024]{1,0:T(8,128)(2,1)S(1)} %copy-done.4, ...), custom_call_target="tpu_custom_call" | custom-call | flops 1024 | bytes 1024 | tf_op jit(solution)/shard_map/filter/pallas_call | solution.py:350
  31.1 1.5 %collective-permute-start.5 = (f32[256]{0:T(256)S(1)}, f32[256]{0:T(256)S(1)}, u32[]{:S(2)}, u32[]{:S(2)}) collective-permute-start(f32[256]{0:T(256)S(1)} %bitcast.1), channel_id=1, source_target_pairs={{0,1},{1,0},{2,3},{3,2},{4,5},{5,4},{6,7},{7,6},{8,9},{9,8},{10,11... | collective-permute-start | bytes 3080 | tf_op jit(solution)/shard_map/ppermute | solution.py:371
  32.6 2.1 %collective-permute-done.5 = f32[256]{0:T(256)S(1)} collective-permute-done((f32[256]{0:T(256)S(1)}, f32[256]{0:T(256)S(1)}, u32[]{:S(2)}, u32[]{:S(2)}) %collective-permute-start.5) | collective-permute-done | bytes 1056 | tf_op jit(solution)/shard_map/ppermute | solution.py:371
  34.6 3.0 %collective-permute-start.6 = (f32[256]{0:T(256)S(1)}, f32[256]{0:T(256)S(1)}, u32[]{:S(2)}, u32[]{:S(2)}) collective-permute-start(f32[256]{0:T(256)S(1)} %add.16), channel_id=1, source_target_pairs={{0,2},{1,3},{2,0},{3,1},{4,6},{5,7},{6,4},{7,5},{8,10},{9,11},{10,... | collective-permute-start | bytes 3080 | tf_op jit(solution)/shard_map/ppermute | solution.py:371
  37.7 0.0 collective-permute-done.8.refs_3_.refs_4_
  37.7 0.1 collective-permute-start.13
  37.8 0.0 collective-permute-done.9.refs_5_
  37.9 0.1 collective-permute-start.11
  38.0 1.8 %collective-permute-done.6 = f32[256]{0:T(256)S(1)} collective-permute-done((f32[256]{0:T(256)S(1)}, f32[256]{0:T(256)S(1)}, u32[]{:S(2)}, u32[]{:S(2)}) %collective-permute-start.6) | collective-permute-done | bytes 1056 | tf_op jit(solution)/shard_map/ppermute | solution.py:371
  39.7 1.3 %collective-permute-start.10 = (bf16[1536,128]{1,0:T(8,128)(2,1)S(1)}, bf16[1536,128]{1,0:T(8,128)(2,1)S(1)}, u32[]{:S(2)}, u32[]{:S(2)}) collective-permute-start(bf16[1536,128]{1,0:T(8,128)(2,1)S(1)} %constant_dynamic-update-slice_fusion), channel_id=1, source_target_pairs={{0,128},{8,136},{16,144},{24,152},{32,160},{40,168},{48,176},{56,1... | collective-permute-start | bytes 1179656 | tf_op jit(solution)/shard_map/ppermute | solution.py:49
  41.0 0.0 collective-permute-done.12.refs_8_
  41.0 3.2 %wave.4 = (f32[1024,256]{1,0:T(8,128)S(1)}, f32[1024,128]{1,0:T(8,128)S(1)}) custom-call(bf16[768,128]{1,0:T(8,128)(2,1)S(1)} %copy-done, bf16[768,128]{1,0:T(8,128)(2,1)S(1)} %collective-permute-done.1.refs_1_.refs_5_, bf16[768,128]{1,0:T(8,128)(2,1)S(1)} %collective-permute-done.2.refs_2_.refs_6_, ...), custom_call_target="tpu_custom_call" | custom-call | flops 1024 | bytes 1024 | tf_op jit(solution)/shard_map/wave/pallas_call | solution.py:246
  44.2 0.0 collective-permute-done.13.refs_4_
  44.2 1.3 %collective-permute-start.14 = (bf16[512,128]{1,0:T(8,128)(2,1)S(1)}, bf16[512,128]{1,0:T(8,128)(2,1)S(1)}, u32[]{:S(2)}, u32[]{:S(2)}) collective-permute-start(bf16[512,128]{1,0:T(8,128)(2,1)S(1)} %collective-permute-done.13.refs_4_), channel_id=1, source_target_pairs={{0,128},{8,136},{16,144},{24,152},{32,160},{40,168},{48,176},{56,1... | collective-permute-start | bytes 393224 | tf_op jit(solution)/shard_map/ppermute | solution.py:49
  45.5 0.0 collective-permute-done.16.refs_7_
  45.6 0.3 collective-permute-start.17
  45.9 0.0 collective-permute-done.11.refs_6_
  45.9 2.5 %wave.5 = (f32[1024,256]{1,0:T(8,128)S(1)}, f32[1024,128]{1,0:T(8,128)S(1)}) custom-call(bf16[768,128]{1,0:T(8,128)(2,1)S(1)} %copy-done, bf16[768,128]{1,0:T(8,128)(2,1)S(1)} %collective-permute-done.1.refs_1_.refs_5_, bf16[768,128]{1,0:T(8,128)(2,1)S(1)} %collective-permute-done.2.refs_2_.refs_6_, ...), custom_call_target="tpu_custom_call" | custom-call | flops 1024 | bytes 1024 | tf_op jit(solution)/shard_map/wave/pallas_call | solution.py:246
  48.4 6.2 %collective-permute-done.10.refs_4_ = bf16[1536,128]{1,0:T(8,128)(2,1)S(1)} collective-permute-done((bf16[1536,128]{1,0:T(8,128)(2,1)S(1)}, bf16[1536,128]{1,0:T(8,128)(2,1)S(1)}, u32[]{:S(2)}, u32[]{:S(2)}) %collective-permute-start.10) | collective-permute-done | bytes 393248 | tf_op jit(solution)/shard_map/ppermute | solution.py:49
  54.6 1.4 %collective-permute-done.14.refs_5_ = bf16[512,128]{1,0:T(8,128)(2,1)S(1)} collective-permute-done((bf16[512,128]{1,0:T(8,128)(2,1)S(1)}, bf16[512,128]{1,0:T(8,128)(2,1)S(1)}, u32[]{:S(2)}, u32[]{:S(2)}) %collective-permute-start.14) | collective-permute-done | bytes 131104 | tf_op jit(solution)/shard_map/ppermute | solution.py:49
  56.0 0.1 collective-permute-start.15
  56.1 1.4 %collective-permute-start.7 = (f32[256]{0:T(256)S(1)}, f32[256]{0:T(256)S(1)}, u32[]{:S(2)}, u32[]{:S(2)}) collective-permute-start(f32[256]{0:T(256)S(1)} %add.17), channel_id=1, source_target_pairs={{0,4},{1,5},{2,6},{3,7},{4,0},{5,1},{6,2},{7,3},{8,12},{9,13},{10,... | collective-permute-start | bytes 3080 | tf_op jit(solution)/shard_map/ppermute | solution.py:371
  57.5 2.3 %collective-permute-done.7 = f32[256]{0:T(256)S(1)} collective-permute-done((f32[256]{0:T(256)S(1)}, f32[256]{0:T(256)S(1)}, u32[]{:S(2)}, u32[]{:S(2)}) %collective-permute-start.7) | collective-permute-done | bytes 1056 | tf_op jit(solution)/shard_map/ppermute | solution.py:371
  59.8 0.0 collective-permute-done.17.refs_5_
  59.8 3.2 %wave.6 = (f32[1024,256]{1,0:T(8,128)S(1)}, f32[1024,128]{1,0:T(8,128)S(1)}) custom-call(bf16[768,128]{1,0:T(8,128)(2,1)S(1)} %copy-done, bf16[768,128]{1,0:T(8,128)(2,1)S(1)} %collective-permute-done.1.refs_1_.refs_5_, bf16[768,128]{1,0:T(8,128)(2,1)S(1)} %collective-permute-done.2.refs_2_.refs_6_, ...), custom_call_target="tpu_custom_call" | custom-call | flops 1024 | bytes 1024 | tf_op jit(solution)/shard_map/wave/pallas_call | solution.py:246
  63.0 0.0 collective-permute-done.15.refs_6_
  63.0 0.0 copy-start.7
  63.1 0.0 copy-start.9
  63.1 2.8 %wave.7 = (bf16[256,128]{1,0:T(8,128)(2,1)S(1)}, bf16[256,128]{1,0:T(8,128)(2,1)S(1)}, bf16[256,128]{1,0:T(8,128)(2,1)S(1)}, bf16[256,128]{1,0:T(8,128)(2,1)S(1)}) custom-call(bf16[768,128]{1,0:T(8,128)(2,1)S(1)} %copy-done, bf16[768,128]{1,0:T(8,128)(2,1)S(1)} %collective-permute-done.1.refs_1_.refs_5_, ...), custom_call_target="tpu_custom_call" | custom-call | flops 1024 | bytes 1024 | tf_op jit(solution)/shard_map/wave/pallas_call | solution.py:246
  65.9 1.8 %collective-permute-start.18 = (bf16[256,128]{1,0:T(8,128)(2,1)S(1)}, bf16[256,128]{1,0:T(8,128)(2,1)S(1)}, u32[]{:S(2)}, u32[]{:S(2)}) collective-permute-start(bf16[256,128]{1,0:T(8,128)(2,1)S(1)} %get-tuple-element.62), channel_id=1, source_target_pairs={{112,0},{120,8},{32,16},{40,24},{16,32},{24,40},{64,48},{72,56},{4... | collective-permute-start | bytes 196616 | tf_op jit(solution)/shard_map/ppermute | solution.py:53
  67.7 4.6 %collective-permute-start.19 = (bf16[256,128]{1,0:T(8,128)(2,1)S(1)}, bf16[256,128]{1,0:T(8,128)(2,1)S(1)}, u32[]{:S(2)}, u32[]{:S(2)}) collective-permute-start(bf16[256,128]{1,0:T(8,128)(2,1)S(1)} %get-tuple-element.63), channel_id=1, source_target_pairs={{32,0},{40,8},{112,16},{120,24},{64,32},{72,40},{16,48},{24,56},{9... | collective-permute-start | bytes 196616 | tf_op jit(solution)/shard_map/ppermute | solution.py:53
  72.3 0.0 collective-permute-start.20
  72.3 0.0 copy-done.9
  72.3 1.0 %multiply_convert_fusion = bf16[256,1024]{1,0:T(8,128)(2,1)} fusion(bf16[256,1024]{1,0:T(8,128)(2,1)S(1)} %copy-done.7, f32[1024]{0:T(1024)S(1)} %copy-done.9, f32[256]{0:T(256)S(1)} %add_rsqrt_fusion), kind=kLoop, calls=%fused_computation | loop fusion | flops 1048576 | bytes 1053696 | tf_op jit(solution)/shard_map/convert_element_type | solution.py:465
  73.3 0.0 collective-permute-done.18.o1
  73.3 1.0 %collective-permute-done.19.o2 = bf16[256,128]{1,0:T(8,128)(2,1)S(1)} collective-permute-done((bf16[256,128]{1,0:T(8,128)(2,1)S(1)}, bf16[256,128]{1,0:T(8,128)(2,1)S(1)}, u32[]{:S(2)}, u32[]{:S(2)}) %collective-permute-start.19) | collective-permute-done | bytes 65568 | tf_op jit(solution)/shard_map/ppermute | solution.py:53
  74.2 5.6 %collective-permute-done.20.o3 = bf16[256,128]{1,0:T(8,128)(2,1)S(1)} collective-permute-done((bf16[256,128]{1,0:T(8,128)(2,1)S(1)}, bf16[256,128]{1,0:T(8,128)(2,1)S(1)}, u32[]{:S(2)}, u32[]{:S(2)}) %collective-permute-start.20) | collective-permute-done | bytes 65568 | tf_op jit(solution)/shard_map/ppermute | solution.py:53
  79.8 0.8 unpack.1
  (20 shorter events, 0.3 us)
Async XLA Ops:
  3.3 21.1 %copy-start.8 = (bf16[512,128]{1,0:T(8,128)(2,1)S(1)}, bf16[512,128]{1,0:T(8,128)(2,1)}, u32[]{:S(2)}) copy-start(bf16[512,128]{1,0:T(8,128)(2,1)} %get-tuple-element.43) | copy-start | bytes 393220
  3.4 14.6 %collective-permute-start.1 = (bf16[768,128]{1,0:T(8,128)(2,1)}, bf16[768,128]{1,0:T(8,128)(2,1)S(1)}, u32[]{:S(2)}, u32[]{:S(2)}) collective-permute-start(bf16[768,128]{1,0:T(8,128)(2,1)} %get-tuple-element.41), channel_id=1, source_target_pairs={{0,112},{8,120},{16,32},{24,40},{32,16},{40,24},{48,64},{56,72},{6... | collective-permute-start | bytes 589832 | tf_op jit(solution)/shard_map/ppermute | solution.py:49
  9.3 10.1 %collective-permute-start.2 = (bf16[768,128]{1,0:T(8,128)(2,1)}, bf16[768,128]{1,0:T(8,128)(2,1)S(1)}, u32[]{:S(2)}, u32[]{:S(2)}) collective-permute-start(bf16[768,128]{1,0:T(8,128)(2,1)} %get-tuple-element.42), channel_id=1, source_target_pairs={{0,32},{8,40},{16,112},{24,120},{32,64},{40,72},{48,16},{56,24},{6... | collective-permute-start | bytes 589832 | tf_op jit(solution)/shard_map/ppermute | solution.py:49
  9.3 10.2 %collective-permute-start.3 = (bf16[512,128]{1,0:T(8,128)(2,1)}, bf16[512,128]{1,0:T(8,128)(2,1)S(1)}, u32[]{:S(2)}, u32[]{:S(2)}) collective-permute-start(bf16[512,128]{1,0:T(8,128)(2,1)} %get-tuple-element.43), channel_id=1, source_target_pairs={{0,16},{8,24},{16,0},{24,8},{32,48},{40,56},{48,32},{56,40},{64,80... | collective-permute-start | bytes 393224 | tf_op jit(solution)/shard_map/ppermute | solution.py:49
  10.9 8.7 %collective-permute-start.4 = (bf16[512,128]{1,0:T(8,128)(2,1)}, bf16[512,128]{1,0:T(8,128)(2,1)S(1)}, u32[]{:S(2)}, u32[]{:S(2)}) collective-permute-start(bf16[512,128]{1,0:T(8,128)(2,1)} %get-tuple-element.43), channel_id=1, source_target_pairs={{0,128},{8,136},{16,144},{24,152},{32,160},{40,168},{48,176},{56,1... | collective-permute-start | bytes 393224 | tf_op jit(solution)/shard_map/ppermute | solution.py:49
  12.1 13.8 %collective-permute-start = (bf16[128,1024]{1,0:T(8,128)(2,1)}, bf16[128,1024]{1,0:T(8,128)(2,1)S(1)}, u32[]{:S(2)}, u32[]{:S(2)}) collective-permute-start(bf16[128,1024]{1,0:T(8,128)(2,1)} %get-tuple-element.40), channel_id=1, source_target_pairs={{0,8},{8,16},{16,24},{24,32},{32,40},{40,48},{48,56},{56,64},{64,7... | collective-permute-start | bytes 786440 | tf_op jit(solution)/shard_map/ppermute | solution.py:49
  18.0 8.0 %copy-start.6 = (bf16[1024,128]{1,0:T(8,128)(2,1)S(1)}, bf16[1024,128]{1,0:T(8,128)(2,1)}, u32[]{:S(2)}) copy-start(bf16[1024,128]{1,0:T(8,128)(2,1)} %taps_ref) | copy-start | bytes 786436
  19.4 6.5 %copy-start.5 = (bf16[384,512]{1,0:T(8,128)(2,1)S(1)}, bf16[384,512]{1,0:T(8,128)(2,1)}, u32[]{:S(2)}) copy-start(bf16[384,512]{1,0:T(8,128)(2,1)} %constant.7.clone.matrix_ref) | copy-start | bytes 1179652
  19.4 6.5 %copy-start.4 = (bf16[256,1024]{1,0:T(8,128)(2,1)S(1)}, bf16[256,1024]{1,0:T(8,128)(2,1)}, u32[]{:S(2)}) copy-start(bf16[256,1024]{1,0:T(8,128)(2,1)} %res_ref) | copy-start | bytes 1572868
  19.5 6.5 %copy-start.1 = (bf16[256,1024]{1,0:T(8,128)(2,1)S(1)}, bf16[256,1024]{1,0:T(8,128)(2,1)}, u32[]{:S(2)}) copy-start(bf16[256,1024]{1,0:T(8,128)(2,1)} %key_ref.2) | copy-start | bytes 1572868
  19.5 6.5 %copy-start.2 = (bf16[256,1024]{1,0:T(8,128)(2,1)S(1)}, bf16[256,1024]{1,0:T(8,128)(2,1)}, u32[]{:S(2)}) copy-start(bf16[256,1024]{1,0:T(8,128)(2,1)} %value_ref.2) | copy-start | bytes 1572868
  19.5 6.5 %copy-start.3 = (bf16[256,1024]{1,0:T(8,128)(2,1)S(1)}, bf16[256,1024]{1,0:T(8,128)(2,1)}, u32[]{:S(2)}) copy-start(bf16[256,1024]{1,0:T(8,128)(2,1)} %gate_ref) | copy-start | bytes 1572868
  19.5 18.1 %collective-permute-start.8 = (bf16[768,128]{1,0:T(8,128)(2,1)}, bf16[768,128]{1,0:T(8,128)(2,1)S(1)}, u32[]{:S(2)}, u32[]{:S(2)}) collective-permute-start(bf16[768,128]{1,0:T(8,128)(2,1)} %get-tuple-element.49), channel_id=1, source_target_pairs={{0,80},{8,88},{16,64},{24,72},{32,112},{40,120},{48,96},{56,104},{... | collective-permute-start | bytes 589832 | tf_op jit(solution)/shard_map/ppermute | solution.py:49
  22.4 15.4 %collective-permute-start.9 = (bf16[1024,128]{1,0:T(8,128)(2,1)S(1)}, bf16[1024,128]{1,0:T(8,128)(2,1)S(1)}, u32[]{:S(2)}, u32[]{:S(2)}) collective-permute-start(bf16[1024,128]{1,0:T(8,128)(2,1)S(1)} %pad_maximum_fusion.4), channel_id=1, source_target_pairs={{0,16},{8,24},{16,0},{24,8},{32,48},{40,56},{48,32},{56,40},{64,80... | collective-permute-start | bytes 786440 | tf_op jit(solution)/shard_map/ppermute | solution.py:49
  24.5 16.5 %collective-permute-start.12 = (bf16[2048,128]{1,0:T(8,128)(2,1)S(1)}, bf16[2048,128]{1,0:T(8,128)(2,1)S(1)}, u32[]{:S(2)}, u32[]{:S(2)}) collective-permute-start(bf16[2048,128]{1,0:T(8,128)(2,1)S(1)} %pad_maximum_fusion.1), channel_id=1, source_target_pairs={{0,8},{8,0},{16,24},{24,16},{32,40},{40,32},{48,56},{56,48},{64,72... | collective-permute-start | bytes 1572872 | tf_op jit(solution)/shard_map/ppermute | solution.py:49
  24.6 20.9 %collective-permute-start.16 = (bf16[1536,128]{1,0:T(8,128)(2,1)S(1)}, bf16[1536,128]{1,0:T(8,128)(2,1)S(1)}, u32[]{:S(2)}, u32[]{:S(2)}) collective-permute-start(bf16[1536,128]{1,0:T(8,128)(2,1)S(1)} %pad_maximum_fusion.3), channel_id=1, source_target_pairs={{0,128},{8,136},{16,144},{24,152},{32,160},{40,168},{48,176},{56,1... | collective-permute-start | bytes 1179656 | tf_op jit(solution)/shard_map/ppermute | solution.py:49
  31.1 10.0 %copy-start = (bf16[768,128]{1,0:T(8,128)(2,1)S(1)}, bf16[768,128]{1,0:T(8,128)(2,1)}, u32[]{:S(2)}) copy-start(bf16[768,128]{1,0:T(8,128)(2,1)} %get-tuple-element.34.refs_0_.refs_4_) | copy-start | bytes 589828
  31.1 3.6 %collective-permute-start.5 = (f32[256]{0:T(256)S(1)}, f32[256]{0:T(256)S(1)}, u32[]{:S(2)}, u32[]{:S(2)}) collective-permute-start(f32[256]{0:T(256)S(1)} %bitcast.1), channel_id=1, source_target_pairs={{0,1},{1,0},{2,3},{3,2},{4,5},{5,4},{6,7},{7,6},{8,9},{9,8},{10,11... | collective-permute-start | bytes 3080 | tf_op jit(solution)/shard_map/ppermute | solution.py:371
  34.6 5.1 %collective-permute-start.6 = (f32[256]{0:T(256)S(1)}, f32[256]{0:T(256)S(1)}, u32[]{:S(2)}, u32[]{:S(2)}) collective-permute-start(f32[256]{0:T(256)S(1)} %add.16), channel_id=1, source_target_pairs={{0,2},{1,3},{2,0},{3,1},{4,6},{5,7},{6,4},{7,5},{8,10},{9,11},{10,... | collective-permute-start | bytes 3080 | tf_op jit(solution)/shard_map/ppermute | solution.py:371
  37.7 6.6 %collective-permute-start.13 = (bf16[512,128]{1,0:T(8,128)(2,1)S(1)}, bf16[512,128]{1,0:T(8,128)(2,1)S(1)}, u32[]{:S(2)}, u32[]{:S(2)}) collective-permute-start(bf16[512,128]{1,0:T(8,128)(2,1)S(1)} %slice.18), channel_id=1, source_target_pairs={{0,16},{8,24},{16,0},{24,8},{32,48},{40,56},{48,32},{56,40},{64,80... | collective-permute-start | bytes 393224 | tf_op jit(solution)/shard_map/ppermute | solution.py:49
  37.9 8.0 %collective-permute-start.11 = (bf16[1536,128]{1,0:T(8,128)(2,1)S(1)}, bf16[1536,128]{1,0:T(8,128)(2,1)S(1)}, u32[]{:S(2)}, u32[]{:S(2)}) collective-permute-start(bf16[1536,128]{1,0:T(8,128)(2,1)S(1)} %constant_dynamic-update-slice_fusion), channel_id=1, source_target_pairs={{0,8},{8,0},{16,24},{24,16},{32,40},{40,32},{48,56},{56,48},{64,72... | collective-permute-start | bytes 1179656 | tf_op jit(solution)/shard_map/ppermute | solution.py:49
  39.7 14.8 %collective-permute-start.10 = (bf16[1536,128]{1,0:T(8,128)(2,1)S(1)}, bf16[1536,128]{1,0:T(8,128)(2,1)S(1)}, u32[]{:S(2)}, u32[]{:S(2)}) collective-permute-start(bf16[1536,128]{1,0:T(8,128)(2,1)S(1)} %constant_dynamic-update-slice_fusion), channel_id=1, source_target_pairs={{0,128},{8,136},{16,144},{24,152},{32,160},{40,168},{48,176},{56,1... | collective-permute-start | bytes 1179656 | tf_op jit(solution)/shard_map/ppermute | solution.py:49
  44.2 11.7 %collective-permute-start.14 = (bf16[512,128]{1,0:T(8,128)(2,1)S(1)}, bf16[512,128]{1,0:T(8,128)(2,1)S(1)}, u32[]{:S(2)}, u32[]{:S(2)}) collective-permute-start(bf16[512,128]{1,0:T(8,128)(2,1)S(1)} %collective-permute-done.13.refs_4_), channel_id=1, source_target_pairs={{0,128},{8,136},{16,144},{24,152},{32,160},{40,168},{48,176},{56,1... | collective-permute-start | bytes 393224 | tf_op jit(solution)/shard_map/ppermute | solution.py:49
  45.6 14.2 %collective-permute-start.17 = (bf16[2560,128]{1,0:T(8,128)(2,1)S(1)}, bf16[2560,128]{1,0:T(8,128)(2,1)S(1)}, u32[]{:S(2)}, u32[]{:S(2)}) collective-permute-start(bf16[2560,128]{1,0:T(8,128)(2,1)S(1)} %pad_maximum_fusion), channel_id=1, source_target_pairs={{0,8},{8,0},{16,24},{24,16},{32,40},{40,32},{48,56},{56,48},{64,72... | collective-permute-start | bytes 1966088 | tf_op jit(solution)/shard_map/ppermute | solution.py:49
  56.0 7.0 %collective-permute-start.15 = (bf16[2048,128]{1,0:T(8,128)(2,1)S(1)}, bf16[2048,128]{1,0:T(8,128)(2,1)S(1)}, u32[]{:S(2)}, u32[]{:S(2)}) collective-permute-start(bf16[2048,128]{1,0:T(8,128)(2,1)S(1)} %pad_maximum_fusion.2), channel_id=1, source_target_pairs={{0,8},{8,0},{16,24},{24,16},{32,40},{40,32},{48,56},{56,48},{64,72... | collective-permute-start | bytes 1572872 | tf_op jit(solution)/shard_map/ppermute | solution.py:49
  56.1 3.7 %collective-permute-start.7 = (f32[256]{0:T(256)S(1)}, f32[256]{0:T(256)S(1)}, u32[]{:S(2)}, u32[]{:S(2)}) collective-permute-start(f32[256]{0:T(256)S(1)} %add.17), channel_id=1, source_target_pairs={{0,4},{1,5},{2,6},{3,7},{4,0},{5,1},{6,2},{7,3},{8,12},{9,13},{10,... | collective-permute-start | bytes 3080 | tf_op jit(solution)/shard_map/ppermute | solution.py:371
  63.0 9.2 %copy-start.7 = (bf16[256,1024]{1,0:T(8,128)(2,1)S(1)}, bf16[256,1024]{1,0:T(8,128)(2,1)}, u32[]{:S(2)}) copy-start(bf16[256,1024]{1,0:T(8,128)(2,1)} %get-tuple-element.31) | copy-start | bytes 1572868
  63.1 9.2 %copy-start.9 = (f32[1024]{0:T(1024)S(1)}, f32[1024]{0:T(1024)}, u32[]{:S(2)}) copy-start(f32[1024]{0:T(1024)} %param.15) | copy-start | bytes 12292
  65.9 7.4 %collective-permute-start.18 = (bf16[256,128]{1,0:T(8,128)(2,1)S(1)}, bf16[256,128]{1,0:T(8,128)(2,1)S(1)}, u32[]{:S(2)}, u32[]{:S(2)}) collective-permute-start(bf16[256,128]{1,0:T(8,128)(2,1)S(1)} %get-tuple-element.62), channel_id=1, source_target_pairs={{112,0},{120,8},{32,16},{40,24},{16,32},{24,40},{64,48},{72,56},{4... | collective-permute-start | bytes 196616 | tf_op jit(solution)/shard_map/ppermute | solution.py:53
  67.7 6.5 %collective-permute-start.19 = (bf16[256,128]{1,0:T(8,128)(2,1)S(1)}, bf16[256,128]{1,0:T(8,128)(2,1)S(1)}, u32[]{:S(2)}, u32[]{:S(2)}) collective-permute-start(bf16[256,128]{1,0:T(8,128)(2,1)S(1)} %get-tuple-element.63), channel_id=1, source_target_pairs={{32,0},{40,8},{112,16},{120,24},{64,32},{72,40},{16,48},{24,56},{9... | collective-permute-start | bytes 196616 | tf_op jit(solution)/shard_map/ppermute | solution.py:53
  72.3 7.6 %collective-permute-start.20 = (bf16[256,128]{1,0:T(8,128)(2,1)S(1)}, bf16[256,128]{1,0:T(8,128)(2,1)S(1)}, u32[]{:S(2)}, u32[]{:S(2)}) collective-permute-start(bf16[256,128]{1,0:T(8,128)(2,1)S(1)} %get-tuple-element.64), channel_id=1, source_target_pairs={{80,0},{88,8},{64,16},{72,24},{112,32},{120,40},{96,48},{104,56},{... | collective-permute-start | bytes 196616 | tf_op jit(solution)/shard_map/ppermute | solution.py:53

commit v3 on v2

--- a/solution.py
+++ b/solution.py
@@ -302,8 +302,7 @@
 
 
 def filter_kernel(
-    matrix_ref, key_ref, value_ref, gate_ref, res_ref, taps_ref, halo_ref,
-    out_ref, squares_ref,
+    tile, matrix_ref, key_ref, value_ref, gate_ref, res_ref, taps_ref, halo_ref, out_ref, squares_ref
 ):
     def dot(a, b):
         return jnp.dot(a, b, preferred_element_type=F32)
@@ -314,61 +313,52 @@
     half = SPAN // 2
     fh, fl = matrix_ref[:SPAN, :SPAN], matrix_ref[:SPAN, SPAN:]
     gh, gl = matrix_ref[SPAN:, :SPAN], matrix_ref[SPAN:, SPAN:]
-    gated = (key_ref[...].astype(F32) * value_ref[...].astype(F32)).astype(BF16)
-    width = gated.shape[1]
-    x = jnp.concatenate(
-        [jnp.concatenate([halo_ref[...], gated[:TAPS]], axis=0), gated], axis=1
-    )
-    spectrum = dot(fh, x) + dot(fl, x)
-    taps = taps_ref[...]
-    weight = dot_t(fh[:, :TAPS], taps) + dot_t(fl[:, :TAPS], taps)
-    xc, xs = spectrum[:half], spectrum[half:]
-    wc, ws = [jnp.concatenate([w, w], axis=1) for w in (weight[:half], weight[half:])]
-    both = jnp.concatenate([xc * wc - xs * ws, xc * ws + xs * wc], axis=0)
-    top, low = split(both)
-    filtered = dot(gh, top) + dot(gh, low) + dot(gl, top)
-    filtered = jnp.concatenate([filtered[:, :width], filtered[:, width:]], axis=0)
-    out = (res_ref[...].astype(F32) + gate_ref[...].astype(F32) * filtered).astype(BF16)
-    out_ref[...] = out
-    wide = out.astype(F32)
-    s_top, s_low = split(wide * wide)
-    ones = jnp.ones((8, out.shape[1]), BF16)
-
-    @pl.when(pl.program_id(0) == 0)
-    def _():
-        squares_ref[...] = jnp.zeros_like(squares_ref)
-
-    squares_ref[...] += dot_t(ones, s_top) + dot_t(ones, s_low)
+    ones = jnp.ones((8, tile), BF16)
+    squares = jnp.zeros((8, ROWS), F32)
+    for first in range(0, key_ref.shape[1], tile):
+        columns = slice(first, first + tile)
+        gated = (key_ref[:, columns].astype(F32) * value_ref[:, columns].astype(F32)).astype(BF16)
+        x = jnp.concatenate(
+            [jnp.concatenate([halo_ref[:, columns], gated[:TAPS]], axis=0), gated], axis=1
+        )
+        spectrum = dot(fh, x) + dot(fl, x)
+        taps = taps_ref[columns, :]
+        weight = dot_t(fh[:, :TAPS], taps) + dot_t(fl[:, :TAPS], taps)
+        xc, xs = spectrum[:half], spectrum[half:]
+        wc, ws = [jnp.concatenate([w, w], axis=1) for w in (weight[:half], weight[half:])]
+        both = jnp.concatenate([xc * wc - xs * ws, xc * ws + xs * wc], axis=0)
+        top, low = split(both)
+        filtered = dot(gh, top) + dot(gh, low) + dot(gl, top)
+        filtered = jnp.concatenate([filtered[:, :tile], filtered[:, tile:]], axis=0)
+        out = (
+            res_ref[:, columns].astype(F32) + gate_ref[:, columns].astype(F32) * filtered
+        ).astype(BF16)
+        out_ref[:, columns] = out
+        wide = out.astype(F32)
+        s_top, s_low = split(wide * wide)
+        squares = squares + dot_t(ones, s_top) + dot_t(ones, s_low)
+    squares_ref[...] = squares
 
 
 def filter_block(gate, key, value, filters, residual, halo):
     channels = gate.shape[1]
-    tile = 256
-    rows = pl.BlockSpec((ROWS, tile), lambda i: (0, i))
-    whole = lambda a: pl.BlockSpec(a.shape, lambda i: (0, 0))
-    matrix = jnp.asarray(transform())
+    vmem = pl.BlockSpec(memory_space=pltpu.VMEM)
     return pl.pallas_call(
-        filter_kernel,
-        grid=(channels // tile,),
+        functools.partial(filter_kernel, 256),
         out_shape=[
             jax.ShapeDtypeStruct((ROWS, channels), BF16),
             jax.ShapeDtypeStruct((8, ROWS), F32),
         ],
-        in_specs=[whole(matrix)]
-        + [rows] * 4
-        + [
-            pl.BlockSpec((tile, TAPS), lambda i: (i, 0)),
-            pl.BlockSpec((TAPS, tile), lambda i: (0, i)),
-        ],
-        out_specs=[rows, pl.BlockSpec((8, ROWS), lambda i: (0, 0))],
+        in_specs=[vmem] * 7,
+        out_specs=[vmem] * 2,
         compiler_params=pltpu.CompilerParams(vmem_limit_bytes=32 << 20),
         cost_estimate=SMALL,
         name="filter",
-    )(matrix, key, value, gate, residual, filters, halo)
-
-
-def swap_sum(x, bit):
-    return x + lax.ppermute(x, "tensor", [(i, i ^ bit) for i in range(8)])
+    )(jnp.asarray(transform()), key, value, gate, residual, filters, halo)
+
+
+def swap_sum(x, bit, *before):
+    return lax.ppermute(x, "tensor", [(i, i ^ bit) for i in range(8)]) + tie(x, *before)
 
 
 def local(
@@ -402,10 +392,9 @@
     residual_out, squares = filter_block(
         gate_proj, key_proj, value_proj, filters, residual_in, tie(halo, kv12)
     )
-    total = swap_sum(squares[0], 1)
-
     kv3 = tie(kv_of(three), squares)
     far3 = send(kv3, SIBLING)
+    total = swap_sum(squares[0], 1, kv3)
     late = jnp.concatenate([kv3, far12])
     low3 = send(late, DOWN)
     core2 = send(late, CORE)
@@ -424,26 +413,24 @@
     far3 = tie(far3, state[1])
     low4 = send(far3, DOWN)
     core3 = send(jnp.concatenate([far3, low0, low12]), CORE)
-    total = swap_sum(total, 2)
+    total = swap_sum(total, 2, state[1])
     state = wave(
         got,
-        [got[3], far12, tie(core2, total)],
+        [got[3], far12, tie(core2, total), far3, low0, low12],
         [block(0, ROWS, False, False, 3, False)]
         + group(1, second[1:], False, False)
-        + group(2, second, False, True),
+        + group(2, second, False, True)
+        + group(3, third, False, False)
+        + group(4, first[:1], True, False)
+        + group(5, first[1:], True, False),
         state,
     )
     low3 = tie(low3, state[1])
     core4 = send(jnp.concatenate([low3, low4]), CORE)
-    total = swap_sum(total, 4)
     state = wave(
         got,
-        [far3, tie(core3, total), low0, low12],
-        group(0, third, False, False)
-        + group(1, third, False, True)
-        + group(1, first, True, True, 2 * ROWS)
-        + group(2, first[:1], True, False)
-        + group(3, first[1:], True, False),
+        [core3],
+        group(0, third, False, True) + group(0, first, True, True, 2 * ROWS),
         state,
     )
     pieces = wave(
@@ -455,6 +442,7 @@
         state,
         last=True,
     )
+    total = swap_sum(total, 4, pieces[0])
     returning = [back(pieces[j], NEAR[j]) for j in (3, 2, 1)]
     returned = [pieces[0]] + returning[::-1]
     heads_out = unpack(returned)

time: 80.8 us -> 71.8 us (0.89)
  waiting for transfers between devices: 25.6 us -> 16.7 us
  Pallas kernels: 20.3 us -> 19 us
    ppermute x3, waiting for transfers between devices: 6.13 us -> 0.01 us  [swap_sum(): lax.ppermute(x, 'tensor', [(i, i ^ bit) for i in range(8)])]
    ppermute x15, waiting for transfers between devices: 12.9 us -> 10.7 us  [send(): return lax.ppermute(x, 'context', where)]
    pallas_call x1, Pallas kernels: 5.06 us -> 3.91 us  [filter_block(): pl.pallas_call(functools.partial(filter_kernel, 256), out_shape=[jax.Shap...]
    ppermute x15, starting transfers between devices: 20.1 us -> 21 us  [send(): return lax.ppermute(x, 'context', where)]
  transfers between devices with their start and end apart: 21 -> 21, of which waited for: 9 -> 6; matrix products, arithmetic and copies ran while one was open for 2% -> 2% of each run, Pallas kernels for 17% -> 22%
where the time goes in v3:
time: 71.8 us; the launch traced here: 70.9 us
  starting transfers between devices  32.9 us (46%)
  Pallas kernels  19 us (26%)
  waiting for transfers between devices  16.7 us (23%)
  other arithmetic  1.16 us (2%)
  between operations  1.01 us (1%)
    ppermute x15, starting transfers between devices, send(): return lax.ppermute(x, 'context', where)  21 us
    pallas_call x4, Pallas kernels, wave(): pl.pallas_call(functools.partial(wave_kernel, blocks, first, last, len(ar...  11.6 us
    ppermute x15, waiting for transfers between devices, send(): return lax.ppermute(x, 'context', where)  10.7 us
    ppermute x3, starting transfers between devices, swap_sum(): lax.ppermute(x, 'tensor', [(i, i ^ bit) for i in range(8)])  6.15 us
    ppermute x3, waiting for transfers between devices, back(): return lax.ppermute(x, 'context', [(b, a) for a, b in where])  6.04 us
    ppermute x3, starting transfers between devices, back(): return lax.ppermute(x, 'context', [(b, a) for a, b in where])  5.69 us
    pallas_call x1, Pallas kernels, filter_block(): pl.pallas_call(functools.partial(filter_kernel, 256), out_shape=[jax.Shap...  3.91 us
    pallas_call x1, Pallas kernels, pack(): pl.pallas_call(pack_kernel, out_shape=[jax.ShapeDtypeStruct((TAPS, channe...  2.71 us
  transfers between devices with their start and end apart: 21, of which 6 were waited for; matrix products, arithmetic and copies ran while one was open for 2% of the time, Pallas kernels for 22%

profile of v3, /device:TPU:16, one launch (start us, length us, event | category | flops | bytes accessed | tf_op | source)
XLA Modules:
  0.0 70.9 jit_solution(11640941496645068967)
XLA Ops:
  0.6 2.7 %pack.1 = (bf16[128,1024]{1,0:T(8,128)(2,1)}, bf16[768,128]{1,0:T(8,128)(2,1)}, bf16[768,128]{1,0:T(8,128)(2,1)}, bf16[768,128]{1,0:T(8,128)(2,1)}, bf16[768,128]{1,0:T(8,128)(2,1)}, /*index=5*/bf16[512,128]{1,0:T(8,128)(2,1)}) custom-call(bf16[256,512]{1,0:T(8,128)(2,1)} %q_ref.1, bf16[256,512]{1,0:T(8,128)(2,1)} %k_ref.1, bf16[256,512]{1,0:T(8,128)(2,1)} %v_ref.1, ...), custom_call_target="tpu_custom_call" | custom-call | tf_op jit(solution)/shard_map/pack/pallas_call | solution.py:105
  3.3 0.0 copy-start.8
  3.4 5.9 %collective-permute-start.1 = (bf16[768,128]{1,0:T(8,128)(2,1)}, bf16[768,128]{1,0:T(8,128)(2,1)S(1)}, u32[]{:S(2)}, u32[]{:S(2)}) collective-permute-start(bf16[768,128]{1,0:T(8,128)(2,1)} %get-tuple-element.43), channel_id=1, source_target_pairs={{0,112},{8,120},{16,32},{24,40},{32,16},{40,24},{48,64},{56,72},{6... | collective-permute-start | bytes 589832 | tf_op jit(solution)/shard_map/ppermute | solution.py:49
  9.3 0.0 collective-permute-start.2
  9.3 1.3 %collective-permute-start.4 = (bf16[512,128]{1,0:T(8,128)(2,1)}, bf16[512,128]{1,0:T(8,128)(2,1)S(1)}, u32[]{:S(2)}, u32[]{:S(2)}) collective-permute-start(bf16[512,128]{1,0:T(8,128)(2,1)} %get-tuple-element.45), channel_id=1, source_target_pairs={{0,128},{8,136},{16,144},{24,152},{32,160},{40,168},{48,176},{56,1... | collective-permute-start | bytes 393224 | tf_op jit(solution)/shard_map/ppermute | solution.py:49
  10.6 1.6 %collective-permute-start.3 = (bf16[512,128]{1,0:T(8,128)(2,1)}, bf16[512,128]{1,0:T(8,128)(2,1)S(1)}, u32[]{:S(2)}, u32[]{:S(2)}) collective-permute-start(bf16[512,128]{1,0:T(8,128)(2,1)} %get-tuple-element.45), channel_id=1, source_target_pairs={{0,16},{8,24},{16,0},{24,8},{32,48},{40,56},{48,32},{56,40},{64,80... | collective-permute-start | bytes 393224 | tf_op jit(solution)/shard_map/ppermute | solution.py:49
  12.2 1.9 %collective-permute-start = (bf16[128,1024]{1,0:T(8,128)(2,1)}, bf16[128,1024]{1,0:T(8,128)(2,1)S(1)}, u32[]{:S(2)}, u32[]{:S(2)}) collective-permute-start(bf16[128,1024]{1,0:T(8,128)(2,1)} %get-tuple-element.42), channel_id=1, source_target_pairs={{0,8},{8,16},{16,24},{24,32},{32,40},{40,48},{48,56},{56,64},{64,7... | collective-permute-start | bytes 786440 | tf_op jit(solution)/shard_map/ppermute | solution.py:49
  14.1 3.8 %collective-permute-done.1.refs_1_.refs_5_ = bf16[768,128]{1,0:T(8,128)(2,1)S(1)} collective-permute-done((bf16[768,128]{1,0:T(8,128)(2,1)}, bf16[768,128]{1,0:T(8,128)(2,1)S(1)}, u32[]{:S(2)}, u32[]{:S(2)}) %collective-permute-start.1) | collective-permute-done | bytes 196640 | tf_op jit(solution)/shard_map/ppermute | solution.py:49
  18.0 3.3 %collective-permute-start.6 = (bf16[768,128]{1,0:T(8,128)(2,1)}, bf16[768,128]{1,0:T(8,128)(2,1)S(1)}, u32[]{:S(2)}, u32[]{:S(2)}) collective-permute-start(bf16[768,128]{1,0:T(8,128)(2,1)} %get-tuple-element.51), channel_id=1, source_target_pairs={{0,80},{8,88},{16,64},{24,72},{32,112},{40,120},{48,96},{56,104},{... | collective-permute-start | bytes 589832 | tf_op jit(solution)/shard_map/ppermute | solution.py:49
  21.3 0.0 collective-permute-done.2.refs_2_.refs_6_
  21.3 0.0 copy-start.5
  21.3 0.0 copy-start.4
  21.3 0.0 copy-start.1
  21.4 0.0 copy-start.2
  21.4 0.0 copy-start.3
  21.4 0.0 collective-permute-done.4.refs_8_
  21.4 0.0 collective-permute-done.3.refs_7_
  21.4 2.3 %collective-permute-start.10 = (bf16[1024,128]{1,0:T(8,128)(2,1)S(1)}, bf16[1024,128]{1,0:T(8,128)(2,1)S(1)}, u32[]{:S(2)}, u32[]{:S(2)}) collective-permute-start(bf16[1024,128]{1,0:T(8,128)(2,1)S(1)} %pad_maximum_fusion.4), channel_id=1, source_target_pairs={{0,16},{8,24},{16,0},{24,8},{32,48},{40,56},{48,32},{56,40},{64,80... | collective-permute-start | bytes 786440 | tf_op jit(solution)/shard_map/ppermute | solution.py:49
  23.7 0.0 copy-done.8
  23.8 0.1 collective-permute-start.8
  23.9 1.3 %collective-permute-start.14 = (bf16[1536,128]{1,0:T(8,128)(2,1)S(1)}, bf16[1536,128]{1,0:T(8,128)(2,1)S(1)}, u32[]{:S(2)}, u32[]{:S(2)}) collective-permute-start(bf16[1536,128]{1,0:T(8,128)(2,1)S(1)} %pad_maximum_fusion.3), channel_id=1, source_target_pairs={{0,128},{8,136},{16,144},{24,152},{32,160},{40,168},{48,176},{56,1... | collective-permute-start | bytes 1179656 | tf_op jit(solution)/shard_map/ppermute | solution.py:49
  25.2 0.0 collective-permute-done.halo_ref
  25.2 0.0 copy-done.6
  25.2 0.0 copy-done.5
  25.2 0.0 copy-done.4
  25.3 3.9 %filter.1 = (bf16[256,1024]{1,0:T(8,128)(2,1)}, f32[8,256]{1,0:T(8,128)S(1)}) custom-call(bf16[384,512]{1,0:T(8,128)(2,1)S(1)} %copy-done.5, bf16[256,1024]{1,0:T(8,128)(2,1)S(1)} %copy-done.1, bf16[256,1024]{1,0:T(8,128)(2,1)S(1)} %copy-done.2, bf16[256,1024]{1,0:T(8,128)(2,1)S(1)} %copy-done.3, bf16[256,1024]{1,0:T(8,128)(2,1)S(1)} %copy-done.4, ...), custom_call_target="tpu_custom_call" | custom-call | flops 1024 | bytes 1024 | tf_op jit(solution)/shard_map/filter/pallas_call | solution.py:346
  29.2 1.5 %collective-permute-start.5 = (f32[256]{0:T(256)S(1)}, f32[256]{0:T(256)S(1)}, u32[]{:S(2)}, u32[]{:S(2)}) collective-permute-start(f32[256]{0:T(256)S(1)} %bitcast.1), channel_id=1, source_target_pairs={{0,1},{1,0},{2,3},{3,2},{4,5},{5,4},{6,7},{7,6},{8,9},{9,8},{10,11... | collective-permute-start | bytes 3080 | tf_op jit(solution)/shard_map/ppermute | solution.py:361
  30.7 0.0 collective-permute-done.6.refs_3_.refs_4_
  30.7 0.3 collective-permute-start.13
  31.0 2.2 %collective-permute-done.10.refs_5_ = bf16[1024,128]{1,0:T(8,128)(2,1)S(1)} collective-permute-done((bf16[1024,128]{1,0:T(8,128)(2,1)S(1)}, bf16[1024,128]{1,0:T(8,128)(2,1)S(1)}, u32[]{:S(2)}, u32[]{:S(2)}) %collective-permute-start.10) | collective-permute-done | bytes 262176 | tf_op jit(solution)/shard_map/ppermute | solution.py:49
  33.2 0.1 collective-permute-start.12
  33.3 0.0 collective-permute-done.5
  33.3 1.3 %collective-permute-start.11 = (bf16[1536,128]{1,0:T(8,128)(2,1)S(1)}, bf16[1536,128]{1,0:T(8,128)(2,1)S(1)}, u32[]{:S(2)}, u32[]{:S(2)}) collective-permute-start(bf16[1536,128]{1,0:T(8,128)(2,1)S(1)} %constant_dynamic-update-slice_fusion), channel_id=1, source_target_pairs={{0,128},{8,136},{16,144},{24,152},{32,160},{40,168},{48,176},{56,1... | collective-permute-start | bytes 1179656 | tf_op jit(solution)/shard_map/ppermute | solution.py:49
  34.6 0.0 collective-permute-done.8.refs_8_
  34.6 3.3 %collective-permute-start.7 = (f32[256]{0:T(256)S(1)}, f32[256]{0:T(256)S(1)}, u32[]{:S(2)}, u32[]{:S(2)}) collective-permute-start(f32[256]{0:T(256)S(1)} %add.16), channel_id=1, source_target_pairs={{0,2},{1,3},{2,0},{3,1},{4,6},{5,7},{6,4},{7,5},{8,10},{9,11},{10,... | collective-permute-start | bytes 3080 | tf_op jit(solution)/shard_map/ppermute | solution.py:361
  37.9 3.2 %wave.4 = (f32[1024,256]{1,0:T(8,128)S(1)}, f32[1024,128]{1,0:T(8,128)S(1)}) custom-call(bf16[768,128]{1,0:T(8,128)(2,1)S(1)} %copy-done, bf16[768,128]{1,0:T(8,128)(2,1)S(1)} %collective-permute-done.1.refs_1_.refs_5_, bf16[768,128]{1,0:T(8,128)(2,1)S(1)} %collective-permute-done.2.refs_2_.refs_6_, ...), custom_call_target="tpu_custom_call" | custom-call | flops 1024 | bytes 1024 | tf_op jit(solution)/shard_map/wave/pallas_call | solution.py:246
  41.1 0.0 collective-permute-done.13.refs_7_
  41.1 1.3 %collective-permute-start.15 = (bf16[512,128]{1,0:T(8,128)(2,1)S(1)}, bf16[512,128]{1,0:T(8,128)(2,1)S(1)}, u32[]{:S(2)}, u32[]{:S(2)}) collective-permute-start(bf16[512,128]{1,0:T(8,128)(2,1)S(1)} %collective-permute-done.13.refs_7_), channel_id=1, source_target_pairs={{0,128},{8,136},{16,144},{24,152},{32,160},{40,168},{48,176},{56,1... | collective-permute-start | bytes 393224 | tf_op jit(solution)/shard_map/ppermute | solution.py:49
  42.4 0.0 collective-permute-done.14.refs_9_
  42.5 0.3 collective-permute-start.17
  42.7 0.0 collective-permute-done.7
  42.7 0.0 collective-permute-done.12.refs_6_
  42.7 3.6 %wave.5 = (f32[1024,256]{1,0:T(8,128)S(1)}, f32[1024,128]{1,0:T(8,128)S(1)}) custom-call(bf16[768,128]{1,0:T(8,128)(2,1)S(1)} %copy-done, bf16[768,128]{1,0:T(8,128)(2,1)S(1)} %collective-permute-done.1.refs_1_.refs_5_, bf16[768,128]{1,0:T(8,128)(2,1)S(1)} %collective-permute-done.2.refs_2_.refs_6_, ...), custom_call_target="tpu_custom_call" | custom-call | flops 1024 | bytes 1024 | tf_op jit(solution)/shard_map/wave/pallas_call | solution.py:246
  46.3 2.3 %collective-permute-done.11.refs_4_ = bf16[1536,128]{1,0:T(8,128)(2,1)S(1)} collective-permute-done((bf16[1536,128]{1,0:T(8,128)(2,1)S(1)}, bf16[1536,128]{1,0:T(8,128)(2,1)S(1)}, u32[]{:S(2)}, u32[]{:S(2)}) %collective-permute-start.11) | collective-permute-done | bytes 393248 | tf_op jit(solution)/shard_map/ppermute | solution.py:49
  48.6 2.4 %collective-permute-done.15.refs_5_ = bf16[512,128]{1,0:T(8,128)(2,1)S(1)} collective-permute-done((bf16[512,128]{1,0:T(8,128)(2,1)S(1)}, bf16[512,128]{1,0:T(8,128)(2,1)S(1)}, u32[]{:S(2)}, u32[]{:S(2)}) %collective-permute-start.15) | collective-permute-done | bytes 131104 | tf_op jit(solution)/shard_map/ppermute | solution.py:49
  51.0 0.1 collective-permute-start.16
  51.1 1.4 %collective-permute-start.9 = (f32[256]{0:T(256)S(1)}, f32[256]{0:T(256)S(1)}, u32[]{:S(2)}, u32[]{:S(2)}) collective-permute-start(f32[256]{0:T(256)S(1)} %add.17), channel_id=1, source_target_pairs={{0,4},{1,5},{2,6},{3,7},{4,0},{5,1},{6,2},{7,3},{8,12},{9,13},{10,... | collective-permute-start | bytes 3080 | tf_op jit(solution)/shard_map/ppermute | solution.py:361
  52.5 0.0 collective-permute-done.17.refs_4_
  52.5 2.0 %wave.6 = (f32[1024,256]{1,0:T(8,128)S(1)}, f32[1024,128]{1,0:T(8,128)S(1)}) custom-call(bf16[768,128]{1,0:T(8,128)(2,1)S(1)} %copy-done, bf16[768,128]{1,0:T(8,128)(2,1)S(1)} %collective-permute-done.1.refs_1_.refs_5_, bf16[768,128]{1,0:T(8,128)(2,1)S(1)} %collective-permute-done.2.refs_2_.refs_6_, ...), custom_call_target="tpu_custom_call" | custom-call | flops 1024 | bytes 1024 | tf_op jit(solution)/shard_map/wave/pallas_call | solution.py:246
  54.5 0.0 collective-permute-done.16.refs_6_
  54.5 0.0 copy-start.7
  54.6 0.0 copy-start.9
  54.6 2.8 %wave.7 = (bf16[256,128]{1,0:T(8,128)(2,1)S(1)}, bf16[256,128]{1,0:T(8,128)(2,1)S(1)}, bf16[256,128]{1,0:T(8,128)(2,1)S(1)}, bf16[256,128]{1,0:T(8,128)(2,1)S(1)}) custom-call(bf16[768,128]{1,0:T(8,128)(2,1)S(1)} %copy-done, bf16[768,128]{1,0:T(8,128)(2,1)S(1)} %collective-permute-done.1.refs_1_.refs_5_, ...), custom_call_target="tpu_custom_call" | custom-call | flops 1024 | bytes 1024 | tf_op jit(solution)/shard_map/wave/pallas_call | solution.py:246
  57.4 1.3 %collective-permute-start.18 = (bf16[256,128]{1,0:T(8,128)(2,1)S(1)}, bf16[256,128]{1,0:T(8,128)(2,1)S(1)}, u32[]{:S(2)}, u32[]{:S(2)}) collective-permute-start(bf16[256,128]{1,0:T(8,128)(2,1)S(1)} %get-tuple-element.66), channel_id=1, source_target_pairs={{112,0},{120,8},{32,16},{40,24},{16,32},{24,40},{64,48},{72,56},{4... | collective-permute-start | bytes 196616 | tf_op jit(solution)/shard_map/ppermute | solution.py:53
  58.7 3.3 %collective-permute-start.19 = (bf16[256,128]{1,0:T(8,128)(2,1)S(1)}, bf16[256,128]{1,0:T(8,128)(2,1)S(1)}, u32[]{:S(2)}, u32[]{:S(2)}) collective-permute-start(bf16[256,128]{1,0:T(8,128)(2,1)S(1)} %get-tuple-element.67), channel_id=1, source_target_pairs={{32,0},{40,8},{112,16},{120,24},{64,32},{72,40},{16,48},{24,56},{9... | collective-permute-start | bytes 196616 | tf_op jit(solution)/shard_map/ppermute | solution.py:53
  62.0 1.1 %collective-permute-start.20 = (bf16[256,128]{1,0:T(8,128)(2,1)S(1)}, bf16[256,128]{1,0:T(8,128)(2,1)S(1)}, u32[]{:S(2)}, u32[]{:S(2)}) collective-permute-start(bf16[256,128]{1,0:T(8,128)(2,1)S(1)} %get-tuple-element.68), channel_id=1, source_target_pairs={{80,0},{88,8},{64,16},{72,24},{112,32},{120,40},{96,48},{104,56},{... | collective-permute-start | bytes 196616 | tf_op jit(solution)/shard_map/ppermute | solution.py:53
  63.1 0.0 collective-permute-done.9
  63.1 0.0 copy-done.7
  63.1 0.0 copy-done.9
  63.1 1.0 %multiply_convert_fusion = bf16[256,1024]{1,0:T(8,128)(2,1)} fusion(bf16[256,1024]{1,0:T(8,128)(2,1)S(1)} %copy-done.7, f32[1024]{0:T(1024)S(1)} %copy-done.9, f32[256]{0:T(256)S(1)} %add_rsqrt_fusion), kind=kLoop, calls=%fused_computation | loop fusion | flops 1048576 | bytes 1053696 | tf_op jit(solution)/shard_map/convert_element_type | solution.py:453
  64.1 0.0 collective-permute-done.18.o1
  64.1 0.9 %collective-permute-done.19.o2 = bf16[256,128]{1,0:T(8,128)(2,1)S(1)} collective-permute-done((bf16[256,128]{1,0:T(8,128)(2,1)S(1)}, bf16[256,128]{1,0:T(8,128)(2,1)S(1)}, u32[]{:S(2)}, u32[]{:S(2)}) %collective-permute-start.19) | collective-permute-done | bytes 65568 | tf_op jit(solution)/shard_map/ppermute | solution.py:53
  65.0 5.1 %collective-permute-done.20.o3 = bf16[256,128]{1,0:T(8,128)(2,1)S(1)} collective-permute-done((bf16[256,128]{1,0:T(8,128)(2,1)S(1)}, bf16[256,128]{1,0:T(8,128)(2,1)S(1)}, u32[]{:S(2)}, u32[]{:S(2)}) %collective-permute-start.20) | collective-permute-done | bytes 65568 | tf_op jit(solution)/shard_map/ppermute | solution.py:53
  70.1 0.8 %unpack.1 = bf16[256,512]{1,0:T(8,128)(2,1)} custom-call(bf16[256,128]{1,0:T(8,128)(2,1)S(1)} %get-tuple-element.64.o0, bf16[256,128]{1,0:T(8,128)(2,1)S(1)} %collective-permute-done.18.o1, bf16[256,128]{1,0:T(8,128)(2,1)S(1)} %collective-permute-done.19.o2, bf16[256,128]{1,0:T(8,128)(2,1)S(1)} %collective-permute-done.20.o3), custom_call_target="tpu_custom_call" | custom-call | tf_op jit(solution)/shard_map/unpack/pallas_call | solution.py:126
  (20 shorter events, 0.3 us)
Async XLA Ops:
  3.3 20.4 %copy-start.8 = (bf16[512,128]{1,0:T(8,128)(2,1)S(1)}, bf16[512,128]{1,0:T(8,128)(2,1)}, u32[]{:S(2)}) copy-start(bf16[512,128]{1,0:T(8,128)(2,1)} %get-tuple-element.45) | copy-start | bytes 393220
  3.4 14.6 %collective-permute-start.1 = (bf16[768,128]{1,0:T(8,128)(2,1)}, bf16[768,128]{1,0:T(8,128)(2,1)S(1)}, u32[]{:S(2)}, u32[]{:S(2)}) collective-permute-start(bf16[768,128]{1,0:T(8,128)(2,1)} %get-tuple-element.43), channel_id=1, source_target_pairs={{0,112},{8,120},{16,32},{24,40},{32,16},{40,24},{48,64},{56,72},{6... | collective-permute-start | bytes 589832 | tf_op jit(solution)/shard_map/ppermute | solution.py:49
  9.3 12.0 %collective-permute-start.2 = (bf16[768,128]{1,0:T(8,128)(2,1)}, bf16[768,128]{1,0:T(8,128)(2,1)S(1)}, u32[]{:S(2)}, u32[]{:S(2)}) collective-permute-start(bf16[768,128]{1,0:T(8,128)(2,1)} %get-tuple-element.44), channel_id=1, source_target_pairs={{0,32},{8,40},{16,112},{24,120},{32,64},{40,72},{48,16},{56,24},{6... | collective-permute-start | bytes 589832 | tf_op jit(solution)/shard_map/ppermute | solution.py:49
  9.3 12.1 %collective-permute-start.4 = (bf16[512,128]{1,0:T(8,128)(2,1)}, bf16[512,128]{1,0:T(8,128)(2,1)S(1)}, u32[]{:S(2)}, u32[]{:S(2)}) collective-permute-start(bf16[512,128]{1,0:T(8,128)(2,1)} %get-tuple-element.45), channel_id=1, source_target_pairs={{0,128},{8,136},{16,144},{24,152},{32,160},{40,168},{48,176},{56,1... | collective-permute-start | bytes 393224 | tf_op jit(solution)/shard_map/ppermute | solution.py:49
  10.6 10.8 %collective-permute-start.3 = (bf16[512,128]{1,0:T(8,128)(2,1)}, bf16[512,128]{1,0:T(8,128)(2,1)S(1)}, u32[]{:S(2)}, u32[]{:S(2)}) collective-permute-start(bf16[512,128]{1,0:T(8,128)(2,1)} %get-tuple-element.45), channel_id=1, source_target_pairs={{0,16},{8,24},{16,0},{24,8},{32,48},{40,56},{48,32},{56,40},{64,80... | collective-permute-start | bytes 393224 | tf_op jit(solution)/shard_map/ppermute | solution.py:49
  12.2 13.0 %collective-permute-start = (bf16[128,1024]{1,0:T(8,128)(2,1)}, bf16[128,1024]{1,0:T(8,128)(2,1)S(1)}, u32[]{:S(2)}, u32[]{:S(2)}) collective-permute-start(bf16[128,1024]{1,0:T(8,128)(2,1)} %get-tuple-element.42), channel_id=1, source_target_pairs={{0,8},{8,16},{16,24},{24,32},{32,40},{40,48},{48,56},{56,64},{64,7... | collective-permute-start | bytes 786440 | tf_op jit(solution)/shard_map/ppermute | solution.py:49
  18.0 12.7 %collective-permute-start.6 = (bf16[768,128]{1,0:T(8,128)(2,1)}, bf16[768,128]{1,0:T(8,128)(2,1)S(1)}, u32[]{:S(2)}, u32[]{:S(2)}) collective-permute-start(bf16[768,128]{1,0:T(8,128)(2,1)} %get-tuple-element.51), channel_id=1, source_target_pairs={{0,80},{8,88},{16,64},{24,72},{32,112},{40,120},{48,96},{56,104},{... | collective-permute-start | bytes 589832 | tf_op jit(solution)/shard_map/ppermute | solution.py:49
  21.3 3.9 %copy-start.6 = (bf16[1024,128]{1,0:T(8,128)(2,1)S(1)}, bf16[1024,128]{1,0:T(8,128)(2,1)}, u32[]{:S(2)}) copy-start(bf16[1024,128]{1,0:T(8,128)(2,1)} %taps_ref) | copy-start | bytes 786436
  21.3 3.9 %copy-start.5 = (bf16[384,512]{1,0:T(8,128)(2,1)S(1)}, bf16[384,512]{1,0:T(8,128)(2,1)}, u32[]{:S(2)}) copy-start(bf16[384,512]{1,0:T(8,128)(2,1)} %constant.7.clone.matrix_ref) | copy-start | bytes 1179652
  21.3 3.9 %copy-start.4 = (bf16[256,1024]{1,0:T(8,128)(2,1)S(1)}, bf16[256,1024]{1,0:T(8,128)(2,1)}, u32[]{:S(2)}) copy-start(bf16[256,1024]{1,0:T(8,128)(2,1)} %res_ref) | copy-start | bytes 1572868
  21.3 3.9 %copy-start.1 = (bf16[256,1024]{1,0:T(8,128)(2,1)S(1)}, bf16[256,1024]{1,0:T(8,128)(2,1)}, u32[]{:S(2)}) copy-start(bf16[256,1024]{1,0:T(8,128)(2,1)} %key_ref.2) | copy-start | bytes 1572868
  21.4 3.9 %copy-start.2 = (bf16[256,1024]{1,0:T(8,128)(2,1)S(1)}, bf16[256,1024]{1,0:T(8,128)(2,1)}, u32[]{:S(2)}) copy-start(bf16[256,1024]{1,0:T(8,128)(2,1)} %value_ref.2) | copy-start | bytes 1572868
  21.4 3.9 %copy-start.3 = (bf16[256,1024]{1,0:T(8,128)(2,1)S(1)}, bf16[256,1024]{1,0:T(8,128)(2,1)}, u32[]{:S(2)}) copy-start(bf16[256,1024]{1,0:T(8,128)(2,1)} %gate_ref) | copy-start | bytes 1572868
  21.4 11.7 %collective-permute-start.10 = (bf16[1024,128]{1,0:T(8,128)(2,1)S(1)}, bf16[1024,128]{1,0:T(8,128)(2,1)S(1)}, u32[]{:S(2)}, u32[]{:S(2)}) collective-permute-start(bf16[1024,128]{1,0:T(8,128)(2,1)S(1)} %pad_maximum_fusion.4), channel_id=1, source_target_pairs={{0,16},{8,24},{16,0},{24,8},{32,48},{40,56},{48,32},{56,40},{64,80... | collective-permute-start | bytes 786440 | tf_op jit(solution)/shard_map/ppermute | solution.py:49
  23.8 10.8 %collective-permute-start.8 = (bf16[2048,128]{1,0:T(8,128)(2,1)S(1)}, bf16[2048,128]{1,0:T(8,128)(2,1)S(1)}, u32[]{:S(2)}, u32[]{:S(2)}) collective-permute-start(bf16[2048,128]{1,0:T(8,128)(2,1)S(1)} %pad_maximum_fusion.1), channel_id=1, source_target_pairs={{0,8},{8,0},{16,24},{24,16},{32,40},{40,32},{48,56},{56,48},{64,72... | collective-permute-start | bytes 1572872 | tf_op jit(solution)/shard_map/ppermute | solution.py:49
  23.9 18.5 %collective-permute-start.14 = (bf16[1536,128]{1,0:T(8,128)(2,1)S(1)}, bf16[1536,128]{1,0:T(8,128)(2,1)S(1)}, u32[]{:S(2)}, u32[]{:S(2)}) collective-permute-start(bf16[1536,128]{1,0:T(8,128)(2,1)S(1)} %pad_maximum_fusion.3), channel_id=1, source_target_pairs={{0,128},{8,136},{16,144},{24,152},{32,160},{40,168},{48,176},{56,1... | collective-permute-start | bytes 1179656 | tf_op jit(solution)/shard_map/ppermute | solution.py:49
  29.2 8.7 %copy-start = (bf16[768,128]{1,0:T(8,128)(2,1)S(1)}, bf16[768,128]{1,0:T(8,128)(2,1)}, u32[]{:S(2)}) copy-start(bf16[768,128]{1,0:T(8,128)(2,1)} %get-tuple-element.36.refs_0_.refs_4_) | copy-start | bytes 589828
  29.2 4.1 %collective-permute-start.5 = (f32[256]{0:T(256)S(1)}, f32[256]{0:T(256)S(1)}, u32[]{:S(2)}, u32[]{:S(2)}) collective-permute-start(f32[256]{0:T(256)S(1)} %bitcast.1), channel_id=1, source_target_pairs={{0,1},{1,0},{2,3},{3,2},{4,5},{5,4},{6,7},{7,6},{8,9},{9,8},{10,11... | collective-permute-start | bytes 3080 | tf_op jit(solution)/shard_map/ppermute | solution.py:361
  30.7 10.4 %collective-permute-start.13 = (bf16[512,128]{1,0:T(8,128)(2,1)S(1)}, bf16[512,128]{1,0:T(8,128)(2,1)S(1)}, u32[]{:S(2)}, u32[]{:S(2)}) collective-permute-start(bf16[512,128]{1,0:T(8,128)(2,1)S(1)} %slice.18), channel_id=1, source_target_pairs={{0,16},{8,24},{16,0},{24,8},{32,48},{40,56},{48,32},{56,40},{64,80... | collective-permute-start | bytes 393224 | tf_op jit(solution)/shard_map/ppermute | solution.py:49
  33.2 9.6 %collective-permute-start.12 = (bf16[1536,128]{1,0:T(8,128)(2,1)S(1)}, bf16[1536,128]{1,0:T(8,128)(2,1)S(1)}, u32[]{:S(2)}, u32[]{:S(2)}) collective-permute-start(bf16[1536,128]{1,0:T(8,128)(2,1)S(1)} %constant_dynamic-update-slice_fusion), channel_id=1, source_target_pairs={{0,8},{8,0},{16,24},{24,16},{32,40},{40,32},{48,56},{56,48},{64,72... | collective-permute-start | bytes 1179656 | tf_op jit(solution)/shard_map/ppermute | solution.py:49
  33.3 15.3 %collective-permute-start.11 = (bf16[1536,128]{1,0:T(8,128)(2,1)S(1)}, bf16[1536,128]{1,0:T(8,128)(2,1)S(1)}, u32[]{:S(2)}, u32[]{:S(2)}) collective-permute-start(bf16[1536,128]{1,0:T(8,128)(2,1)S(1)} %constant_dynamic-update-slice_fusion), channel_id=1, source_target_pairs={{0,128},{8,136},{16,144},{24,152},{32,160},{40,168},{48,176},{56,1... | collective-permute-start | bytes 1179656 | tf_op jit(solution)/shard_map/ppermute | solution.py:49
  34.6 8.1 %collective-permute-start.7 = (f32[256]{0:T(256)S(1)}, f32[256]{0:T(256)S(1)}, u32[]{:S(2)}, u32[]{:S(2)}) collective-permute-start(f32[256]{0:T(256)S(1)} %add.16), channel_id=1, source_target_pairs={{0,2},{1,3},{2,0},{3,1},{4,6},{5,7},{6,4},{7,5},{8,10},{9,11},{10,... | collective-permute-start | bytes 3080 | tf_op jit(solution)/shard_map/ppermute | solution.py:361
  41.1 9.9 %collective-permute-start.15 = (bf16[512,128]{1,0:T(8,128)(2,1)S(1)}, bf16[512,128]{1,0:T(8,128)(2,1)S(1)}, u32[]{:S(2)}, u32[]{:S(2)}) collective-permute-start(bf16[512,128]{1,0:T(8,128)(2,1)S(1)} %collective-permute-done.13.refs_7_), channel_id=1, source_target_pairs={{0,128},{8,136},{16,144},{24,152},{32,160},{40,168},{48,176},{56,1... | collective-permute-start | bytes 393224 | tf_op jit(solution)/shard_map/ppermute | solution.py:49
  42.5 10.0 %collective-permute-start.17 = (bf16[2560,128]{1,0:T(8,128)(2,1)S(1)}, bf16[2560,128]{1,0:T(8,128)(2,1)S(1)}, u32[]{:S(2)}, u32[]{:S(2)}) collective-permute-start(bf16[2560,128]{1,0:T(8,128)(2,1)S(1)} %pad_maximum_fusion), channel_id=1, source_target_pairs={{0,8},{8,0},{16,24},{24,16},{32,40},{40,32},{48,56},{56,48},{64,72... | collective-permute-start | bytes 1966088 | tf_op jit(solution)/shard_map/ppermute | solution.py:49
  51.0 3.5 %collective-permute-start.16 = (bf16[2048,128]{1,0:T(8,128)(2,1)S(1)}, bf16[2048,128]{1,0:T(8,128)(2,1)S(1)}, u32[]{:S(2)}, u32[]{:S(2)}) collective-permute-start(bf16[2048,128]{1,0:T(8,128)(2,1)S(1)} %pad_maximum_fusion.2), channel_id=1, source_target_pairs={{0,8},{8,0},{16,24},{24,16},{32,40},{40,32},{48,56},{56,48},{64,72... | collective-permute-start | bytes 1572872 | tf_op jit(solution)/shard_map/ppermute | solution.py:49
  51.1 12.0 %collective-permute-start.9 = (f32[256]{0:T(256)S(1)}, f32[256]{0:T(256)S(1)}, u32[]{:S(2)}, u32[]{:S(2)}) collective-permute-start(f32[256]{0:T(256)S(1)} %add.17), channel_id=1, source_target_pairs={{0,4},{1,5},{2,6},{3,7},{4,0},{5,1},{6,2},{7,3},{8,12},{9,13},{10,... | collective-permute-start | bytes 3080 | tf_op jit(solution)/shard_map/ppermute | solution.py:361
  54.5 8.5 %copy-start.7 = (bf16[256,1024]{1,0:T(8,128)(2,1)S(1)}, bf16[256,1024]{1,0:T(8,128)(2,1)}, u32[]{:S(2)}) copy-start(bf16[256,1024]{1,0:T(8,128)(2,1)} %get-tuple-element.33) | copy-start | bytes 1572868
  54.6 8.5 %copy-start.9 = (f32[1024]{0:T(1024)S(1)}, f32[1024]{0:T(1024)}, u32[]{:S(2)}) copy-start(f32[1024]{0:T(1024)} %param.15) | copy-start | bytes 12292
  57.4 6.7 %collective-permute-start.18 = (bf16[256,128]{1,0:T(8,128)(2,1)S(1)}, bf16[256,128]{1,0:T(8,128)(2,1)S(1)}, u32[]{:S(2)}, u32[]{:S(2)}) collective-permute-start(bf16[256,128]{1,0:T(8,128)(2,1)S(1)} %get-tuple-element.66), channel_id=1, source_target_pairs={{112,0},{120,8},{32,16},{40,24},{16,32},{24,40},{64,48},{72,56},{4... | collective-permute-start | bytes 196616 | tf_op jit(solution)/shard_map/ppermute | solution.py:53
  58.7 6.3 %collective-permute-start.19 = (bf16[256,128]{1,0:T(8,128)(2,1)S(1)}, bf16[256,128]{1,0:T(8,128)(2,1)S(1)}, u32[]{:S(2)}, u32[]{:S(2)}) collective-permute-start(bf16[256,128]{1,0:T(8,128)(2,1)S(1)} %get-tuple-element.67), channel_id=1, source_target_pairs={{32,0},{40,8},{112,16},{120,24},{64,32},{72,40},{16,48},{24,56},{9... | collective-permute-start | bytes 196616 | tf_op jit(solution)/shard_map/ppermute | solution.py:53
  62.0 8.1 %collective-permute-start.20 = (bf16[256,128]{1,0:T(8,128)(2,1)S(1)}, bf16[256,128]{1,0:T(8,128)(2,1)S(1)}, u32[]{:S(2)}, u32[]{:S(2)}) collective-permute-start(bf16[256,128]{1,0:T(8,128)(2,1)S(1)} %get-tuple-element.68), channel_id=1, source_target_pairs={{80,0},{88,8},{64,16},{72,24},{112,32},{120,40},{96,48},{104,56},{... | collective-permute-start | bytes 196616 | tf_op jit(solution)/shard_map/ppermute | solution.py:53

commit v4 on v3

--- a/solution.py
+++ b/solution.py
@@ -42,6 +42,7 @@
 SIBLING = pairs(lambda p, z, c: (p, z ^ 1, c))
 CORE = pairs(lambda p, z, c: (p, z, 1 - c))
 DOWN = pairs(lambda p, z, c: (1, z, c) if p == 0 else None)
+ASLANT = pairs(lambda p, z, c: (1, z ^ 1, c) if p == 0 else None)
 NEXT = [(i, i + 1) for i in range(2 * ZS * 2 - 1)]
 
 
@@ -67,30 +68,36 @@
     return [lax.div(lax.rem(z + o + ZS, ZS), 2) for o in offsets]
 
 
-def pack_kernel(
-    q_ref, k_ref, v_ref, key_ref, value_ref, edge, o0, o1, o2, o3, own, key_tail, value_tail, sems
+def column_copies(refs, out, head, sems):
+    columns = pl.ds(pl.multiple_of(head * DH, DH), DH)
+    return [
+        pltpu.make_async_copy(ref.at[:, columns], out.at[n * ROWS : (n + 1) * ROWS, :], sems.at[n])
+        for n, ref in enumerate(refs)
+    ]
+
+
+def pack_kernel(q_ref, k_ref, v_ref, o1, o2, sems):
+    heads = target_heads(place()[1])
+    copies = []
+    for n, (j, out) in enumerate(((1, o1), (2, o2))):
+        copies += column_copies((q_ref, k_ref, v_ref), out, heads[j], sems.at[n])
+    for copy in copies:
+        copy.start()
+    for copy in copies:
+        copy.wait()
+
+
+def pack_rest_kernel(
+    q_ref, k_ref, v_ref, key_ref, value_ref, edge, o0, o3, own, key_tail, value_tail, sems
 ):
-    _, z, _ = place()
+    heads = target_heads(place()[1])
     tails = [
-        pltpu.make_async_copy(ref.at[ROWS - TAPS : ROWS, :], tail, sems.at[12 + n])
+        pltpu.make_async_copy(ref.at[ROWS - TAPS : ROWS, :], tail, sems.at[3, n])
         for n, (ref, tail) in enumerate(((key_ref, key_tail), (value_ref, value_tail)))
     ]
-    copies = []
-    for j, (head, out) in enumerate(zip(target_heads(z), (o0, o1, o2, o3))):
-        columns = pl.ds(pl.multiple_of(head * DH, DH), DH)
-        for n, ref in enumerate((q_ref, k_ref, v_ref)):
-            copies.append(
-                pltpu.make_async_copy(
-                    ref.at[:, columns], out.at[n * ROWS : (n + 1) * ROWS, :], sems.at[3 * j + n]
-                )
-            )
-    columns = pl.ds(pl.multiple_of(target_heads(z)[0] * DH, DH), DH)
-    for n, ref in enumerate((k_ref, v_ref)):
-        copies.append(
-            pltpu.make_async_copy(
-                ref.at[:, columns], own.at[n * ROWS : (n + 1) * ROWS, :], sems.at[14 + n]
-            )
-        )
+    copies = column_copies((k_ref, v_ref), own, heads[0], sems.at[0])
+    for n, (j, out) in enumerate(((0, o0), (3, o3))):
+        copies += column_copies((q_ref, k_ref, v_ref), out, heads[j], sems.at[1 + n])
     for copy in copies + tails:
         copy.start()
     for copy in tails:
@@ -100,19 +107,31 @@
         copy.wait()
 
 
-def pack(q, k, v, key, value):
+def pack(q, k, v):
+    return pl.pallas_call(
+        pack_kernel,
+        out_shape=[jax.ShapeDtypeStruct((3 * ROWS, DH), BF16)] * 2,
+        in_specs=[pl.BlockSpec(memory_space=pltpu.HBM)] * 3,
+        out_specs=[pl.BlockSpec(memory_space=pltpu.VMEM)] * 2,
+        scratch_shapes=[pltpu.SemaphoreType.DMA((2, 3))],
+        compiler_params=pltpu.CompilerParams(vmem_limit_bytes=60 << 20),
+        name="pack",
+    )(q, k, v)
+
+
+def pack_rest(q, k, v, key, value):
     channels = key.shape[1]
     return pl.pallas_call(
-        pack_kernel,
+        pack_rest_kernel,
         out_shape=[jax.ShapeDtypeStruct((TAPS, channels), BF16)]
-        + [jax.ShapeDtypeStruct((3 * ROWS, DH), BF16)] * 4
+        + [jax.ShapeDtypeStruct((3 * ROWS, DH), BF16)] * 2
         + [jax.ShapeDtypeStruct((2 * ROWS, DH), BF16)],
         in_specs=[pl.BlockSpec(memory_space=pltpu.HBM)] * 5,
-        out_specs=[pl.BlockSpec(memory_space=pltpu.VMEM)] * 6,
+        out_specs=[pl.BlockSpec(memory_space=pltpu.VMEM)] * 4,
         scratch_shapes=[pltpu.VMEM((TAPS, channels), BF16)] * 2
-        + [pltpu.SemaphoreType.DMA((16,))],
+        + [pltpu.SemaphoreType.DMA((4, 3))],
         compiler_params=pltpu.CompilerParams(vmem_limit_bytes=60 << 20),
-        name="pack",
+        name="pack_rest",
     )(q, k, v, key, value)
 
 
@@ -372,9 +391,13 @@
     attn_keys,
     attn_values,
 ):
-    edge, *messages, kv0 = pack(queries, attn_keys, attn_values, key_proj, value_proj)
-    one = send(messages[1], NEAR[1])
-    two = send(messages[2], NEAR[2])
+    message1, message2 = pack(queries, attn_keys, attn_values)
+    one = send(message1, NEAR[1])
+    two = send(message2, NEAR[2])
+    edge, message0, message3, kv0 = pack_rest(
+        tie(queries, message1), attn_keys, attn_values, key_proj, value_proj
+    )
+    messages = [message0, message1, message2, message3]
     far0 = send(kv0, SIBLING)
     low0 = send(kv0, DOWN)
     halo = send(edge, NEXT)
@@ -397,6 +420,7 @@
     total = swap_sum(squares[0], 1, kv3)
     late = jnp.concatenate([kv3, far12])
     low3 = send(late, DOWN)
+    low4 = send(kv3, ASLANT)
     core2 = send(late, CORE)
     got = [messages[0], one, two, three]
     first = [(False, 0), (False, 1), (False, 2), (True, 0)]
@@ -411,7 +435,6 @@
         None,
     )
     far3 = tie(far3, state[1])
-    low4 = send(far3, DOWN)
     core3 = send(jnp.concatenate([far3, low0, low12]), CORE)
     total = swap_sum(total, 2, state[1])
     state = wave(

time: 71.8 us -> 70.4 us (0.981)
  waiting for transfers between devices: 16.7 us -> 12.4 us
  starting transfers between devices: 32.9 us -> 34.6 us
  Pallas kernels: 19 us -> 20.5 us
    ppermute x15, waiting for transfers between devices: 10.7 us -> 6.64 us  [send(): return lax.ppermute(x, 'context', where)]
    ppermute x3, waiting for transfers between devices: 6.04 us -> 4.03 us  [back(): return lax.ppermute(x, 'context', [(b, a) for a, b in where])]
    ppermute x3, waiting for transfers between devices: 0.01 us -> 1.72 us  [swap_sum(): lax.ppermute(x, 'tensor', [(i, i ^ bit) for i in range(8)])]
    ppermute x15, starting transfers between devices: 21 us -> 22.7 us  [send(): return lax.ppermute(x, 'context', where)]
    pallas_call x1 -> x2, Pallas kernels: 2.71 us -> 4.2 us  [the longest x1 2.36 us: pack_rest(): pl.pallas_call(pack_rest_kernel, out_shape=[jax.ShapeDtypeStruct((TAPS, c...]
  transfers between devices with their start and end apart: 21 -> 21, of which waited for: 6 -> 7; matrix products, arithmetic and copies ran while one was open for 2% -> 2% of each run, Pallas kernels for 22% -> 26%
where the time goes in v4:
time: 70.4 us; the launch traced here: 69.7 us
  starting transfers between devices  34.6 us (49%)
  Pallas kernels  20.5 us (29%)
  waiting for transfers between devices  12.4 us (18%)
  other arithmetic  1.16 us (2%)
  between operations  1.01 us (1%)
    ppermute x15, starting transfers between devices, send(): return lax.ppermute(x, 'context', where)  22.7 us
    pallas_call x4, Pallas kernels, wave(): pl.pallas_call(functools.partial(wave_kernel, blocks, first, last, len(ar...  11.6 us
    ppermute x15, waiting for transfers between devices, send(): return lax.ppermute(x, 'context', where)  6.64 us
    ppermute x3, starting transfers between devices, swap_sum(): lax.ppermute(x, 'tensor', [(i, i ^ bit) for i in range(8)])  6.16 us
    ppermute x3, starting transfers between devices, back(): return lax.ppermute(x, 'context', [(b, a) for a, b in where])  5.69 us
    ppermute x3, waiting for transfers between devices, back(): return lax.ppermute(x, 'context', [(b, a) for a, b in where])  4.03 us
    pallas_call x1, Pallas kernels, filter_block(): pl.pallas_call(functools.partial(filter_kernel, 256), out_shape=[jax.Shap...  3.91 us
    pallas_call x1, Pallas kernels, pack_rest(): pl.pallas_call(pack_rest_kernel, out_shape=[jax.ShapeDtypeStruct((TAPS, c...  2.36 us
  transfers between devices with their start and end apart: 21, of which 7 were waited for; matrix products, arithmetic and copies ran while one was open for 2% of the time, Pallas kernels for 26%

profile of v4, /device:TPU:16, one launch (start us, length us, event | category | flops | bytes accessed | tf_op | source)
XLA Modules:
  0.0 69.7 jit_solution(16243144092904673093)
XLA Ops:
  0.6 1.8 %pack.1 = (bf16[768,128]{1,0:T(8,128)(2,1)}, bf16[768,128]{1,0:T(8,128)(2,1)}) custom-call(bf16[256,512]{1,0:T(8,128)(2,1)} %q_ref.2, bf16[256,512]{1,0:T(8,128)(2,1)} %k_ref.3, bf16[256,512]{1,0:T(8,128)(2,1)} %v_ref.3), custom_call_target="tpu_custom_call" | custom-call | tf_op jit(solution)/shard_map/pack/pallas_call | solution.py:111
  2.5 5.9 %collective-permute-start.1 = (bf16[768,128]{1,0:T(8,128)(2,1)}, bf16[768,128]{1,0:T(8,128)(2,1)S(1)}, u32[]{:S(2)}, u32[]{:S(2)}) collective-permute-start(bf16[768,128]{1,0:T(8,128)(2,1)} %get-tuple-element.37), channel_id=1, source_target_pairs={{0,112},{8,120},{16,32},{24,40},{32,16},{40,24},{48,64},{56,72},{6... | collective-permute-start | bytes 589832 | tf_op jit(solution)/shard_map/ppermute | solution.py:50
  8.4 0.0 collective-permute-start.2
  8.4 2.4 %pack_rest.1 = (bf16[128,1024]{1,0:T(8,128)(2,1)}, bf16[768,128]{1,0:T(8,128)(2,1)}, bf16[768,128]{1,0:T(8,128)(2,1)}, bf16[512,128]{1,0:T(8,128)(2,1)}) custom-call(bf16[256,512]{1,0:T(8,128)(2,1)} %q_ref.2, bf16[256,512]{1,0:T(8,128)(2,1)} %k_ref.3, bf16[256,512]{1,0:T(8,128)(2,1)} %v_ref.3, bf16[256,1024]{1,0:T(8,128)(2,1)} %key_ref.2, ...), custom_call_target="tpu_custom_call" | custom-call | tf_op jit(solution)/shard_map/pack_rest/pallas_call | solution.py:124
  10.8 0.0 copy-start.8
  10.8 1.4 %collective-permute-start.4 = (bf16[512,128]{1,0:T(8,128)(2,1)}, bf16[512,128]{1,0:T(8,128)(2,1)S(1)}, u32[]{:S(2)}, u32[]{:S(2)}) collective-permute-start(bf16[512,128]{1,0:T(8,128)(2,1)} %get-tuple-element.47), channel_id=1, source_target_pairs={{0,128},{8,136},{16,144},{24,152},{32,160},{40,168},{48,176},{56,1... | collective-permute-start | bytes 393224 | tf_op jit(solution)/shard_map/ppermute | solution.py:50
  12.2 1.6 %collective-permute-start.3 = (bf16[512,128]{1,0:T(8,128)(2,1)}, bf16[512,128]{1,0:T(8,128)(2,1)S(1)}, u32[]{:S(2)}, u32[]{:S(2)}) collective-permute-start(bf16[512,128]{1,0:T(8,128)(2,1)} %get-tuple-element.47), channel_id=1, source_target_pairs={{0,16},{8,24},{16,0},{24,8},{32,48},{40,56},{48,32},{56,40},{64,80... | collective-permute-start | bytes 393224 | tf_op jit(solution)/shard_map/ppermute | solution.py:50
  13.9 1.9 %collective-permute-start = (bf16[128,1024]{1,0:T(8,128)(2,1)}, bf16[128,1024]{1,0:T(8,128)(2,1)S(1)}, u32[]{:S(2)}, u32[]{:S(2)}) collective-permute-start(bf16[128,1024]{1,0:T(8,128)(2,1)} %get-tuple-element.45), channel_id=1, source_target_pairs={{0,8},{8,16},{16,24},{24,32},{32,40},{40,48},{48,56},{56,64},{64,7... | collective-permute-start | bytes 786440 | tf_op jit(solution)/shard_map/ppermute | solution.py:50
  15.8 2.0 %collective-permute-done.1.refs_1_.refs_5_ = bf16[768,128]{1,0:T(8,128)(2,1)S(1)} collective-permute-done((bf16[768,128]{1,0:T(8,128)(2,1)}, bf16[768,128]{1,0:T(8,128)(2,1)S(1)}, u32[]{:S(2)}, u32[]{:S(2)}) %collective-permute-start.1) | collective-permute-done | bytes 196640 | tf_op jit(solution)/shard_map/ppermute | solution.py:50
  17.8 0.0 collective-permute-done.2.refs_2_.refs_6_
  17.8 0.0 copy-start.5
  17.8 0.0 copy-start.4
  17.8 0.0 copy-start.1
  17.8 0.0 copy-start.2
  17.9 0.0 copy-start.3
  17.9 1.6 %collective-permute-done.4.refs_8_ = bf16[512,128]{1,0:T(8,128)(2,1)S(1)} collective-permute-done((bf16[512,128]{1,0:T(8,128)(2,1)}, bf16[512,128]{1,0:T(8,128)(2,1)S(1)}, u32[]{:S(2)}, u32[]{:S(2)}) %collective-permute-start.4) | collective-permute-done | bytes 131104 | tf_op jit(solution)/shard_map/ppermute | solution.py:50
  19.5 0.0 collective-permute-done.3.refs_7_
  19.5 4.6 %collective-permute-start.6 = (bf16[768,128]{1,0:T(8,128)(2,1)}, bf16[768,128]{1,0:T(8,128)(2,1)S(1)}, u32[]{:S(2)}, u32[]{:S(2)}) collective-permute-start(bf16[768,128]{1,0:T(8,128)(2,1)} %get-tuple-element.53), channel_id=1, source_target_pairs={{0,80},{8,88},{16,64},{24,72},{32,112},{40,120},{48,96},{56,104},{... | collective-permute-start | bytes 589832 | tf_op jit(solution)/shard_map/ppermute | solution.py:50
  24.1 0.0 collective-permute-start.10
  24.1 0.0 copy-done.8
  24.1 0.1 collective-permute-start.8
  24.3 1.3 %collective-permute-start.14 = (bf16[1536,128]{1,0:T(8,128)(2,1)S(1)}, bf16[1536,128]{1,0:T(8,128)(2,1)S(1)}, u32[]{:S(2)}, u32[]{:S(2)}) collective-permute-start(bf16[1536,128]{1,0:T(8,128)(2,1)S(1)} %pad_maximum_fusion.3), channel_id=1, source_target_pairs={{0,128},{8,136},{16,144},{24,152},{32,160},{40,168},{48,176},{56,1... | collective-permute-start | bytes 1179656 | tf_op jit(solution)/shard_map/ppermute | solution.py:50
  25.6 0.0 collective-permute-done.halo_ref
  25.6 0.0 copy-done.6
  25.6 0.0 copy-done.5
  25.6 0.0 copy-done.4
  25.6 3.9 %filter.1 = (bf16[256,1024]{1,0:T(8,128)(2,1)}, f32[8,256]{1,0:T(8,128)S(1)}) custom-call(bf16[384,512]{1,0:T(8,128)(2,1)S(1)} %copy-done.5, bf16[256,1024]{1,0:T(8,128)(2,1)S(1)} %copy-done.1, bf16[256,1024]{1,0:T(8,128)(2,1)S(1)} %copy-done.2, bf16[256,1024]{1,0:T(8,128)(2,1)S(1)} %copy-done.3, bf16[256,1024]{1,0:T(8,128)(2,1)S(1)} %copy-done.4, ...), custom_call_target="tpu_custom_call" | custom-call | flops 1024 | bytes 1024 | tf_op jit(solution)/shard_map/filter/pallas_call | solution.py:365
  29.5 1.5 %collective-permute-start.5 = (f32[256]{0:T(256)S(1)}, f32[256]{0:T(256)S(1)}, u32[]{:S(2)}, u32[]{:S(2)}) collective-permute-start(f32[256]{0:T(256)S(1)} %bitcast.1), channel_id=1, source_target_pairs={{0,1},{1,0},{2,3},{3,2},{4,5},{5,4},{6,7},{7,6},{8,9},{9,8},{10,11... | collective-permute-start | bytes 3080 | tf_op jit(solution)/shard_map/ppermute | solution.py:380
  31.0 0.1 collective-permute-done.6.refs_3_.refs_4_
  31.1 2.8 %collective-permute-start.13 = (bf16[512,128]{1,0:T(8,128)(2,1)S(1)}, bf16[512,128]{1,0:T(8,128)(2,1)S(1)}, u32[]{:S(2)}, u32[]{:S(2)}) collective-permute-start(bf16[512,128]{1,0:T(8,128)(2,1)S(1)} %slice.18), channel_id=1, source_target_pairs={{0,16},{8,24},{16,0},{24,8},{32,48},{40,56},{48,32},{56,40},{64,80... | collective-permute-start | bytes 393224 | tf_op jit(solution)/shard_map/ppermute | solution.py:50
  33.9 0.0 collective-permute-done.10.refs_5_
  34.0 0.1 collective-permute-start.12
  34.1 0.0 collective-permute-done.5
  34.1 1.3 %collective-permute-start.11 = (bf16[1536,128]{1,0:T(8,128)(2,1)S(1)}, bf16[1536,128]{1,0:T(8,128)(2,1)S(1)}, u32[]{:S(2)}, u32[]{:S(2)}) collective-permute-start(bf16[1536,128]{1,0:T(8,128)(2,1)S(1)} %constant_dynamic-update-slice_fusion), channel_id=1, source_target_pairs={{0,128},{8,136},{16,144},{24,152},{32,160},{40,168},{48,176},{56,1... | collective-permute-start | bytes 1179656 | tf_op jit(solution)/shard_map/ppermute | solution.py:50
  35.4 0.0 collective-permute-done.8.refs_8_
  35.4 1.3 %collective-permute-start.15 = (bf16[512,128]{1,0:T(8,128)(2,1)S(1)}, bf16[512,128]{1,0:T(8,128)(2,1)S(1)}, u32[]{:S(2)}, u32[]{:S(2)}) collective-permute-start(bf16[512,128]{1,0:T(8,128)(2,1)S(1)} %slice.18), channel_id=1, source_target_pairs={{0,144},{8,152},{16,128},{24,136},{32,176},{40,184},{48,160},{56,1... | collective-permute-start | bytes 393224 | tf_op jit(solution)/shard_map/ppermute | solution.py:50
  36.7 0.0 copy-done
  36.7 3.2 %wave.4 = (f32[1024,256]{1,0:T(8,128)S(1)}, f32[1024,128]{1,0:T(8,128)S(1)}) custom-call(bf16[768,128]{1,0:T(8,128)(2,1)S(1)} %copy-done, bf16[768,128]{1,0:T(8,128)(2,1)S(1)} %collective-permute-done.1.refs_1_.refs_5_, bf16[768,128]{1,0:T(8,128)(2,1)S(1)} %collective-permute-done.2.refs_2_.refs_6_, ...), custom_call_target="tpu_custom_call" | custom-call | flops 1024 | bytes 1024 | tf_op jit(solution)/shard_map/wave/pallas_call | solution.py:265
  39.9 0.0 collective-permute-done.13.refs_7_
  39.9 3.3 %collective-permute-start.7 = (f32[256]{0:T(256)S(1)}, f32[256]{0:T(256)S(1)}, u32[]{:S(2)}, u32[]{:S(2)}) collective-permute-start(f32[256]{0:T(256)S(1)} %add.16), channel_id=1, source_target_pairs={{0,2},{1,3},{2,0},{3,1},{4,6},{5,7},{6,4},{7,5},{8,10},{9,11},{10,... | collective-permute-start | bytes 3080 | tf_op jit(solution)/shard_map/ppermute | solution.py:380
  43.2 0.0 collective-permute-done.14.refs_9_
  43.3 0.3 collective-permute-start.17
  43.6 1.7 %collective-permute-done.7 = f32[256]{0:T(256)S(1)} collective-permute-done((f32[256]{0:T(256)S(1)}, f32[256]{0:T(256)S(1)}, u32[]{:S(2)}, u32[]{:S(2)}) %collective-permute-start.7) | collective-permute-done | bytes 1056 | tf_op jit(solution)/shard_map/ppermute | solution.py:380
  45.3 0.0 collective-permute-done.12.refs_6_
  45.3 3.6 %wave.5 = (f32[1024,256]{1,0:T(8,128)S(1)}, f32[1024,128]{1,0:T(8,128)S(1)}) custom-call(bf16[768,128]{1,0:T(8,128)(2,1)S(1)} %copy-done, bf16[768,128]{1,0:T(8,128)(2,1)S(1)} %collective-permute-done.1.refs_1_.refs_5_, bf16[768,128]{1,0:T(8,128)(2,1)S(1)} %collective-permute-done.2.refs_2_.refs_6_, ...), custom_call_target="tpu_custom_call" | custom-call | flops 1024 | bytes 1024 | tf_op jit(solution)/shard_map/wave/pallas_call | solution.py:265
  48.8 3.0 %collective-permute-done.11.refs_4_ = bf16[1536,128]{1,0:T(8,128)(2,1)S(1)} collective-permute-done((bf16[1536,128]{1,0:T(8,128)(2,1)S(1)}, bf16[1536,128]{1,0:T(8,128)(2,1)S(1)}, u32[]{:S(2)}, u32[]{:S(2)}) %collective-permute-start.11) | collective-permute-done | bytes 393248 | tf_op jit(solution)/shard_map/ppermute | solution.py:50
  51.8 0.0 collective-permute-done.15.refs_5_
  51.8 0.1 collective-permute-start.16
  51.9 1.4 %collective-permute-start.9 = (f32[256]{0:T(256)S(1)}, f32[256]{0:T(256)S(1)}, u32[]{:S(2)}, u32[]{:S(2)}) collective-permute-start(f32[256]{0:T(256)S(1)} %add.17), channel_id=1, source_target_pairs={{0,4},{1,5},{2,6},{3,7},{4,0},{5,1},{6,2},{7,3},{8,12},{9,13},{10,... | collective-permute-start | bytes 3080 | tf_op jit(solution)/shard_map/ppermute | solution.py:380
  53.3 0.0 collective-permute-done.17.refs_4_
  53.3 1.8 %wave.6 = (f32[1024,256]{1,0:T(8,128)S(1)}, f32[1024,128]{1,0:T(8,128)S(1)}) custom-call(bf16[768,128]{1,0:T(8,128)(2,1)S(1)} %copy-done, bf16[768,128]{1,0:T(8,128)(2,1)S(1)} %collective-permute-done.1.refs_1_.refs_5_, bf16[768,128]{1,0:T(8,128)(2,1)S(1)} %collective-permute-done.2.refs_2_.refs_6_, ...), custom_call_target="tpu_custom_call" | custom-call | flops 1024 | bytes 1024 | tf_op jit(solution)/shard_map/wave/pallas_call | solution.py:265
  55.1 0.0 collective-permute-done.16.refs_6_
  55.1 0.0 copy-start.7
  55.2 0.0 copy-start.9
  55.2 3.0 %wave.7 = (bf16[256,128]{1,0:T(8,128)(2,1)S(1)}, bf16[256,128]{1,0:T(8,128)(2,1)S(1)}, bf16[256,128]{1,0:T(8,128)(2,1)S(1)}, bf16[256,128]{1,0:T(8,128)(2,1)S(1)}) custom-call(bf16[768,128]{1,0:T(8,128)(2,1)S(1)} %copy-done, bf16[768,128]{1,0:T(8,128)(2,1)S(1)} %collective-permute-done.1.refs_1_.refs_5_, ...), custom_call_target="tpu_custom_call" | custom-call | flops 1024 | bytes 1024 | tf_op jit(solution)/shard_map/wave/pallas_call | solution.py:265
  58.2 2.9 %collective-permute-start.18 = (bf16[256,128]{1,0:T(8,128)(2,1)S(1)}, bf16[256,128]{1,0:T(8,128)(2,1)S(1)}, u32[]{:S(2)}, u32[]{:S(2)}) collective-permute-start(bf16[256,128]{1,0:T(8,128)(2,1)S(1)} %get-tuple-element.68), channel_id=1, source_target_pairs={{112,0},{120,8},{32,16},{40,24},{16,32},{24,40},{64,48},{72,56},{4... | collective-permute-start | bytes 196616 | tf_op jit(solution)/shard_map/ppermute | solution.py:54
  61.2 0.2 collective-permute-start.19
  61.3 2.6 %collective-permute-start.20 = (bf16[256,128]{1,0:T(8,128)(2,1)S(1)}, bf16[256,128]{1,0:T(8,128)(2,1)S(1)}, u32[]{:S(2)}, u32[]{:S(2)}) collective-permute-start(bf16[256,128]{1,0:T(8,128)(2,1)S(1)} %get-tuple-element.70), channel_id=1, source_target_pairs={{80,0},{88,8},{64,16},{72,24},{112,32},{120,40},{96,48},{104,56},{... | collective-permute-start | bytes 196616 | tf_op jit(solution)/shard_map/ppermute | solution.py:54
  63.9 0.0 collective-permute-done.9
  63.9 1.0 %multiply_convert_fusion = bf16[256,1024]{1,0:T(8,128)(2,1)} fusion(bf16[256,1024]{1,0:T(8,128)(2,1)S(1)} %copy-done.7, f32[1024]{0:T(1024)S(1)} %copy-done.9, f32[256]{0:T(256)S(1)} %add_rsqrt_fusion), kind=kLoop, calls=%fused_computation | loop fusion | flops 1048576 | bytes 1053696 | tf_op jit(solution)/shard_map/convert_element_type | solution.py:476
  64.9 0.0 collective-permute-done.18.o1
  64.9 1.7 %collective-permute-done.19.o2 = bf16[256,128]{1,0:T(8,128)(2,1)S(1)} collective-permute-done((bf16[256,128]{1,0:T(8,128)(2,1)S(1)}, bf16[256,128]{1,0:T(8,128)(2,1)S(1)}, u32[]{:S(2)}, u32[]{:S(2)}) %collective-permute-start.19) | collective-permute-done | bytes 65568 | tf_op jit(solution)/shard_map/ppermute | solution.py:54
  66.6 2.3 %collective-permute-done.20.o3 = bf16[256,128]{1,0:T(8,128)(2,1)S(1)} collective-permute-done((bf16[256,128]{1,0:T(8,128)(2,1)S(1)}, bf16[256,128]{1,0:T(8,128)(2,1)S(1)}, u32[]{:S(2)}, u32[]{:S(2)}) %collective-permute-start.20) | collective-permute-done | bytes 65568 | tf_op jit(solution)/shard_map/ppermute | solution.py:54
  68.9 0.8 %unpack.1 = bf16[256,512]{1,0:T(8,128)(2,1)} custom-call(bf16[256,128]{1,0:T(8,128)(2,1)S(1)} %get-tuple-element.66.o0, bf16[256,128]{1,0:T(8,128)(2,1)S(1)} %collective-permute-done.18.o1, bf16[256,128]{1,0:T(8,128)(2,1)S(1)} %collective-permute-done.19.o2, bf16[256,128]{1,0:T(8,128)(2,1)S(1)} %collective-permute-done.20.o3), custom_call_target="tpu_custom_call" | custom-call | tf_op jit(solution)/shard_map/unpack/pallas_call | solution.py:145
  (21 shorter events, 0.3 us)
Async XLA Ops:
  2.5 15.3 %collective-permute-start.1 = (bf16[768,128]{1,0:T(8,128)(2,1)}, bf16[768,128]{1,0:T(8,128)(2,1)S(1)}, u32[]{:S(2)}, u32[]{:S(2)}) collective-permute-start(bf16[768,128]{1,0:T(8,128)(2,1)} %get-tuple-element.37), channel_id=1, source_target_pairs={{0,112},{8,120},{16,32},{24,40},{32,16},{40,24},{48,64},{56,72},{6... | collective-permute-start | bytes 589832 | tf_op jit(solution)/shard_map/ppermute | solution.py:50
  8.4 9.3 %collective-permute-start.2 = (bf16[768,128]{1,0:T(8,128)(2,1)}, bf16[768,128]{1,0:T(8,128)(2,1)S(1)}, u32[]{:S(2)}, u32[]{:S(2)}) collective-permute-start(bf16[768,128]{1,0:T(8,128)(2,1)} %get-tuple-element.46), channel_id=1, source_target_pairs={{0,32},{8,40},{16,112},{24,120},{32,64},{40,72},{48,16},{56,24},{6... | collective-permute-start | bytes 589832 | tf_op jit(solution)/shard_map/ppermute | solution.py:50
  10.8 13.3 %copy-start.8 = (bf16[512,128]{1,0:T(8,128)(2,1)S(1)}, bf16[512,128]{1,0:T(8,128)(2,1)}, u32[]{:S(2)}) copy-start(bf16[512,128]{1,0:T(8,128)(2,1)} %get-tuple-element.47) | copy-start | bytes 393220
  10.8 8.7 %collective-permute-start.4 = (bf16[512,128]{1,0:T(8,128)(2,1)}, bf16[512,128]{1,0:T(8,128)(2,1)S(1)}, u32[]{:S(2)}, u32[]{:S(2)}) collective-permute-start(bf16[512,128]{1,0:T(8,128)(2,1)} %get-tuple-element.47), channel_id=1, source_target_pairs={{0,128},{8,136},{16,144},{24,152},{32,160},{40,168},{48,176},{56,1... | collective-permute-start | bytes 393224 | tf_op jit(solution)/shard_map/ppermute | solution.py:50
  12.2 7.3 %collective-permute-start.3 = (bf16[512,128]{1,0:T(8,128)(2,1)}, bf16[512,128]{1,0:T(8,128)(2,1)S(1)}, u32[]{:S(2)}, u32[]{:S(2)}) collective-permute-start(bf16[512,128]{1,0:T(8,128)(2,1)} %get-tuple-element.47), channel_id=1, source_target_pairs={{0,16},{8,24},{16,0},{24,8},{32,48},{40,56},{48,32},{56,40},{64,80... | collective-permute-start | bytes 393224 | tf_op jit(solution)/shard_map/ppermute | solution.py:50
  13.9 11.7 %collective-permute-start = (bf16[128,1024]{1,0:T(8,128)(2,1)}, bf16[128,1024]{1,0:T(8,128)(2,1)S(1)}, u32[]{:S(2)}, u32[]{:S(2)}) collective-permute-start(bf16[128,1024]{1,0:T(8,128)(2,1)} %get-tuple-element.45), channel_id=1, source_target_pairs={{0,8},{8,16},{16,24},{24,32},{32,40},{40,48},{48,56},{56,64},{64,7... | collective-permute-start | bytes 786440 | tf_op jit(solution)/shard_map/ppermute | solution.py:50
  17.7 7.8 %copy-start.6 = (bf16[1024,128]{1,0:T(8,128)(2,1)S(1)}, bf16[1024,128]{1,0:T(8,128)(2,1)}, u32[]{:S(2)}) copy-start(bf16[1024,128]{1,0:T(8,128)(2,1)} %taps_ref) | copy-start | bytes 786436
  17.8 7.8 %copy-start.5 = (bf16[384,512]{1,0:T(8,128)(2,1)S(1)}, bf16[384,512]{1,0:T(8,128)(2,1)}, u32[]{:S(2)}) copy-start(bf16[384,512]{1,0:T(8,128)(2,1)} %constant.7.clone.matrix_ref) | copy-start | bytes 1179652
  17.8 7.8 %copy-start.4 = (bf16[256,1024]{1,0:T(8,128)(2,1)S(1)}, bf16[256,1024]{1,0:T(8,128)(2,1)}, u32[]{:S(2)}) copy-start(bf16[256,1024]{1,0:T(8,128)(2,1)} %res_ref) | copy-start | bytes 1572868
  17.8 7.8 %copy-start.1 = (bf16[256,1024]{1,0:T(8,128)(2,1)S(1)}, bf16[256,1024]{1,0:T(8,128)(2,1)}, u32[]{:S(2)}) copy-start(bf16[256,1024]{1,0:T(8,128)(2,1)} %key_ref.2) | copy-start | bytes 1572868
  17.8 7.8 %copy-start.2 = (bf16[256,1024]{1,0:T(8,128)(2,1)S(1)}, bf16[256,1024]{1,0:T(8,128)(2,1)}, u32[]{:S(2)}) copy-start(bf16[256,1024]{1,0:T(8,128)(2,1)} %value_ref.2) | copy-start | bytes 1572868
  17.9 7.8 %copy-start.3 = (bf16[256,1024]{1,0:T(8,128)(2,1)S(1)}, bf16[256,1024]{1,0:T(8,128)(2,1)}, u32[]{:S(2)}) copy-start(bf16[256,1024]{1,0:T(8,128)(2,1)} %gate_ref) | copy-start | bytes 1572868
  19.5 11.6 %collective-permute-start.6 = (bf16[768,128]{1,0:T(8,128)(2,1)}, bf16[768,128]{1,0:T(8,128)(2,1)S(1)}, u32[]{:S(2)}, u32[]{:S(2)}) collective-permute-start(bf16[768,128]{1,0:T(8,128)(2,1)} %get-tuple-element.53), channel_id=1, source_target_pairs={{0,80},{8,88},{16,64},{24,72},{32,112},{40,120},{48,96},{56,104},{... | collective-permute-start | bytes 589832 | tf_op jit(solution)/shard_map/ppermute | solution.py:50
  24.1 9.8 %collective-permute-start.10 = (bf16[1024,128]{1,0:T(8,128)(2,1)S(1)}, bf16[1024,128]{1,0:T(8,128)(2,1)S(1)}, u32[]{:S(2)}, u32[]{:S(2)}) collective-permute-start(bf16[1024,128]{1,0:T(8,128)(2,1)S(1)} %pad_maximum_fusion.4), channel_id=1, source_target_pairs={{0,16},{8,24},{16,0},{24,8},{32,48},{40,56},{48,32},{56,40},{64,80... | collective-permute-start | bytes 786440 | tf_op jit(solution)/shard_map/ppermute | solution.py:50
  24.1 11.3 %collective-permute-start.8 = (bf16[2048,128]{1,0:T(8,128)(2,1)S(1)}, bf16[2048,128]{1,0:T(8,128)(2,1)S(1)}, u32[]{:S(2)}, u32[]{:S(2)}) collective-permute-start(bf16[2048,128]{1,0:T(8,128)(2,1)S(1)} %pad_maximum_fusion.1), channel_id=1, source_target_pairs={{0,8},{8,0},{16,24},{24,16},{32,40},{40,32},{48,56},{56,48},{64,72... | collective-permute-start | bytes 1572872 | tf_op jit(solution)/shard_map/ppermute | solution.py:50
  24.3 19.0 %collective-permute-start.14 = (bf16[1536,128]{1,0:T(8,128)(2,1)S(1)}, bf16[1536,128]{1,0:T(8,128)(2,1)S(1)}, u32[]{:S(2)}, u32[]{:S(2)}) collective-permute-start(bf16[1536,128]{1,0:T(8,128)(2,1)S(1)} %pad_maximum_fusion.3), channel_id=1, source_target_pairs={{0,128},{8,136},{16,144},{24,152},{32,160},{40,168},{48,176},{56,1... | collective-permute-start | bytes 1179656 | tf_op jit(solution)/shard_map/ppermute | solution.py:50
  29.5 7.2 %copy-start = (bf16[768,128]{1,0:T(8,128)(2,1)S(1)}, bf16[768,128]{1,0:T(8,128)(2,1)}, u32[]{:S(2)}) copy-start(bf16[768,128]{1,0:T(8,128)(2,1)} %get-tuple-element.39.refs_0_.refs_4_) | copy-start | bytes 589828
  29.5 4.5 %collective-permute-start.5 = (f32[256]{0:T(256)S(1)}, f32[256]{0:T(256)S(1)}, u32[]{:S(2)}, u32[]{:S(2)}) collective-permute-start(f32[256]{0:T(256)S(1)} %bitcast.1), channel_id=1, source_target_pairs={{0,1},{1,0},{2,3},{3,2},{4,5},{5,4},{6,7},{7,6},{8,9},{9,8},{10,11... | collective-permute-start | bytes 3080 | tf_op jit(solution)/shard_map/ppermute | solution.py:380
  31.1 8.8 %collective-permute-start.13 = (bf16[512,128]{1,0:T(8,128)(2,1)S(1)}, bf16[512,128]{1,0:T(8,128)(2,1)S(1)}, u32[]{:S(2)}, u32[]{:S(2)}) collective-permute-start(bf16[512,128]{1,0:T(8,128)(2,1)S(1)} %slice.18), channel_id=1, source_target_pairs={{0,16},{8,24},{16,0},{24,8},{32,48},{40,56},{48,32},{56,40},{64,80... | collective-permute-start | bytes 393224 | tf_op jit(solution)/shard_map/ppermute | solution.py:50
  34.0 11.3 %collective-permute-start.12 = (bf16[1536,128]{1,0:T(8,128)(2,1)S(1)}, bf16[1536,128]{1,0:T(8,128)(2,1)S(1)}, u32[]{:S(2)}, u32[]{:S(2)}) collective-permute-start(bf16[1536,128]{1,0:T(8,128)(2,1)S(1)} %constant_dynamic-update-slice_fusion), channel_id=1, source_target_pairs={{0,8},{8,0},{16,24},{24,16},{32,40},{40,32},{48,56},{56,48},{64,72... | collective-permute-start | bytes 1179656 | tf_op jit(solution)/shard_map/ppermute | solution.py:50
  34.1 17.7 %collective-permute-start.11 = (bf16[1536,128]{1,0:T(8,128)(2,1)S(1)}, bf16[1536,128]{1,0:T(8,128)(2,1)S(1)}, u32[]{:S(2)}, u32[]{:S(2)}) collective-permute-start(bf16[1536,128]{1,0:T(8,128)(2,1)S(1)} %constant_dynamic-update-slice_fusion), channel_id=1, source_target_pairs={{0,128},{8,136},{16,144},{24,152},{32,160},{40,168},{48,176},{56,1... | collective-permute-start | bytes 1179656 | tf_op jit(solution)/shard_map/ppermute | solution.py:50
  35.4 16.4 %collective-permute-start.15 = (bf16[512,128]{1,0:T(8,128)(2,1)S(1)}, bf16[512,128]{1,0:T(8,128)(2,1)S(1)}, u32[]{:S(2)}, u32[]{:S(2)}) collective-permute-start(bf16[512,128]{1,0:T(8,128)(2,1)S(1)} %slice.18), channel_id=1, source_target_pairs={{0,144},{8,152},{16,128},{24,136},{32,176},{40,184},{48,160},{56,1... | collective-permute-start | bytes 393224 | tf_op jit(solution)/shard_map/ppermute | solution.py:50
  39.9 5.3 %collective-permute-start.7 = (f32[256]{0:T(256)S(1)}, f32[256]{0:T(256)S(1)}, u32[]{:S(2)}, u32[]{:S(2)}) collective-permute-start(f32[256]{0:T(256)S(1)} %add.16), channel_id=1, source_target_pairs={{0,2},{1,3},{2,0},{3,1},{4,6},{5,7},{6,4},{7,5},{8,10},{9,11},{10,... | collective-permute-start | bytes 3080 | tf_op jit(solution)/shard_map/ppermute | solution.py:380
  43.3 10.0 %collective-permute-start.17 = (bf16[2560,128]{1,0:T(8,128)(2,1)S(1)}, bf16[2560,128]{1,0:T(8,128)(2,1)S(1)}, u32[]{:S(2)}, u32[]{:S(2)}) collective-permute-start(bf16[2560,128]{1,0:T(8,128)(2,1)S(1)} %pad_maximum_fusion), channel_id=1, source_target_pairs={{0,8},{8,0},{16,24},{24,16},{32,40},{40,32},{48,56},{56,48},{64,72... | collective-permute-start | bytes 1966088 | tf_op jit(solution)/shard_map/ppermute | solution.py:50
  51.8 3.3 %collective-permute-start.16 = (bf16[2048,128]{1,0:T(8,128)(2,1)S(1)}, bf16[2048,128]{1,0:T(8,128)(2,1)S(1)}, u32[]{:S(2)}, u32[]{:S(2)}) collective-permute-start(bf16[2048,128]{1,0:T(8,128)(2,1)S(1)} %pad_maximum_fusion.2), channel_id=1, source_target_pairs={{0,8},{8,0},{16,24},{24,16},{32,40},{40,32},{48,56},{56,48},{64,72... | collective-permute-start | bytes 1572872 | tf_op jit(solution)/shard_map/ppermute | solution.py:50
  51.9 12.0 %collective-permute-start.9 = (f32[256]{0:T(256)S(1)}, f32[256]{0:T(256)S(1)}, u32[]{:S(2)}, u32[]{:S(2)}) collective-permute-start(f32[256]{0:T(256)S(1)} %add.17), channel_id=1, source_target_pairs={{0,4},{1,5},{2,6},{3,7},{4,0},{5,1},{6,2},{7,3},{8,12},{9,13},{10,... | collective-permute-start | bytes 3080 | tf_op jit(solution)/shard_map/ppermute | solution.py:380
  55.1 8.8 %copy-start.7 = (bf16[256,1024]{1,0:T(8,128)(2,1)S(1)}, bf16[256,1024]{1,0:T(8,128)(2,1)}, u32[]{:S(2)}) copy-start(bf16[256,1024]{1,0:T(8,128)(2,1)} %get-tuple-element.34) | copy-start | bytes 1572868
  55.2 8.8 %copy-start.9 = (f32[1024]{0:T(1024)S(1)}, f32[1024]{0:T(1024)}, u32[]{:S(2)}) copy-start(f32[1024]{0:T(1024)} %param.15) | copy-start | bytes 12292
  58.2 6.7 %collective-permute-start.18 = (bf16[256,128]{1,0:T(8,128)(2,1)S(1)}, bf16[256,128]{1,0:T(8,128)(2,1)S(1)}, u32[]{:S(2)}, u32[]{:S(2)}) collective-permute-start(bf16[256,128]{1,0:T(8,128)(2,1)S(1)} %get-tuple-element.68), channel_id=1, source_target_pairs={{112,0},{120,8},{32,16},{40,24},{16,32},{24,40},{64,48},{72,56},{4... | collective-permute-start | bytes 196616 | tf_op jit(solution)/shard_map/ppermute | solution.py:54
  61.2 5.5 %collective-permute-start.19 = (bf16[256,128]{1,0:T(8,128)(2,1)S(1)}, bf16[256,128]{1,0:T(8,128)(2,1)S(1)}, u32[]{:S(2)}, u32[]{:S(2)}) collective-permute-start(bf16[256,128]{1,0:T(8,128)(2,1)S(1)} %get-tuple-element.69), channel_id=1, source_target_pairs={{32,0},{40,8},{112,16},{120,24},{64,32},{72,40},{16,48},{24,56},{9... | collective-permute-start | bytes 196616 | tf_op jit(solution)/shard_map/ppermute | solution.py:54
  61.3 7.6 %collective-permute-start.20 = (bf16[256,128]{1,0:T(8,128)(2,1)S(1)}, bf16[256,128]{1,0:T(8,128)(2,1)S(1)}, u32[]{:S(2)}, u32[]{:S(2)}) collective-permute-start(bf16[256,128]{1,0:T(8,128)(2,1)S(1)} %get-tuple-element.70), channel_id=1, source_target_pairs={{80,0},{88,8},{64,16},{72,24},{112,32},{120,40},{96,48},{104,56},{... | collective-permute-start | bytes 196616 | tf_op jit(solution)/shard_map/ppermute | solution.py:54

commit v5 on v4

--- a/solution.py
+++ b/solution.py
@@ -330,33 +330,33 @@
         return lax.dot_general(a, b, (((1,), (1,)), ((), ())), preferred_element_type=F32)
 
     half = SPAN // 2
-    fh, fl = matrix_ref[:SPAN, :SPAN], matrix_ref[:SPAN, SPAN:]
-    gh, gl = matrix_ref[SPAN:, :SPAN], matrix_ref[SPAN:, SPAN:]
-    ones = jnp.ones((8, tile), BF16)
-    squares = jnp.zeros((8, ROWS), F32)
+    forward, inverse = matrix_ref[:SPAN, :], matrix_ref[SPAN:, :]
+    on_taps = jnp.concatenate([forward[:, :TAPS], forward[:, SPAN : SPAN + TAPS]], axis=1)
+    squares = jnp.zeros((ROWS, tile), F32)
     for first in range(0, key_ref.shape[1], tile):
         columns = slice(first, first + tile)
         gated = (key_ref[:, columns].astype(F32) * value_ref[:, columns].astype(F32)).astype(BF16)
         x = jnp.concatenate(
             [jnp.concatenate([halo_ref[:, columns], gated[:TAPS]], axis=0), gated], axis=1
         )
-        spectrum = dot(fh, x) + dot(fl, x)
+        spectrum = dot(forward, jnp.concatenate([x, x], axis=0))
         taps = taps_ref[columns, :]
-        weight = dot_t(fh[:, :TAPS], taps) + dot_t(fl[:, :TAPS], taps)
+        weight = dot_t(on_taps, jnp.concatenate([taps, taps], axis=1))
         xc, xs = spectrum[:half], spectrum[half:]
         wc, ws = [jnp.concatenate([w, w], axis=1) for w in (weight[:half], weight[half:])]
         both = jnp.concatenate([xc * wc - xs * ws, xc * ws + xs * wc], axis=0)
         top, low = split(both)
-        filtered = dot(gh, top) + dot(gh, low) + dot(gl, top)
+        filtered = dot(inverse, jnp.concatenate([top, top], axis=0)) + dot(inverse[:, :SPAN], low)
         filtered = jnp.concatenate([filtered[:, :tile], filtered[:, tile:]], axis=0)
         out = (
             res_ref[:, columns].astype(F32) + gate_ref[:, columns].astype(F32) * filtered
         ).astype(BF16)
         out_ref[:, columns] = out
         wide = out.astype(F32)
-        s_top, s_low = split(wide * wide)
-        squares = squares + dot_t(ones, s_top) + dot_t(ones, s_low)
-    squares_ref[...] = squares
+        squares = squares + wide * wide
+    top, low = split(squares)
+    ones = jnp.ones((8, tile), BF16)
+    squares_ref[...] = dot_t(ones, top) + dot_t(ones, low)
 
 
 def filter_block(gate, key, value, filters, residual, halo):
@@ -436,7 +436,6 @@
     )
     far3 = tie(far3, state[1])
     core3 = send(jnp.concatenate([far3, low0, low12]), CORE)
-    total = swap_sum(total, 2, state[1])
     state = wave(
         got,
         [got[3], far12, tie(core2, total), far3, low0, low12],
@@ -448,7 +447,8 @@
         + group(5, first[1:], True, False),
         state,
     )
-    low3 = tie(low3, state[1])
+    total = swap_sum(total, 2, state[1])
+    low3 = tie(low3, state[1], total)
     core4 = send(jnp.concatenate([low3, low4]), CORE)
     state = wave(
         got,

time: 70.4 us -> 70.4 us (level)
  Pallas kernels: 20.5 us -> 19.6 us
  waiting for transfers between devices: 12.4 us -> 13.2 us
    ppermute x15, waiting for transfers between devices: 6.64 us -> 9.18 us  [send(): return lax.ppermute(x, 'context', where)]
    ppermute x3, waiting for transfers between devices: 1.72 us -> 0.01 us  [swap_sum(): lax.ppermute(x, 'tensor', [(i, i ^ bit) for i in range(8)])]
    pallas_call x1, Pallas kernels: 3.91 us -> 3.06 us  [filter_block(): pl.pallas_call(functools.partial(filter_kernel, 256), out_shape=[jax.Shap...]
  transfers between devices with their start and end apart: 21 -> 21, of which waited for: 7 -> 6; matrix products, arithmetic and copies ran while one was open for 2% -> 2% of each run, Pallas kernels for 26% -> 24%
where the time goes in v5:
time: 70.4 us; the launch traced here: 69.7 us
  starting transfers between devices  34.6 us (49%)
  Pallas kernels  19.6 us (28%)
  waiting for transfers between devices  13.2 us (19%)
  other arithmetic  1.16 us (2%)
  between operations  1.03 us (1%)
    ppermute x15, starting transfers between devices, send(): return lax.ppermute(x, 'context', where)  22.9 us
    pallas_call x4, Pallas kernels, wave(): pl.pallas_call(functools.partial(wave_kernel, blocks, first, last, len(ar...  11.6 us
    ppermute x15, waiting for transfers between devices, send(): return lax.ppermute(x, 'context', where)  9.18 us
    ppermute x3, starting transfers between devices, swap_sum(): lax.ppermute(x, 'tensor', [(i, i ^ bit) for i in range(8)])  5.98 us
    ppermute x3, starting transfers between devices, back(): return lax.ppermute(x, 'context', [(b, a) for a, b in where])  5.69 us
    ppermute x3, waiting for transfers between devices, back(): return lax.ppermute(x, 'context', [(b, a) for a, b in where])  4.03 us
    pallas_call x1, Pallas kernels, filter_block(): pl.pallas_call(functools.partial(filter_kernel, 256), out_shape=[jax.Shap...  3.06 us
    pallas_call x1, Pallas kernels, pack_rest(): pl.pallas_call(pack_rest_kernel, out_shape=[jax.ShapeDtypeStruct((TAPS, c...  2.36 us
  transfers between devices with their start and end apart: 21, of which 6 were waited for; matrix products, arithmetic and copies ran while one was open for 2% of the time, Pallas kernels for 24%

profile of v5, /device:TPU:16, one launch (start us, length us, event | category | flops | bytes accessed | tf_op | source)
XLA Modules:
  0.0 69.7 jit_solution(2652679793908794142)
XLA Ops:
  0.6 1.8 %pack.1 = (bf16[768,128]{1,0:T(8,128)(2,1)}, bf16[768,128]{1,0:T(8,128)(2,1)}) custom-call(bf16[256,512]{1,0:T(8,128)(2,1)} %q_ref.2, bf16[256,512]{1,0:T(8,128)(2,1)} %k_ref.3, bf16[256,512]{1,0:T(8,128)(2,1)} %v_ref.3), custom_call_target="tpu_custom_call" | custom-call | tf_op jit(solution)/shard_map/pack/pallas_call | solution.py:111
  2.5 5.9 %collective-permute-start.1 = (bf16[768,128]{1,0:T(8,128)(2,1)}, bf16[768,128]{1,0:T(8,128)(2,1)S(1)}, u32[]{:S(2)}, u32[]{:S(2)}) collective-permute-start(bf16[768,128]{1,0:T(8,128)(2,1)} %get-tuple-element.37), channel_id=1, source_target_pairs={{0,112},{8,120},{16,32},{24,40},{32,16},{40,24},{48,64},{56,72},{6... | collective-permute-start | bytes 589832 | tf_op jit(solution)/shard_map/ppermute | solution.py:50
  8.4 0.0 collective-permute-start.2
  8.4 2.4 %pack_rest.1 = (bf16[128,1024]{1,0:T(8,128)(2,1)}, bf16[768,128]{1,0:T(8,128)(2,1)}, bf16[768,128]{1,0:T(8,128)(2,1)}, bf16[512,128]{1,0:T(8,128)(2,1)}) custom-call(bf16[256,512]{1,0:T(8,128)(2,1)} %q_ref.2, bf16[256,512]{1,0:T(8,128)(2,1)} %k_ref.3, bf16[256,512]{1,0:T(8,128)(2,1)} %v_ref.3, bf16[256,1024]{1,0:T(8,128)(2,1)} %key_ref.2, ...), custom_call_target="tpu_custom_call" | custom-call | tf_op jit(solution)/shard_map/pack_rest/pallas_call | solution.py:124
  10.8 0.0 copy-start.8
  10.8 1.4 %collective-permute-start.4 = (bf16[512,128]{1,0:T(8,128)(2,1)}, bf16[512,128]{1,0:T(8,128)(2,1)S(1)}, u32[]{:S(2)}, u32[]{:S(2)}) collective-permute-start(bf16[512,128]{1,0:T(8,128)(2,1)} %get-tuple-element.47), channel_id=1, source_target_pairs={{0,128},{8,136},{16,144},{24,152},{32,160},{40,168},{48,176},{56,1... | collective-permute-start | bytes 393224 | tf_op jit(solution)/shard_map/ppermute | solution.py:50
  12.2 1.6 %collective-permute-start.3 = (bf16[512,128]{1,0:T(8,128)(2,1)}, bf16[512,128]{1,0:T(8,128)(2,1)S(1)}, u32[]{:S(2)}, u32[]{:S(2)}) collective-permute-start(bf16[512,128]{1,0:T(8,128)(2,1)} %get-tuple-element.47), channel_id=1, source_target_pairs={{0,16},{8,24},{16,0},{24,8},{32,48},{40,56},{48,32},{56,40},{64,80... | collective-permute-start | bytes 393224 | tf_op jit(solution)/shard_map/ppermute | solution.py:50
  13.9 1.9 %collective-permute-start = (bf16[128,1024]{1,0:T(8,128)(2,1)}, bf16[128,1024]{1,0:T(8,128)(2,1)S(1)}, u32[]{:S(2)}, u32[]{:S(2)}) collective-permute-start(bf16[128,1024]{1,0:T(8,128)(2,1)} %get-tuple-element.45), channel_id=1, source_target_pairs={{0,8},{8,16},{16,24},{24,32},{32,40},{40,48},{48,56},{56,64},{64,7... | collective-permute-start | bytes 786440 | tf_op jit(solution)/shard_map/ppermute | solution.py:50
  15.8 2.0 %collective-permute-done.1.refs_1_.refs_5_ = bf16[768,128]{1,0:T(8,128)(2,1)S(1)} collective-permute-done((bf16[768,128]{1,0:T(8,128)(2,1)}, bf16[768,128]{1,0:T(8,128)(2,1)S(1)}, u32[]{:S(2)}, u32[]{:S(2)}) %collective-permute-start.1) | collective-permute-done | bytes 196640 | tf_op jit(solution)/shard_map/ppermute | solution.py:50
  17.8 0.0 collective-permute-done.2.refs_2_.refs_6_
  17.8 0.0 copy-start.5
  17.8 0.0 copy-start.4
  17.8 0.0 copy-start.1
  17.8 0.0 copy-start.2
  17.9 0.0 copy-start.3
  17.9 1.6 %collective-permute-done.4.refs_8_ = bf16[512,128]{1,0:T(8,128)(2,1)S(1)} collective-permute-done((bf16[512,128]{1,0:T(8,128)(2,1)}, bf16[512,128]{1,0:T(8,128)(2,1)S(1)}, u32[]{:S(2)}, u32[]{:S(2)}) %collective-permute-start.4) | collective-permute-done | bytes 131104 | tf_op jit(solution)/shard_map/ppermute | solution.py:50
  19.5 0.0 collective-permute-done.3.refs_7_
  19.5 4.6 %collective-permute-start.6 = (bf16[768,128]{1,0:T(8,128)(2,1)}, bf16[768,128]{1,0:T(8,128)(2,1)S(1)}, u32[]{:S(2)}, u32[]{:S(2)}) collective-permute-start(bf16[768,128]{1,0:T(8,128)(2,1)} %get-tuple-element.53), channel_id=1, source_target_pairs={{0,80},{8,88},{16,64},{24,72},{32,112},{40,120},{48,96},{56,104},{... | collective-permute-start | bytes 589832 | tf_op jit(solution)/shard_map/ppermute | solution.py:50
  24.1 0.0 collective-permute-start.8
  24.1 0.0 copy-done.8
  24.1 0.1 collective-permute-start.11
  24.3 1.3 %collective-permute-start.12 = (bf16[1536,128]{1,0:T(8,128)(2,1)S(1)}, bf16[1536,128]{1,0:T(8,128)(2,1)S(1)}, u32[]{:S(2)}, u32[]{:S(2)}) collective-permute-start(bf16[1536,128]{1,0:T(8,128)(2,1)S(1)} %pad_maximum_fusion.3), channel_id=1, source_target_pairs={{0,128},{8,136},{16,144},{24,152},{32,160},{40,168},{48,176},{56,1... | collective-permute-start | bytes 1179656 | tf_op jit(solution)/shard_map/ppermute | solution.py:50
  25.6 0.0 collective-permute-done.halo_ref
  25.6 0.0 copy-done.6
  25.6 0.0 copy-done.5
  25.6 0.0 copy-done.4
  25.6 3.1 %filter.1 = (bf16[256,1024]{1,0:T(8,128)(2,1)}, f32[8,256]{1,0:T(8,128)S(1)}) custom-call(bf16[384,512]{1,0:T(8,128)(2,1)S(1)} %copy-done.5, bf16[256,1024]{1,0:T(8,128)(2,1)S(1)} %copy-done.1, bf16[256,1024]{1,0:T(8,128)(2,1)S(1)} %copy-done.2, bf16[256,1024]{1,0:T(8,128)(2,1)S(1)} %copy-done.3, bf16[256,1024]{1,0:T(8,128)(2,1)S(1)} %copy-done.4, ...), custom_call_target="tpu_custom_call" | custom-call | flops 1024 | bytes 1024 | tf_op jit(solution)/shard_map/filter/pallas_call | solution.py:365
  28.7 1.5 %collective-permute-start.5 = (f32[256]{0:T(256)S(1)}, f32[256]{0:T(256)S(1)}, u32[]{:S(2)}, u32[]{:S(2)}) collective-permute-start(f32[256]{0:T(256)S(1)} %bitcast.1), channel_id=1, source_target_pairs={{0,1},{1,0},{2,3},{3,2},{4,5},{5,4},{6,7},{7,6},{8,9},{9,8},{10,11... | collective-permute-start | bytes 3080 | tf_op jit(solution)/shard_map/ppermute | solution.py:380
  30.2 0.9 %collective-permute-done.6.refs_3_.refs_4_ = bf16[768,128]{1,0:T(8,128)(2,1)S(1)} collective-permute-done((bf16[768,128]{1,0:T(8,128)(2,1)}, bf16[768,128]{1,0:T(8,128)(2,1)S(1)}, u32[]{:S(2)}, u32[]{:S(2)}) %collective-permute-start.6) | collective-permute-done | bytes 196640 | tf_op jit(solution)/shard_map/ppermute | solution.py:50
  31.1 2.8 %collective-permute-start.10 = (bf16[512,128]{1,0:T(8,128)(2,1)S(1)}, bf16[512,128]{1,0:T(8,128)(2,1)S(1)}, u32[]{:S(2)}, u32[]{:S(2)}) collective-permute-start(bf16[512,128]{1,0:T(8,128)(2,1)S(1)} %slice.18), channel_id=1, source_target_pairs={{0,16},{8,24},{16,0},{24,8},{32,48},{40,56},{48,32},{56,40},{64,80... | collective-permute-start | bytes 393224 | tf_op jit(solution)/shard_map/ppermute | solution.py:50
  33.9 0.0 collective-permute-done.8.refs_5_
  34.0 0.1 collective-permute-start.9
  34.1 0.0 collective-permute-done.5
  34.1 1.3 %collective-permute-start.14 = (bf16[1536,128]{1,0:T(8,128)(2,1)S(1)}, bf16[1536,128]{1,0:T(8,128)(2,1)S(1)}, u32[]{:S(2)}, u32[]{:S(2)}) collective-permute-start(bf16[1536,128]{1,0:T(8,128)(2,1)S(1)} %constant_dynamic-update-slice_fusion), channel_id=1, source_target_pairs={{0,128},{8,136},{16,144},{24,152},{32,160},{40,168},{48,176},{56,1... | collective-permute-start | bytes 1179656 | tf_op jit(solution)/shard_map/ppermute | solution.py:50
  35.4 0.0 collective-permute-done.11.refs_8_
  35.4 1.3 %collective-permute-start.15 = (bf16[512,128]{1,0:T(8,128)(2,1)S(1)}, bf16[512,128]{1,0:T(8,128)(2,1)S(1)}, u32[]{:S(2)}, u32[]{:S(2)}) collective-permute-start(bf16[512,128]{1,0:T(8,128)(2,1)S(1)} %slice.18), channel_id=1, source_target_pairs={{0,144},{8,152},{16,128},{24,136},{32,176},{40,184},{48,160},{56,1... | collective-permute-start | bytes 393224 | tf_op jit(solution)/shard_map/ppermute | solution.py:50
  36.7 0.0 copy-done
  36.7 3.2 %wave.4 = (f32[1024,256]{1,0:T(8,128)S(1)}, f32[1024,128]{1,0:T(8,128)S(1)}) custom-call(bf16[768,128]{1,0:T(8,128)(2,1)S(1)} %copy-done, bf16[768,128]{1,0:T(8,128)(2,1)S(1)} %collective-permute-done.1.refs_1_.refs_5_, bf16[768,128]{1,0:T(8,128)(2,1)S(1)} %collective-permute-done.2.refs_2_.refs_6_, ...), custom_call_target="tpu_custom_call" | custom-call | flops 1024 | bytes 1024 | tf_op jit(solution)/shard_map/wave/pallas_call | solution.py:265
  39.9 0.0 collective-permute-done.10.refs_7_
  39.9 3.1 %collective-permute-start.7 = (f32[256]{0:T(256)S(1)}, f32[256]{0:T(256)S(1)}, u32[]{:S(2)}, u32[]{:S(2)}) collective-permute-start(f32[256]{0:T(256)S(1)} %add.16), channel_id=1, source_target_pairs={{0,2},{1,3},{2,0},{3,1},{4,6},{5,7},{6,4},{7,5},{8,10},{9,11},{10,... | collective-permute-start | bytes 3080 | tf_op jit(solution)/shard_map/ppermute | solution.py:380
  43.0 0.0 collective-permute-done.12.refs_9_
  43.1 0.5 collective-permute-start.17
  43.6 0.0 collective-permute-done.9.refs_6_
  43.6 3.6 %wave.5 = (f32[1024,256]{1,0:T(8,128)S(1)}, f32[1024,128]{1,0:T(8,128)S(1)}) custom-call(bf16[768,128]{1,0:T(8,128)(2,1)S(1)} %copy-done, bf16[768,128]{1,0:T(8,128)(2,1)S(1)} %collective-permute-done.1.refs_1_.refs_5_, bf16[768,128]{1,0:T(8,128)(2,1)S(1)} %collective-permute-done.2.refs_2_.refs_6_, ...), custom_call_target="tpu_custom_call" | custom-call | flops 1024 | bytes 1024 | tf_op jit(solution)/shard_map/wave/pallas_call | solution.py:265
  47.1 0.0 collective-permute-done.7
  47.1 4.7 %collective-permute-done.14.refs_4_ = bf16[1536,128]{1,0:T(8,128)(2,1)S(1)} collective-permute-done((bf16[1536,128]{1,0:T(8,128)(2,1)S(1)}, bf16[1536,128]{1,0:T(8,128)(2,1)S(1)}, u32[]{:S(2)}, u32[]{:S(2)}) %collective-permute-start.14) | collective-permute-done | bytes 393248 | tf_op jit(solution)/shard_map/ppermute | solution.py:50
  51.8 0.0 collective-permute-done.15.refs_5_
  51.8 0.1 collective-permute-start.16
  51.9 1.4 %collective-permute-start.13 = (f32[256]{0:T(256)S(1)}, f32[256]{0:T(256)S(1)}, u32[]{:S(2)}, u32[]{:S(2)}) collective-permute-start(f32[256]{0:T(256)S(1)} %add.17), channel_id=1, source_target_pairs={{0,4},{1,5},{2,6},{3,7},{4,0},{5,1},{6,2},{7,3},{8,12},{9,13},{10,... | collective-permute-start | bytes 3080 | tf_op jit(solution)/shard_map/ppermute | solution.py:380
  53.3 0.0 collective-permute-done.17.refs_4_
  53.3 1.8 %wave.6 = (f32[1024,256]{1,0:T(8,128)S(1)}, f32[1024,128]{1,0:T(8,128)S(1)}) custom-call(bf16[768,128]{1,0:T(8,128)(2,1)S(1)} %copy-done, bf16[768,128]{1,0:T(8,128)(2,1)S(1)} %collective-permute-done.1.refs_1_.refs_5_, bf16[768,128]{1,0:T(8,128)(2,1)S(1)} %collective-permute-done.2.refs_2_.refs_6_, ...), custom_call_target="tpu_custom_call" | custom-call | flops 1024 | bytes 1024 | tf_op jit(solution)/shard_map/wave/pallas_call | solution.py:265
  55.1 0.0 collective-permute-done.16.refs_6_
  55.1 0.0 copy-start.7
  55.2 0.0 copy-start.9
  55.2 3.0 %wave.7 = (bf16[256,128]{1,0:T(8,128)(2,1)S(1)}, bf16[256,128]{1,0:T(8,128)(2,1)S(1)}, bf16[256,128]{1,0:T(8,128)(2,1)S(1)}, bf16[256,128]{1,0:T(8,128)(2,1)S(1)}) custom-call(bf16[768,128]{1,0:T(8,128)(2,1)S(1)} %copy-done, bf16[768,128]{1,0:T(8,128)(2,1)S(1)} %collective-permute-done.1.refs_1_.refs_5_, ...), custom_call_target="tpu_custom_call" | custom-call | flops 1024 | bytes 1024 | tf_op jit(solution)/shard_map/wave/pallas_call | solution.py:265
  58.2 3.0 %collective-permute-start.18 = (bf16[256,128]{1,0:T(8,128)(2,1)S(1)}, bf16[256,128]{1,0:T(8,128)(2,1)S(1)}, u32[]{:S(2)}, u32[]{:S(2)}) collective-permute-start(bf16[256,128]{1,0:T(8,128)(2,1)S(1)} %get-tuple-element.68), channel_id=1, source_target_pairs={{112,0},{120,8},{32,16},{40,24},{16,32},{24,40},{64,48},{72,56},{4... | collective-permute-start | bytes 196616 | tf_op jit(solution)/shard_map/ppermute | solution.py:54
  61.2 0.1 collective-permute-start.19
  61.3 2.6 %collective-permute-start.20 = (bf16[256,128]{1,0:T(8,128)(2,1)S(1)}, bf16[256,128]{1,0:T(8,128)(2,1)S(1)}, u32[]{:S(2)}, u32[]{:S(2)}) collective-permute-start(bf16[256,128]{1,0:T(8,128)(2,1)S(1)} %get-tuple-element.70), channel_id=1, source_target_pairs={{80,0},{88,8},{64,16},{72,24},{112,32},{120,40},{96,48},{104,56},{... | collective-permute-start | bytes 196616 | tf_op jit(solution)/shard_map/ppermute | solution.py:54
  63.9 0.0 collective-permute-done.13
  63.9 1.0 %multiply_convert_fusion = bf16[256,1024]{1,0:T(8,128)(2,1)} fusion(bf16[256,1024]{1,0:T(8,128)(2,1)S(1)} %copy-done.7, f32[1024]{0:T(1024)S(1)} %copy-done.9, f32[256]{0:T(256)S(1)} %add_rsqrt_fusion), kind=kLoop, calls=%fused_computation | loop fusion | flops 1048576 | bytes 1053696 | tf_op jit(solution)/shard_map/convert_element_type | solution.py:476
  64.9 0.0 collective-permute-done.18.o1
  64.9 1.7 %collective-permute-done.19.o2 = bf16[256,128]{1,0:T(8,128)(2,1)S(1)} collective-permute-done((bf16[256,128]{1,0:T(8,128)(2,1)S(1)}, bf16[256,128]{1,0:T(8,128)(2,1)S(1)}, u32[]{:S(2)}, u32[]{:S(2)}) %collective-permute-start.19) | collective-permute-done | bytes 65568 | tf_op jit(solution)/shard_map/ppermute | solution.py:54
  66.6 2.3 %collective-permute-done.20.o3 = bf16[256,128]{1,0:T(8,128)(2,1)S(1)} collective-permute-done((bf16[256,128]{1,0:T(8,128)(2,1)S(1)}, bf16[256,128]{1,0:T(8,128)(2,1)S(1)}, u32[]{:S(2)}, u32[]{:S(2)}) %collective-permute-start.20) | collective-permute-done | bytes 65568 | tf_op jit(solution)/shard_map/ppermute | solution.py:54
  68.9 0.8 %unpack.1 = bf16[256,512]{1,0:T(8,128)(2,1)} custom-call(bf16[256,128]{1,0:T(8,128)(2,1)S(1)} %get-tuple-element.66.o0, bf16[256,128]{1,0:T(8,128)(2,1)S(1)} %collective-permute-done.18.o1, bf16[256,128]{1,0:T(8,128)(2,1)S(1)} %collective-permute-done.19.o2, bf16[256,128]{1,0:T(8,128)(2,1)S(1)} %collective-permute-done.20.o3), custom_call_target="tpu_custom_call" | custom-call | tf_op jit(solution)/shard_map/unpack/pallas_call | solution.py:145
  (21 shorter events, 0.3 us)
Async XLA Ops:
  2.5 15.3 %collective-permute-start.1 = (bf16[768,128]{1,0:T(8,128)(2,1)}, bf16[768,128]{1,0:T(8,128)(2,1)S(1)}, u32[]{:S(2)}, u32[]{:S(2)}) collective-permute-start(bf16[768,128]{1,0:T(8,128)(2,1)} %get-tuple-element.37), channel_id=1, source_target_pairs={{0,112},{8,120},{16,32},{24,40},{32,16},{40,24},{48,64},{56,72},{6... | collective-permute-start | bytes 589832 | tf_op jit(solution)/shard_map/ppermute | solution.py:50
  8.4 9.3 %collective-permute-start.2 = (bf16[768,128]{1,0:T(8,128)(2,1)}, bf16[768,128]{1,0:T(8,128)(2,1)S(1)}, u32[]{:S(2)}, u32[]{:S(2)}) collective-permute-start(bf16[768,128]{1,0:T(8,128)(2,1)} %get-tuple-element.46), channel_id=1, source_target_pairs={{0,32},{8,40},{16,112},{24,120},{32,64},{40,72},{48,16},{56,24},{6... | collective-permute-start | bytes 589832 | tf_op jit(solution)/shard_map/ppermute | solution.py:50
  10.8 13.3 %copy-start.8 = (bf16[512,128]{1,0:T(8,128)(2,1)S(1)}, bf16[512,128]{1,0:T(8,128)(2,1)}, u32[]{:S(2)}) copy-start(bf16[512,128]{1,0:T(8,128)(2,1)} %get-tuple-element.47) | copy-start | bytes 393220
  10.8 8.7 %collective-permute-start.4 = (bf16[512,128]{1,0:T(8,128)(2,1)}, bf16[512,128]{1,0:T(8,128)(2,1)S(1)}, u32[]{:S(2)}, u32[]{:S(2)}) collective-permute-start(bf16[512,128]{1,0:T(8,128)(2,1)} %get-tuple-element.47), channel_id=1, source_target_pairs={{0,128},{8,136},{16,144},{24,152},{32,160},{40,168},{48,176},{56,1... | collective-permute-start | bytes 393224 | tf_op jit(solution)/shard_map/ppermute | solution.py:50
  12.2 7.3 %collective-permute-start.3 = (bf16[512,128]{1,0:T(8,128)(2,1)}, bf16[512,128]{1,0:T(8,128)(2,1)S(1)}, u32[]{:S(2)}, u32[]{:S(2)}) collective-permute-start(bf16[512,128]{1,0:T(8,128)(2,1)} %get-tuple-element.47), channel_id=1, source_target_pairs={{0,16},{8,24},{16,0},{24,8},{32,48},{40,56},{48,32},{56,40},{64,80... | collective-permute-start | bytes 393224 | tf_op jit(solution)/shard_map/ppermute | solution.py:50
  13.9 11.7 %collective-permute-start = (bf16[128,1024]{1,0:T(8,128)(2,1)}, bf16[128,1024]{1,0:T(8,128)(2,1)S(1)}, u32[]{:S(2)}, u32[]{:S(2)}) collective-permute-start(bf16[128,1024]{1,0:T(8,128)(2,1)} %get-tuple-element.45), channel_id=1, source_target_pairs={{0,8},{8,16},{16,24},{24,32},{32,40},{40,48},{48,56},{56,64},{64,7... | collective-permute-start | bytes 786440 | tf_op jit(solution)/shard_map/ppermute | solution.py:50
  17.7 7.8 %copy-start.6 = (bf16[1024,128]{1,0:T(8,128)(2,1)S(1)}, bf16[1024,128]{1,0:T(8,128)(2,1)}, u32[]{:S(2)}) copy-start(bf16[1024,128]{1,0:T(8,128)(2,1)} %taps_ref) | copy-start | bytes 786436
  17.8 7.8 %copy-start.5 = (bf16[384,512]{1,0:T(8,128)(2,1)S(1)}, bf16[384,512]{1,0:T(8,128)(2,1)}, u32[]{:S(2)}) copy-start(bf16[384,512]{1,0:T(8,128)(2,1)} %constant.7.clone.matrix_ref) | copy-start | bytes 1179652
  17.8 7.8 %copy-start.4 = (bf16[256,1024]{1,0:T(8,128)(2,1)S(1)}, bf16[256,1024]{1,0:T(8,128)(2,1)}, u32[]{:S(2)}) copy-start(bf16[256,1024]{1,0:T(8,128)(2,1)} %res_ref) | copy-start | bytes 1572868
  17.8 7.8 %copy-start.1 = (bf16[256,1024]{1,0:T(8,128)(2,1)S(1)}, bf16[256,1024]{1,0:T(8,128)(2,1)}, u32[]{:S(2)}) copy-start(bf16[256,1024]{1,0:T(8,128)(2,1)} %key_ref.2) | copy-start | bytes 1572868
  17.8 7.8 %copy-start.2 = (bf16[256,1024]{1,0:T(8,128)(2,1)S(1)}, bf16[256,1024]{1,0:T(8,128)(2,1)}, u32[]{:S(2)}) copy-start(bf16[256,1024]{1,0:T(8,128)(2,1)} %value_ref.2) | copy-start | bytes 1572868
  17.9 7.8 %copy-start.3 = (bf16[256,1024]{1,0:T(8,128)(2,1)S(1)}, bf16[256,1024]{1,0:T(8,128)(2,1)}, u32[]{:S(2)}) copy-start(bf16[256,1024]{1,0:T(8,128)(2,1)} %gate_ref) | copy-start | bytes 1572868
  19.5 11.6 %collective-permute-start.6 = (bf16[768,128]{1,0:T(8,128)(2,1)}, bf16[768,128]{1,0:T(8,128)(2,1)S(1)}, u32[]{:S(2)}, u32[]{:S(2)}) collective-permute-start(bf16[768,128]{1,0:T(8,128)(2,1)} %get-tuple-element.53), channel_id=1, source_target_pairs={{0,80},{8,88},{16,64},{24,72},{32,112},{40,120},{48,96},{56,104},{... | collective-permute-start | bytes 589832 | tf_op jit(solution)/shard_map/ppermute | solution.py:50
  24.1 9.8 %collective-permute-start.8 = (bf16[1024,128]{1,0:T(8,128)(2,1)S(1)}, bf16[1024,128]{1,0:T(8,128)(2,1)S(1)}, u32[]{:S(2)}, u32[]{:S(2)}) collective-permute-start(bf16[1024,128]{1,0:T(8,128)(2,1)S(1)} %pad_maximum_fusion.4), channel_id=1, source_target_pairs={{0,16},{8,24},{16,0},{24,8},{32,48},{40,56},{48,32},{56,40},{64,80... | collective-permute-start | bytes 786440 | tf_op jit(solution)/shard_map/ppermute | solution.py:50
  24.1 11.3 %collective-permute-start.11 = (bf16[2048,128]{1,0:T(8,128)(2,1)S(1)}, bf16[2048,128]{1,0:T(8,128)(2,1)S(1)}, u32[]{:S(2)}, u32[]{:S(2)}) collective-permute-start(bf16[2048,128]{1,0:T(8,128)(2,1)S(1)} %pad_maximum_fusion.1), channel_id=1, source_target_pairs={{0,8},{8,0},{16,24},{24,16},{32,40},{40,32},{48,56},{56,48},{64,72... | collective-permute-start | bytes 1572872 | tf_op jit(solution)/shard_map/ppermute | solution.py:50
  24.3 18.8 %collective-permute-start.12 = (bf16[1536,128]{1,0:T(8,128)(2,1)S(1)}, bf16[1536,128]{1,0:T(8,128)(2,1)S(1)}, u32[]{:S(2)}, u32[]{:S(2)}) collective-permute-start(bf16[1536,128]{1,0:T(8,128)(2,1)S(1)} %pad_maximum_fusion.3), channel_id=1, source_target_pairs={{0,128},{8,136},{16,144},{24,152},{32,160},{40,168},{48,176},{56,1... | collective-permute-start | bytes 1179656 | tf_op jit(solution)/shard_map/ppermute | solution.py:50
  28.7 8.0 %copy-start = (bf16[768,128]{1,0:T(8,128)(2,1)S(1)}, bf16[768,128]{1,0:T(8,128)(2,1)}, u32[]{:S(2)}) copy-start(bf16[768,128]{1,0:T(8,128)(2,1)} %get-tuple-element.39.refs_0_.refs_4_) | copy-start | bytes 589828
  28.7 5.4 %collective-permute-start.5 = (f32[256]{0:T(256)S(1)}, f32[256]{0:T(256)S(1)}, u32[]{:S(2)}, u32[]{:S(2)}) collective-permute-start(f32[256]{0:T(256)S(1)} %bitcast.1), channel_id=1, source_target_pairs={{0,1},{1,0},{2,3},{3,2},{4,5},{5,4},{6,7},{7,6},{8,9},{9,8},{10,11... | collective-permute-start | bytes 3080 | tf_op jit(solution)/shard_map/ppermute | solution.py:380
  31.1 8.8 %collective-permute-start.10 = (bf16[512,128]{1,0:T(8,128)(2,1)S(1)}, bf16[512,128]{1,0:T(8,128)(2,1)S(1)}, u32[]{:S(2)}, u32[]{:S(2)}) collective-permute-start(bf16[512,128]{1,0:T(8,128)(2,1)S(1)} %slice.18), channel_id=1, source_target_pairs={{0,16},{8,24},{16,0},{24,8},{32,48},{40,56},{48,32},{56,40},{64,80... | collective-permute-start | bytes 393224 | tf_op jit(solution)/shard_map/ppermute | solution.py:50
  34.0 9.6 %collective-permute-start.9 = (bf16[1536,128]{1,0:T(8,128)(2,1)S(1)}, bf16[1536,128]{1,0:T(8,128)(2,1)S(1)}, u32[]{:S(2)}, u32[]{:S(2)}) collective-permute-start(bf16[1536,128]{1,0:T(8,128)(2,1)S(1)} %constant_dynamic-update-slice_fusion), channel_id=1, source_target_pairs={{0,8},{8,0},{16,24},{24,16},{32,40},{40,32},{48,56},{56,48},{64,72... | collective-permute-start | bytes 1179656 | tf_op jit(solution)/shard_map/ppermute | solution.py:50
  34.1 17.7 %collective-permute-start.14 = (bf16[1536,128]{1,0:T(8,128)(2,1)S(1)}, bf16[1536,128]{1,0:T(8,128)(2,1)S(1)}, u32[]{:S(2)}, u32[]{:S(2)}) collective-permute-start(bf16[1536,128]{1,0:T(8,128)(2,1)S(1)} %constant_dynamic-update-slice_fusion), channel_id=1, source_target_pairs={{0,128},{8,136},{16,144},{24,152},{32,160},{40,168},{48,176},{56,1... | collective-permute-start | bytes 1179656 | tf_op jit(solution)/shard_map/ppermute | solution.py:50
  35.4 16.4 %collective-permute-start.15 = (bf16[512,128]{1,0:T(8,128)(2,1)S(1)}, bf16[512,128]{1,0:T(8,128)(2,1)S(1)}, u32[]{:S(2)}, u32[]{:S(2)}) collective-permute-start(bf16[512,128]{1,0:T(8,128)(2,1)S(1)} %slice.18), channel_id=1, source_target_pairs={{0,144},{8,152},{16,128},{24,136},{32,176},{40,184},{48,160},{56,1... | collective-permute-start | bytes 393224 | tf_op jit(solution)/shard_map/ppermute | solution.py:50
  39.9 7.2 %collective-permute-start.7 = (f32[256]{0:T(256)S(1)}, f32[256]{0:T(256)S(1)}, u32[]{:S(2)}, u32[]{:S(2)}) collective-permute-start(f32[256]{0:T(256)S(1)} %add.16), channel_id=1, source_target_pairs={{0,2},{1,3},{2,0},{3,1},{4,6},{5,7},{6,4},{7,5},{8,10},{9,11},{10,... | collective-permute-start | bytes 3080 | tf_op jit(solution)/shard_map/ppermute | solution.py:380
  43.1 10.2 %collective-permute-start.17 = (bf16[2560,128]{1,0:T(8,128)(2,1)S(1)}, bf16[2560,128]{1,0:T(8,128)(2,1)S(1)}, u32[]{:S(2)}, u32[]{:S(2)}) collective-permute-start(bf16[2560,128]{1,0:T(8,128)(2,1)S(1)} %pad_maximum_fusion), channel_id=1, source_target_pairs={{0,8},{8,0},{16,24},{24,16},{32,40},{40,32},{48,56},{56,48},{64,72... | collective-permute-start | bytes 1966088 | tf_op jit(solution)/shard_map/ppermute | solution.py:50
  51.8 3.3 %collective-permute-start.16 = (bf16[2048,128]{1,0:T(8,128)(2,1)S(1)}, bf16[2048,128]{1,0:T(8,128)(2,1)S(1)}, u32[]{:S(2)}, u32[]{:S(2)}) collective-permute-start(bf16[2048,128]{1,0:T(8,128)(2,1)S(1)} %pad_maximum_fusion.2), channel_id=1, source_target_pairs={{0,8},{8,0},{16,24},{24,16},{32,40},{40,32},{48,56},{56,48},{64,72... | collective-permute-start | bytes 1572872 | tf_op jit(solution)/shard_map/ppermute | solution.py:50
  51.9 12.0 %collective-permute-start.13 = (f32[256]{0:T(256)S(1)}, f32[256]{0:T(256)S(1)}, u32[]{:S(2)}, u32[]{:S(2)}) collective-permute-start(f32[256]{0:T(256)S(1)} %add.17), channel_id=1, source_target_pairs={{0,4},{1,5},{2,6},{3,7},{4,0},{5,1},{6,2},{7,3},{8,12},{9,13},{10,... | collective-permute-start | bytes 3080 | tf_op jit(solution)/shard_map/ppermute | solution.py:380
  55.1 8.8 %copy-start.7 = (bf16[256,1024]{1,0:T(8,128)(2,1)S(1)}, bf16[256,1024]{1,0:T(8,128)(2,1)}, u32[]{:S(2)}) copy-start(bf16[256,1024]{1,0:T(8,128)(2,1)} %get-tuple-element.34) | copy-start | bytes 1572868
  55.2 8.8 %copy-start.9 = (f32[1024]{0:T(1024)S(1)}, f32[1024]{0:T(1024)}, u32[]{:S(2)}) copy-start(f32[1024]{0:T(1024)} %param.15) | copy-start | bytes 12292
  58.2 6.7 %collective-permute-start.18 = (bf16[256,128]{1,0:T(8,128)(2,1)S(1)}, bf16[256,128]{1,0:T(8,128)(2,1)S(1)}, u32[]{:S(2)}, u32[]{:S(2)}) collective-permute-start(bf16[256,128]{1,0:T(8,128)(2,1)S(1)} %get-tuple-element.68), channel_id=1, source_target_pairs={{112,0},{120,8},{32,16},{40,24},{16,32},{24,40},{64,48},{72,56},{4... | collective-permute-start | bytes 196616 | tf_op jit(solution)/shard_map/ppermute | solution.py:54
  61.2 5.5 %collective-permute-start.19 = (bf16[256,128]{1,0:T(8,128)(2,1)S(1)}, bf16[256,128]{1,0:T(8,128)(2,1)S(1)}, u32[]{:S(2)}, u32[]{:S(2)}) collective-permute-start(bf16[256,128]{1,0:T(8,128)(2,1)S(1)} %get-tuple-element.69), channel_id=1, source_target_pairs={{32,0},{40,8},{112,16},{120,24},{64,32},{72,40},{16,48},{24,56},{9... | collective-permute-start | bytes 196616 | tf_op jit(solution)/shard_map/ppermute | solution.py:54
  61.3 7.6 %collective-permute-start.20 = (bf16[256,128]{1,0:T(8,128)(2,1)S(1)}, bf16[256,128]{1,0:T(8,128)(2,1)S(1)}, u32[]{:S(2)}, u32[]{:S(2)}) collective-permute-start(bf16[256,128]{1,0:T(8,128)(2,1)S(1)} %get-tuple-element.70), channel_id=1, source_target_pairs={{80,0},{88,8},{64,16},{72,24},{112,32},{120,40},{96,48},{104,56},{... | collective-permute-start | bytes 196616 | tf_op jit(solution)/shard_map/ppermute | solution.py:54
